TPU v7x, 32 devices: a whole 2x2x4 slice. The times are simulated.
32 devices in a mesh: dp: 8 (over z, y), tensor: 4 (over x, core).
Axes of the slice: x: 2, y: 2, z: 4, core: 2. Of those that a mesh axis runs over, the one named last changes fastest.
Arguments:
- tokens: bfloat16 [2048, 2048], P('dp'), may hold values from -24 to 24
- segment_ids: int32 [2048], P('dp'), may hold values from 1 to 3, as said below
- routes: int32 [2048, 8], P('dp'), may hold values from 0 to 15, all different within a row; in each aligned block of 256 rows (0 to 255, 256 to 511, ...) at most 256 rows name the same one
- norm1_gain: float32 [2048], replicated, may hold values from 0.5 to 1.5
- w_query: bfloat16 [2048, 2048], P(None, 'tensor'), may hold values from -0.125 to 0.125
- w_key: bfloat16 [2048, 2048], P(None, 'tensor'), may hold values from -0.125 to 0.125
- w_value: bfloat16 [2048, 2048], P(None, 'tensor'), may hold values from -0.125 to 0.125
- query_gain: float32 [16, 128], P('tensor'), may hold values from 0.5 to 1.5
- key_gain: float32 [16, 128], P('tensor'), may hold values from 0.5 to 1.5
- w_out: bfloat16 [2048, 2048], P('tensor'), may hold values from -4 to 4
- norm2_gain: float32 [2048], replicated, may hold values from 0.5 to 1.5
- w_router: bfloat16 [2048, 16], replicated, may hold values from -0.0625 to 0.0625
- w_gate: bfloat16 [16, 2048, 1024], P('dp', None, 'tensor'), may hold values from -0.125 to 0.125
- w_up: bfloat16 [16, 2048, 1024], P('dp', None, 'tensor'), may hold values from -0.125 to 0.125
- w_down: bfloat16 [16, 1024, 2048], P('dp', 'tensor'), may hold values from -7.1875 to 7.1875
- cotangent: bfloat16 [2048, 2048], P('dp'), may hold values from -6 to 6
Outputs:
- block_output: bfloat16 [2048, 2048], P('dp')
- input_grad: float32 [2048, 2048], P('dp')
- d_norm1_gain: float32 [2048], P('dp')
- d_w_query: float32 [2048, 2048], P('dp', 'tensor')
- d_w_key: float32 [2048, 2048], P('dp', 'tensor')
- d_w_value: float32 [2048, 2048], P('dp', 'tensor')
- d_query_gain: float32 [16, 128], P('tensor', 'dp')
- d_key_gain: float32 [16, 128], P('tensor', 'dp')
- d_w_out: float32 [2048, 2048], P('tensor', 'dp')
- d_norm2_gain: float32 [2048], P('dp')
- d_w_router: float32 [2048, 16], P('dp')
- d_w_gate: float32 [16, 2048, 1024], P('dp', None, 'tensor')
- d_w_up: float32 [16, 2048, 1024], P('dp', None, 'tensor')
- d_w_down: float32 [16, 1024, 2048], P('dp', 'tensor')
Inputs may be any that keep to these rules, and one draw needn't show every extreme that they name: `routes`: in each aligned block of 256 tokens every token names 8 different experts and no expert is named by more than 256 tokens of the block; some expert is named by exactly 256 tokens of some block in every draw. `segment_ids`: ids never fall along the tokens. The one packed sequence of 2048 tokens holds three documents with ids of their own, and one of them has exactly 1920 tokens.
All inputs are finite; a program needn't handle non-finite values.
Results may differ from a plain program's by a relative error of at most 0.025.
Values may be sent and summed in bfloat16 or wider, within the bound.
No kernel may reach another device: no remote copies, remote signals or barrier semaphores. Data moves between devices by JAX's collectives and lax.ppermute only.
A program may use at most 384 MiB of HBM per device.

v0:
```python
import math

import jax
import jax.numpy as jnp
from jax import lax
from jax.sharding import PartitionSpec as P

SPAN = 8


EPSILON = 1e-05
ROPE_BASE = 10000.0
NEGATIVE = -1e30


def from_behind(array, axis, by):
    count = lax.axis_size(axis)
    pairs = [(i, i + by) for i in range(count) if 0 <= i + by < count]
    return lax.ppermute(array, axis, pairs)


def rope_tables(positions, head_size):
    frequency = ROPE_BASE ** (-jnp.arange(0, head_size, 2, dtype=jnp.float32) / head_size)
    angles = positions[:, None] * frequency[None, :]
    cos_table = jnp.concatenate([jnp.cos(angles), jnp.cos(angles)], -1)[:, None, :]
    sin_table = jnp.concatenate([jnp.sin(angles), jnp.sin(angles)], -1)[:, None, :]
    return (cos_table, sin_table)


def rotate(vector, cos_table, sin_table):
    half_size = vector.shape[-1] // 2
    turned = jnp.concatenate([-vector[..., half_size:], vector[..., :half_size]], -1)
    return vector * cos_table + turned * sin_table


def unrotate(gradient, cos_table, sin_table):
    half_size = gradient.shape[-1] // 2
    scaled = gradient * sin_table
    turned = jnp.concatenate([scaled[..., half_size:], -scaled[..., :half_size]], -1)
    return gradient * cos_table + turned


def place_rows(route_block, experts, capacity):
    tok_count, top_count = route_block.shape
    flat_ids = route_block.reshape(-1)
    onehot = (flat_ids[:, None] == jnp.arange(experts, dtype=jnp.int32)[None, :]).astype(jnp.int32)
    slot_rank = jnp.sum(jnp.cumsum(onehot, 0) * onehot, 1) - 1
    dest_slot = flat_ids * capacity + slot_rank
    owner_tok = jnp.arange(tok_count * top_count, dtype=jnp.int32) // top_count
    slot_token = jnp.full((experts * capacity,), tok_count, jnp.int32).at[dest_slot].set(owner_tok)
    return (dest_slot, slot_token)


def over_rows(left_side, right_side):
    return lax.dot_general(
        left_side, right_side, (((0,), (0,)), ((), ())), preferred_element_type=jnp.float32
    )


def by_transpose(left_side, right_side):
    return lax.dot_general(
        left_side, right_side, (((1,), (1,)), ((), ())), preferred_element_type=jnp.float32
    )


def weigh_rows(rows_back, gate_values, out_grad):
    rows_float = rows_back.astype(jnp.float32)
    expert_part = jnp.zeros((rows_float.shape[0], rows_float.shape[2]), jnp.float32)
    for choice_num in range(rows_float.shape[1]):
        expert_part = expert_part + gate_values[:, choice_num, None] * rows_float[:, choice_num]
    gate_dots = jnp.sum(out_grad[:, None, :] * rows_float, -1)
    return (expert_part, gate_dots)


def per_device(
    tokens,
    segment_ids,
    routes,
    norm1_gain,
    w_query,
    w_key,
    w_value,
    query_gain,
    key_gain,
    w_out,
    norm2_gain,
    w_router,
    w_gate,
    w_up,
    w_down,
    cotangent,
):
    tok_count, model_width = tokens.shape
    heads_here, head_size = query_gain.shape
    local_width = heads_here * head_size
    tensor_count = lax.axis_size("tensor")
    full_width = local_width * tensor_count
    top_count = routes.shape[1]
    experts = w_router.shape[1]
    capacity = 2 * tok_count * top_count // experts
    owners = lax.axis_size("dp")
    local_experts = w_gate.shape[0]
    dp_place = lax.axis_index("dp")
    score_root = math.sqrt(head_size)
    state_in = tokens.astype(jnp.float32)
    scale_in = lax.rsqrt(jnp.mean(state_in * state_in, -1, keepdims=True) + EPSILON)
    unit_in = state_in * scale_in
    normed_in = (unit_in * norm1_gain).astype(jnp.bfloat16)
    query_raw = jnp.dot(normed_in, w_query, preferred_element_type=jnp.float32)
    key_raw = jnp.dot(normed_in, w_key, preferred_element_type=jnp.float32)
    value_att = jnp.dot(normed_in, w_value, preferred_element_type=jnp.float32).astype(jnp.bfloat16)
    query_sq, key_sq = lax.psum(
        (jnp.sum(query_raw * query_raw, -1), jnp.sum(key_raw * key_raw, -1)), "tensor"
    )
    query_scale = lax.rsqrt(query_sq / full_width + EPSILON)[:, None]
    key_scale = lax.rsqrt(key_sq / full_width + EPSILON)[:, None]
    query_unit = query_raw * query_scale
    key_unit = key_raw * key_scale
    local_pos = jnp.arange(tok_count, dtype=jnp.int32)
    positions = (dp_place % SPAN * tok_count + local_pos).astype(jnp.float32)
    cos_table, sin_table = rope_tables(positions, head_size)
    query_att = rotate(
        (query_unit * query_gain.reshape(-1)).reshape(tok_count, heads_here, head_size),
        cos_table,
        sin_table,
    ).astype(jnp.bfloat16)
    key_att = rotate(
        (key_unit * key_gain.reshape(-1)).reshape(tok_count, heads_here, head_size),
        cos_table,
        sin_table,
    ).astype(jnp.bfloat16)
    value_heads = value_att.reshape(tok_count, heads_here, head_size)
    segment_low = segment_ids.astype(jnp.bfloat16)
    query_pos = dp_place * tok_count + local_pos
    key_blocks, value_blocks, segment_blocks, position_blocks = ([], [], [], [])
    for distance in range(SPAN - 1, 0, -1):
        key_far, value_far, segment_far = from_behind(
            (key_att, value_heads, segment_low), "dp", distance
        )
        key_blocks.append(key_far)
        value_blocks.append(value_far)
        segment_blocks.append(segment_far)
        position_blocks.append((dp_place - distance) * tok_count + local_pos)
    key_blocks.append(key_att)
    value_blocks.append(value_heads)
    segment_blocks.append(segment_low)
    position_blocks.append(query_pos)
    key_all = jnp.concatenate(key_blocks, 0)
    value_all = jnp.concatenate(value_blocks, 0)
    segment_all = jnp.concatenate(segment_blocks, 0)
    position_all = jnp.concatenate(position_blocks, 0)
    visible = (
        (segment_all[None, :] == segment_low[:, None])
        & (position_all[None, :] <= query_pos[:, None])
        & (position_all[None, :] >= 0)
    )
    raw_scores = (
        jnp.einsum("qhd,khd->hqk", query_att, key_all, preferred_element_type=jnp.float32)
        / score_root
    )
    masked = jnp.where(visible[None], raw_scores, NEGATIVE)
    row_top = jnp.max(masked, -1, keepdims=True)
    log_total = row_top + jnp.log(jnp.sum(jnp.exp(masked - row_top), -1, keepdims=True))
    attn_probs = jnp.where(visible[None], jnp.exp(masked - log_total), 0.0)
    probs_low = attn_probs.astype(jnp.bfloat16)
    attn_heads = jnp.einsum(
        "hqk,khd->qhd", probs_low, value_all, preferred_element_type=jnp.float32
    ).astype(jnp.bfloat16)
    attn_mix = attn_heads.reshape(tok_count, local_width)
    attn_full = lax.psum(jnp.dot(attn_mix, w_out, preferred_element_type=jnp.float32), "tensor")
    resid_state = state_in + attn_full
    scale_mid = lax.rsqrt(jnp.mean(resid_state * resid_state, -1, keepdims=True) + EPSILON)
    unit_mid = resid_state * scale_mid
    normed_mid = (unit_mid * norm2_gain).astype(jnp.bfloat16)
    logits = jnp.dot(normed_mid, w_router, preferred_element_type=jnp.float32)
    router_probs = jax.nn.softmax(logits, -1)
    chosen = (routes[:, :, None] == jnp.arange(experts, dtype=jnp.int32)[None, None, :]).astype(
        jnp.float32
    )
    gate_values = jnp.sum(chosen * router_probs[:, None, :], -1)
    dest_slot, slot_token = place_rows(routes, experts, capacity)
    padded = jnp.concatenate([normed_mid, jnp.zeros((1, model_width), jnp.bfloat16)], 0)
    slot_grid = slot_token.reshape(owners, local_experts, capacity)
    rows_in = lax.all_to_all(padded[slot_grid], "dp", split_axis=0, concat_axis=0, tiled=True)
    gate_pre = jnp.einsum("necd,edf->necf", rows_in, w_gate, preferred_element_type=jnp.float32)
    up_pre = jnp.einsum("necd,edf->necf", rows_in, w_up, preferred_element_type=jnp.float32)
    sigma_gate = jax.nn.sigmoid(gate_pre)
    silu_gate = gate_pre * sigma_gate
    hidden = (silu_gate * up_pre).astype(jnp.bfloat16)
    partial_rows = jnp.einsum(
        "necf,efd->necd", hidden, w_down, preferred_element_type=jnp.float32
    ).astype(jnp.bfloat16)
    out_grad = cotangent.astype(jnp.float32)
    returned = lax.all_to_all(partial_rows, "dp", split_axis=0, concat_axis=0, tiled=True)
    rows_back = returned.reshape(experts * capacity, model_width)[dest_slot].reshape(
        tok_count, top_count, model_width
    )
    expert_part, gate_dots = weigh_rows(rows_back, gate_values, out_grad)
    expert_full, gate_grad = lax.psum((expert_part, gate_dots), "tensor")
    block_output = (resid_state + expert_full).astype(jnp.bfloat16)
    gate_slots = (
        jnp.zeros((experts * capacity,), jnp.float32).at[dest_slot].set(gate_values.reshape(-1))
    )
    gate_grid = gate_slots.reshape(owners, local_experts, capacity)
    grad_padded = jnp.concatenate([out_grad, jnp.zeros((1, model_width), jnp.float32)], 0)
    part_grad = (gate_grid[..., None] * grad_padded[slot_grid]).astype(jnp.bfloat16)
    part_back = lax.all_to_all(part_grad, "dp", split_axis=0, concat_axis=0, tiled=True)
    d_w_down = jnp.einsum("necf,necd->efd", hidden, part_back, preferred_element_type=jnp.float32)
    hidden_grad = jnp.einsum(
        "necd,efd->necf", part_back, w_down, preferred_element_type=jnp.float32
    )
    gate_low = (hidden_grad * up_pre * sigma_gate * (1.0 + gate_pre * (1.0 - sigma_gate))).astype(
        jnp.bfloat16
    )
    up_low = (hidden_grad * silu_gate).astype(jnp.bfloat16)
    d_w_gate = jnp.einsum("necd,necf->edf", rows_in, gate_low, preferred_element_type=jnp.float32)
    d_w_up = jnp.einsum("necd,necf->edf", rows_in, up_low, preferred_element_type=jnp.float32)
    row_grad = jnp.einsum(
        "necf,edf->necd", gate_low, w_gate, preferred_element_type=jnp.float32
    ) + jnp.einsum("necf,edf->necd", up_low, w_up, preferred_element_type=jnp.float32)
    row_home = lax.all_to_all(row_grad, "dp", split_axis=0, concat_axis=0, tiled=True)
    row_tokens = row_home.reshape(experts * capacity, model_width)[dest_slot].reshape(
        tok_count, top_count, model_width
    )
    expert_input = lax.psum(jnp.sum(row_tokens, 1), "tensor")
    probs_grad = jnp.sum(chosen * gate_grad[:, :, None], 1)
    logit_low = (
        router_probs * (probs_grad - jnp.sum(router_probs * probs_grad, -1, keepdims=True))
    ).astype(jnp.bfloat16)
    d_router = over_rows(normed_mid, logit_low)
    mid_grad = expert_input + by_transpose(logit_low, w_router)
    d_gain_mid = jnp.sum(mid_grad * unit_mid, 0)
    mid_scaled = mid_grad * norm2_gain
    resid_grad = out_grad + scale_mid * (
        mid_scaled - unit_mid * jnp.mean(mid_scaled * unit_mid, -1, keepdims=True)
    )
    resid_low = resid_grad.astype(jnp.bfloat16)
    d_out = over_rows(attn_mix, resid_low)
    mix_grad = (
        by_transpose(resid_low, w_out)
        .astype(jnp.bfloat16)
        .reshape(tok_count, heads_here, head_size)
    )
    p_grad = jnp.einsum("qhd,khd->hqk", mix_grad, value_all, preferred_element_type=jnp.float32)
    score_low = (attn_probs * (p_grad - jnp.sum(attn_probs * p_grad, -1, keepdims=True))).astype(
        jnp.bfloat16
    )
    query_att_grad = (
        jnp.einsum("hqk,khd->qhd", score_low, key_all, preferred_element_type=jnp.float32)
        / score_root
    ).astype(jnp.bfloat16)
    key_grad_all = (
        jnp.einsum("hqk,qhd->khd", score_low, query_att, preferred_element_type=jnp.float32)
        / score_root
    )
    value_grad_all = jnp.einsum(
        "hqk,qhd->khd", probs_low, mix_grad, preferred_element_type=jnp.float32
    )
    key_total = key_grad_all[(SPAN - 1) * tok_count :]
    value_total = value_grad_all[(SPAN - 1) * tok_count :]
    for block_num, distance in enumerate(range(SPAN - 1, 0, -1)):
        lower = block_num * tok_count
        key_home, value_home = (
            from_behind(
                key_grad_all[lower : lower + tok_count].astype(jnp.bfloat16), "dp", -distance
            ).astype(jnp.float32),
            from_behind(
                value_grad_all[lower : lower + tok_count].astype(jnp.bfloat16), "dp", -distance
            ).astype(jnp.float32),
        )
        key_total = key_total + key_home
        value_total = value_total + value_home
    key_att_grad = key_total.astype(jnp.bfloat16)
    value_low = value_total.astype(jnp.bfloat16).reshape(tok_count, local_width)
    query_gain_in = unrotate(query_att_grad.astype(jnp.float32), cos_table, sin_table).reshape(
        tok_count, local_width
    )
    key_gain_in = unrotate(key_att_grad.astype(jnp.float32), cos_table, sin_table).reshape(
        tok_count, local_width
    )
    d_query_gain = jnp.sum(query_gain_in * query_unit, 0).reshape(heads_here, head_size)
    d_key_gain = jnp.sum(key_gain_in * key_unit, 0).reshape(heads_here, head_size)
    query_scaled = query_gain_in * query_gain.reshape(-1)
    key_scaled = key_gain_in * key_gain.reshape(-1)
    query_dot, key_dot = lax.psum(
        (jnp.sum(query_scaled * query_unit, -1), jnp.sum(key_scaled * key_unit, -1)), "tensor"
    )
    query_low = (
        query_scale * (query_scaled - query_unit * (query_dot / full_width)[:, None])
    ).astype(jnp.bfloat16)
    key_low = (key_scale * (key_scaled - key_unit * (key_dot / full_width)[:, None])).astype(
        jnp.bfloat16
    )
    d_query = over_rows(normed_in, query_low)
    d_key = over_rows(normed_in, key_low)
    d_value = over_rows(normed_in, value_low)
    in_part = (
        by_transpose(query_low, w_query)
        + by_transpose(key_low, w_key)
        + by_transpose(value_low, w_value)
    )
    in_grad_norm = lax.psum(in_part.astype(jnp.bfloat16), "tensor").astype(jnp.float32)
    d_gain_in = jnp.sum(in_grad_norm * unit_in, 0)
    in_scaled = in_grad_norm * norm1_gain
    input_grad = resid_grad + scale_in * (
        in_scaled - unit_in * jnp.mean(in_scaled * unit_in, -1, keepdims=True)
    )
    summed = (
        lax.psum_scatter(
            d_gain_in.astype(jnp.bfloat16), "dp", scatter_dimension=0, tiled=True
        ).astype(jnp.float32),
        lax.psum_scatter(
            d_query.astype(jnp.bfloat16), "dp", scatter_dimension=0, tiled=True
        ).astype(jnp.float32),
        lax.psum_scatter(d_key.astype(jnp.bfloat16), "dp", scatter_dimension=0, tiled=True).astype(
            jnp.float32
        ),
        lax.psum_scatter(
            d_value.astype(jnp.bfloat16), "dp", scatter_dimension=0, tiled=True
        ).astype(jnp.float32),
        lax.psum_scatter(
            d_query_gain.astype(jnp.bfloat16), "dp", scatter_dimension=1, tiled=True
        ).astype(jnp.float32),
        lax.psum_scatter(
            d_key_gain.astype(jnp.bfloat16), "dp", scatter_dimension=1, tiled=True
        ).astype(jnp.float32),
        lax.psum_scatter(d_out.astype(jnp.bfloat16), "dp", scatter_dimension=1, tiled=True).astype(
            jnp.float32
        ),
        lax.psum_scatter(
            d_gain_mid.astype(jnp.bfloat16), "dp", scatter_dimension=0, tiled=True
        ).astype(jnp.float32),
        lax.psum_scatter(
            d_router.astype(jnp.bfloat16), "dp", scatter_dimension=0, tiled=True
        ).astype(jnp.float32),
    )
    return (
        block_output,
        input_grad,
        summed[0],
        summed[1],
        summed[2],
        summed[3],
        summed[4],
        summed[5],
        summed[6],
        summed[7],
        summed[8],
        d_w_gate,
        d_w_up,
        d_w_down,
    )


def solution(mesh):
    in_specs = (
        P("dp", None),
        P("dp"),
        P("dp", None),
        P(),
        P(None, "tensor"),
        P(None, "tensor"),
        P(None, "tensor"),
        P("tensor", None),
        P("tensor", None),
        P("tensor", None),
        P(),
        P(),
        P("dp", None, "tensor"),
        P("dp", None, "tensor"),
        P("dp", "tensor", None),
        P("dp", None),
    )
    out_specs = (
        P("dp", None),
        P("dp", None),
        P("dp"),
        P("dp", "tensor"),
        P("dp", "tensor"),
        P("dp", "tensor"),
        P("tensor", "dp"),
        P("tensor", "dp"),
        P("tensor", "dp"),
        P("dp"),
        P("dp", None),
        P("dp", None, "tensor"),
        P("dp", None, "tensor"),
        P("dp", "tensor", None),
    )
    return jax.shard_map(
        per_device, mesh=mesh, in_specs=in_specs, out_specs=out_specs, check_vma=False
    )
```

profile of v0, /device:TPU:0, one launch (start us, length us, event | category | flops | bytes accessed | tf_op | source)
XLA Modules:
  0.0 2932.2 jit_solution(2756561536480119578)
XLA Ops:
  44.2 6.1 all-reduce.5
  76.4 11.5 collective-permute-done.14
  90.2 8.3 collective-permute-start.18
  105.6 10.7 collective-permute-start.2
  119.1 16.7 collective-permute-start.1
  167.0 8.1 scatter_custom_fusion
  175.2 48.4 %all-reduce.12.cloned.1.call-done = f32[256,2048]{1,0:T(8,128)} async-done(((f32[256,2048]{1,0:T(8,128)}), f32[256,2048]{1,0:T(8,128)}) %all-reduce.12.cloned.1.call-update) | async-done | bytes 2097168 | tf_op jit(solution)/shard_map/psum | solution.py:170
  228.2 20.9 gather_fusion
  249.0 370.6 %all_to_all.20 = bf16[8,2,256,2048]{3,2,1,0:T(8,128)(2,1)} all-to-all(bf16[8,2,256,2048]{3,2,1,0:T(8,128)(2,1)} %bitcast.279), channel_id=1, replica_groups=mesh['dp'=8,'tensor'=4] {'dp'}, dimensions={0} | all-to-all | bytes 33554432 | tf_op jit(solution)/shard_map/all_to_all | solution.py:184
  619.7 12.9 fusion.6
  632.6 11.8 fusion.13
  644.4 9.7 convert_bitcast_fusion
  654.1 14.1 copy.212
  668.2 6.1 all-to-all-start.1
  677.5 33.3 %gather_fusion.2 = f32[4096,2048]{1,0:T(8,128)} fusion(f32[257,2048]{1,0:T(8,128)} %concatenate.49, s32[4096]{0:T(1024)S(1)} %broadcast_clamp_fusion), kind=kCustom, calls=%fused_computation.2 | custom fusion | bytes 67125248 | tf_op jit(solution)/shard_map/gather | solution.py:206
  711.9 324.2 %all-to-all-done.1 = bf16[8,2,256,2048]{3,2,1,0:T(8,128)(2,1)} async-done(((bf16[8,2,256,2048]{3,2,1,0:T(8,128)(2,1)}), bf16[8,2,256,2048]{3,2,1,0:T(8,128)(2,1)}, u32[]{:S(2)}, u32[]{:S(2)}) %all-to-all-start.1) | async-done | bytes 16777248 | tf_op jit(solution)/shard_map/all_to_all | solution.py:194
  1036.1 24.2 gather_fusion.1
  1060.4 5.7 multiply_reduce_fusion
  1066.1 11.5 psum.68
  1078.5 8.1 scatter_custom_fusion.1
  1086.6 12.0 multiply_convert_fusion
  1098.6 368.2 %all_to_all.21 = bf16[8,2,256,2048]{3,2,1,0:T(8,128)(2,1)} all-to-all(bf16[8,2,256,2048]{3,2,1,0:T(8,128)(2,1)S(1)} %multiply_convert_fusion), channel_id=1, replica_groups=mesh['dp'=8,'tensor'=4] {'dp'}, dimensions={0} | all-to-all | bytes 33554432 | tf_op jit(solution)/shard_map/all_to_all | solution.py:207
  1466.8 12.4 fusion.12
  1479.1 13.2 fusion.51
  1492.3 22.0 add_bitcast_fusion
  1514.3 23.0 copy.223
  1537.3 7.1 all-to-all-start.3
  1544.5 11.3 bitcast_convert_fusion
  1555.8 59.7 %fusion.110 = (f32[256,1,2048]{2,1,0:T(1,128)S(1)}, f32[256,1,2048]{2,1,0:T(1,128)}, f32[256,1,2048]{2,1,0:T(1,128)}, f32[256,1,2048]{2,1,0:T(1,128)}, f32[256,1...) fusion(f32[256,8,2048]{2,1,0:T(8,128)} %bitcast_convert_fusion), kind=kLoop, calls=%fused_computation.249 | loop fusion | bytes 33554432 | tf_op jit(solution)/shard_map/slice | solution.py:70
  1615.5 15.0 fusion.35
  1630.5 635.5 %all-to-all-done.3 = f32[8,2,256,2048]{3,2,1,0:T(8,128)} async-done(((f32[8,2,256,2048]{3,2,1,0:T(8,128)}), f32[8,2,256,2048]{3,2,1,0:T(8,128)}, u32[]{:S(2)}, u32[]{:S(2)}) %all-to-all-start.3) | async-done | bytes 33554464 | tf_op jit(solution)/shard_map/all_to_all | solution.py:221
  2266.0 27.1 gather_fusion.3
  2293.0 9.4 bitcast_reduce_fusion
  2304.9 81.6 %all-reduce.16.cloned.1.call-done = (f32[256,2048]{1,0:T(8,128)}, f32[256,2048]{1,0:T(8,128)}) async-done(((f32[256,2048]{1,0:T(8,128)}, f32[256,2048]{1,0:T(8,128)}), (f32[256,2048]{1,0:T(8,128)}, f32[256,2048]{1,0:T(8,128)})) %all-reduce.16.cloned.1.call-update) | async-done | bytes 4194320 | tf_op jit(solution)/shard_map/psum | solution.py:199
  2392.8 7.0 multiply_reduce_fusion.1
  2430.9 28.2 collective-permute-done.24
  2472.0 5.7 all-reduce.4
  2490.1 12.6 collective-permute-done.31
  2524.1 12.3 convolution_bitcast_fusion
  2536.4 12.3 convolution_bitcast_fusion.1
  2548.8 12.3 fusion.18
  2562.4 39.1 %reduce-scatter.24.cloned.1.call-done = bf16[16,4]{1,0:T(8,128)(2,1)} async-done(((bf16[128,4]{1,0:T(8,128)(2,1)}), bf16[16,4]{1,0:T(8,128)(2,1)}) %reduce-scatter.24.cloned.1.call-update) | async-done | bytes 144
  2602.8 36.1 %all-reduce.14.cloned.1.call-done = bf16[256,2048]{1,0:T(8,128)(2,1)} async-done(((bf16[256,2048]{1,0:T(8,128)(2,1)}), bf16[256,2048]{1,0:T(8,128)(2,1)}) %all-reduce.14.cloned.1.call-update) | async-done | bytes 1048592 | tf_op jit(solution)/shard_map/psum | solution.py:302
  2641.0 21.9 all-reduce.7
  2668.2 43.1 %reduce-scatter.18.cloned.1.call-done = bf16[512,256]{1,0:T(8,128)(2,1)} async-done(((bf16[512,2048]{1,0:T(8,128)(2,1)}), bf16[512,256]{1,0:T(8,128)(2,1)}) %reduce-scatter.18.cloned.1.call-update) | async-done | bytes 262160 | tf_op jit(solution)/shard_map/reduce_scatter | solution.py:327
  2713.1 69.0 %reduce-scatter.16.cloned.1.call-done = bf16[256,512]{1,0:T(8,128)(2,1)} async-done(((bf16[2048,512]{1,0:T(8,128)(2,1)}), bf16[256,512]{1,0:T(8,128)(2,1)}) %reduce-scatter.16.cloned.1.call-update) | async-done | bytes 262160 | tf_op jit(solution)/shard_map/reduce_scatter | solution.py:318
  2783.9 68.8 %reduce-scatter.14.cloned.1.call-done = bf16[256,512]{1,0:T(8,128)(2,1)} async-done(((bf16[2048,512]{1,0:T(8,128)(2,1)}), bf16[256,512]{1,0:T(8,128)(2,1)}) %reduce-scatter.14.cloned.1.call-update) | async-done | bytes 262160 | tf_op jit(solution)/shard_map/reduce_scatter | solution.py:315
  2854.5 68.9 %reduce-scatter.12.cloned.1.call-done = bf16[256,512]{1,0:T(8,128)(2,1)} async-done(((bf16[2048,512]{1,0:T(8,128)(2,1)}), bf16[256,512]{1,0:T(8,128)(2,1)}) %reduce-scatter.12.cloned.1.call-update) | async-done | bytes 262160 | tf_op jit(solution)/shard_map/reduce_scatter | solution.py:312
  (408 shorter events, 218.0 us)
Async XLA Ops:
  7.2 637.2 %copy-start = (bf16[2,256,2048]{2,1,0:T(8,128)(2,1)S(1)}, bf16[2,256,2048]{2,1,0:T(8,128)(2,1)}, u32[]{:S(2)}) copy-start(bf16[2,256,2048]{2,1,0:T(8,128)(2,1)} %param.30) | copy-start | bytes 6291460
  7.2 216.3 %all-reduce.12.cloned.1.call-start = ((), (), s32[]{:S(2)}) async-start(), calls=%async_computation.11 | async-start | bytes 4194304 | tf_op jit(solution)/shard_map/psum | solution.py:170
  8.6 62.7 %collective-permute-start.13 = (bf16[256]{0:T(256)(128)(2,1)}, bf16[256]{0:T(256)(128)(2,1)}, u32[]{:S(2)}, u32[]{:S(2)}) collective-permute-start(bf16[256]{0:T(256)(128)(2,1)} %convert_element_type.239), channel_id=1, source_target_pairs={{0,4},{4,8},{8,12},{12,16},{16,20},{20,24},{24,28},{1,5},{5,9},{9,... | collective-permute-start | bytes 1544 | tf_op jit(solution)/shard_map/ppermute | solution.py:19
  14.1 54.5 %collective-permute-start.12 = (bf16[256]{0:T(256)(128)(2,1)}, bf16[256]{0:T(256)(128)(2,1)}, u32[]{:S(2)}, u32[]{:S(2)}) collective-permute-start(bf16[256]{0:T(256)(128)(2,1)} %convert_element_type.239), channel_id=1, source_target_pairs={{0,8},{4,12},{8,16},{12,20},{16,24},{20,28},{1,9},{5,13},{9,17},{1... | collective-permute-start | bytes 1544 | tf_op jit(solution)/shard_map/ppermute | solution.py:19
  17.5 43.0 %collective-permute-start.9 = (bf16[256]{0:T(256)(128)(2,1)}, bf16[256]{0:T(256)(128)(2,1)}, u32[]{:S(2)}, u32[]{:S(2)}) collective-permute-start(bf16[256]{0:T(256)(128)(2,1)} %convert_element_type.239), channel_id=1, source_target_pairs={{0,20},{4,24},{8,28},{1,21},{5,25},{9,29},{2,22},{6,26},{10,30},{3... | collective-permute-start | bytes 1544 | tf_op jit(solution)/shard_map/ppermute | solution.py:19
  21.4 36.9 %collective-permute-start.8 = (bf16[256]{0:T(256)(128)(2,1)}, bf16[256]{0:T(256)(128)(2,1)}, u32[]{:S(2)}, u32[]{:S(2)}) collective-permute-start(bf16[256]{0:T(256)(128)(2,1)} %convert_element_type.239), channel_id=1, source_target_pairs={{0,24},{4,28},{1,25},{5,29},{2,26},{6,30},{3,27},{7,31}} | collective-permute-start | bytes 1544 | tf_op jit(solution)/shard_map/ppermute | solution.py:19
  23.3 32.9 %collective-permute-start.7 = (bf16[256]{0:T(256)(128)(2,1)}, bf16[256]{0:T(256)(128)(2,1)}, u32[]{:S(2)}, u32[]{:S(2)}) collective-permute-start(bf16[256]{0:T(256)(128)(2,1)} %convert_element_type.239), channel_id=1, source_target_pairs={{0,28},{1,29},{2,30},{3,31}} | collective-permute-start | bytes 1544 | tf_op jit(solution)/shard_map/ppermute | solution.py:19
  56.2 8.0 collective-permute-start.10
  58.3 8.1 collective-permute-start.11
  60.5 93.4 %collective-permute-start.6 = (bf16[256,4,128]{0,2,1:T(8,128)(2,1)}, bf16[256,4,128]{0,2,1:T(8,128)(2,1)}, u32[]{:S(2)}, u32[]{:S(2)}) collective-permute-start(bf16[256,4,128]{0,2,1:T(8,128)(2,1)} %bitcast.284), channel_id=1, source_target_pairs={{0,4},{4,8},{8,12},{12,16},{16,20},{20,24},{24,28},{1,5},{5,9},{9,... | collective-permute-start | bytes 786440 | tf_op jit(solution)/shard_map/ppermute | solution.py:19
  64.2 88.7 %collective-permute-start.5 = (bf16[256,4,128]{0,2,1:T(8,128)(2,1)}, bf16[256,4,128]{0,2,1:T(8,128)(2,1)}, u32[]{:S(2)}, u32[]{:S(2)}) collective-permute-start(bf16[256,4,128]{0,2,1:T(8,128)(2,1)} %bitcast.285), channel_id=1, source_target_pairs={{0,8},{4,12},{8,16},{12,20},{16,24},{20,28},{1,9},{5,13},{9,17},{1... | collective-permute-start | bytes 786440 | tf_op jit(solution)/shard_map/ppermute | solution.py:19
  66.4 33.1 %collective-permute-start.16 = (bf16[256,4,128]{2,0,1:T(8,128)(2,1)}, bf16[256,4,128]{2,0,1:T(8,128)(2,1)}, u32[]{:S(2)}, u32[]{:S(2)}) collective-permute-start(bf16[256,4,128]{2,0,1:T(8,128)(2,1)} %get-tuple-element.70), channel_id=1, source_target_pairs={{0,20},{4,24},{8,28},{1,21},{5,25},{9,29},{2,22},{6,26},{10,30},{3... | collective-permute-start | bytes 786440 | tf_op jit(solution)/shard_map/ppermute | solution.py:19
  68.5 21.6 collective-permute-start.15
  71.3 16.6 collective-permute-start.14
  87.9 15.4 collective-permute-start.17
  90.2 15.4 collective-permute-start.18
  99.5 16.8 collective-permute-start.19
  103.3 15.8 collective-permute-start.20
  105.6 38.8 %collective-permute-start.2 = (bf16[256,4,128]{0,2,1:T(8,128)(2,1)S(1)}, bf16[256,4,128]{0,2,1:T(8,128)(2,1)S(1)}, u32[]{:S(2)}, u32[]{:S(2)}) collective-permute-start(bf16[256,4,128]{0,2,1:T(8,128)(2,1)S(1)} %bitcast.286), channel_id=1, source_target_pairs={{0,20},{4,24},{8,28},{1,21},{5,25},{9,29},{2,22},{6,26},{10,30},{3... | collective-permute-start | bytes 786440 | tf_op jit(solution)/shard_map/ppermute | solution.py:19
  116.3 19.6 collective-permute-start
  119.1 23.4 collective-permute-start.1
  135.9 12.2 collective-permute-start.3
  142.5 10.3 collective-permute-start.4
  668.2 367.9 %all-to-all-start.1 = ((bf16[8,2,256,2048]{3,2,1,0:T(8,128)(2,1)}), bf16[8,2,256,2048]{3,2,1,0:T(8,128)(2,1)}, u32[]{:S(2)}, u32[]{:S(2)}) async-start(bf16[8,2,256,2048]{3,2,1,0:T(8,128)(2,1)} %copy.212), calls=%async_computation.1 | async-start | bytes 33554432 | tf_op jit(solution)/shard_map/all_to_all | solution.py:194
  1537.3 728.6 %all-to-all-start.3 = ((f32[8,2,256,2048]{3,2,1,0:T(8,128)}), f32[8,2,256,2048]{3,2,1,0:T(8,128)}, u32[]{:S(2)}, u32[]{:S(2)}) async-start(f32[8,2,256,2048]{3,2,1,0:T(8,128)} %copy.223), calls=%async_computation.3 | async-start | bytes 67108864 | tf_op jit(solution)/shard_map/all_to_all | solution.py:221
  1544.5 842.0 %all-reduce.16.cloned.1.call-start = ((), (), s32[]{:S(2)}) async-start(), calls=%async_computation.20 | async-start | bytes 8388608 | tf_op jit(solution)/shard_map/psum | solution.py:199
  2302.5 218.0 %reduce-scatter.20.cloned.1.call-start = ((), (), s32[]{:S(2)}) async-start(), calls=%async_computation.17 | async-start | bytes 73728 | tf_op jit(solution)/shard_map/reduce_scatter | solution.py:333
  2304.6 256.5 %reduce-scatter.22.cloned.1.call-start = ((), (), s32[]{:S(2)}) async-start(), calls=%async_computation.18 | async-start | bytes 36864
  2404.5 12.7 collective-permute-start.21
  2405.8 15.6 collective-permute-start.27
  2411.5 12.3 collective-permute-start.26
  2413.0 16.7 collective-permute-start.25
  2414.3 44.9 %collective-permute-start.24 = (bf16[256,4,128]{2,0,1:T(8,128)(2,1)S(1)}, bf16[256,4,128]{2,0,1:T(8,128)(2,1)S(1)}, u32[]{:S(2)}, u32[]{:S(2)}) collective-permute-start(bf16[256,4,128]{2,0,1:T(8,128)(2,1)S(1)} %get-tuple-element.57), channel_id=1, source_target_pairs={{16,0},{20,4},{24,8},{28,12},{17,1},{21,5},{25,9},{29,13},{18,2},{... | collective-permute-start | bytes 786440 | tf_op jit(solution)/shard_map/ppermute | solution.py:19
  2417.2 47.6 %collective-permute-start.23 = (bf16[256,4,128]{2,0,1:T(8,128)(2,1)S(1)}, bf16[256,4,128]{2,0,1:T(8,128)(2,1)S(1)}, u32[]{:S(2)}, u32[]{:S(2)}) collective-permute-start(bf16[256,4,128]{2,0,1:T(8,128)(2,1)S(1)} %get-tuple-element.58), channel_id=1, source_target_pairs={{20,0},{24,4},{28,8},{21,1},{25,5},{29,9},{22,2},{26,6},{30,10},{2... | collective-permute-start | bytes 786440 | tf_op jit(solution)/shard_map/ppermute | solution.py:19
  2421.4 44.7 %collective-permute-start.22 = (bf16[256,4,128]{2,0,1:T(8,128)(2,1)S(1)}, bf16[256,4,128]{2,0,1:T(8,128)(2,1)S(1)}, u32[]{:S(2)}, u32[]{:S(2)}) collective-permute-start(bf16[256,4,128]{2,0,1:T(8,128)(2,1)S(1)} %get-tuple-element.59), channel_id=1, source_target_pairs={{24,0},{28,4},{25,1},{29,5},{26,2},{30,6},{27,3},{31,7}} | collective-permute-start | bytes 786440 | tf_op jit(solution)/shard_map/ppermute | solution.py:19
  2423.9 60.6 %collective-permute-start.28 = (bf16[256,4,128]{0,2,1:T(8,128)(2,1)}, bf16[256,4,128]{0,2,1:T(8,128)(2,1)}, u32[]{:S(2)}, u32[]{:S(2)}) collective-permute-start(bf16[256,4,128]{0,2,1:T(8,128)(2,1)} %get-tuple-element.46), channel_id=1, source_target_pairs={{28,0},{29,1},{30,2},{31,3}} | collective-permute-start | bytes 786440 | tf_op jit(solution)/shard_map/ppermute | solution.py:19
  2429.6 56.1 %collective-permute-start.34 = (bf16[256,4,128]{0,2,1:T(8,128)(2,1)}, bf16[256,4,128]{0,2,1:T(8,128)(2,1)}, u32[]{:S(2)}, u32[]{:S(2)}) collective-permute-start(bf16[256,4,128]{0,2,1:T(8,128)(2,1)} %get-tuple-element.47), channel_id=1, source_target_pairs={{4,0},{8,4},{12,8},{16,12},{20,16},{24,20},{28,24},{5,1},{9,5},{13... | collective-permute-start | bytes 786440 | tf_op jit(solution)/shard_map/ppermute | solution.py:19
  2459.2 30.9 %collective-permute-start.33 = (bf16[256,4,128]{0,2,1:T(8,128)(2,1)}, bf16[256,4,128]{0,2,1:T(8,128)(2,1)}, u32[]{:S(2)}, u32[]{:S(2)}) collective-permute-start(bf16[256,4,128]{0,2,1:T(8,128)(2,1)} %get-tuple-element.48), channel_id=1, source_target_pairs={{8,0},{12,4},{16,8},{20,12},{24,16},{28,20},{9,1},{13,5},{17,9},{2... | collective-permute-start | bytes 786440 | tf_op jit(solution)/shard_map/ppermute | solution.py:19
  2464.8 25.3 collective-permute-start.32
  2466.1 36.6 %collective-permute-start.31 = (bf16[256,4,128]{0,2,1:T(8,128)(2,1)}, bf16[256,4,128]{0,2,1:T(8,128)(2,1)}, u32[]{:S(2)}, u32[]{:S(2)}) collective-permute-start(bf16[256,4,128]{0,2,1:T(8,128)(2,1)} %get-tuple-element.50), channel_id=1, source_target_pairs={{16,0},{20,4},{24,8},{28,12},{17,1},{21,5},{25,9},{29,13},{18,2},{... | collective-permute-start | bytes 786440 | tf_op jit(solution)/shard_map/ppermute | solution.py:19
  2483.4 118.1 %reduce-scatter.24.cloned.1.call-start = ((), (), s32[]{:S(2)}) async-start(), calls=%async_computation.19 | async-start | bytes 36864
  2484.2 154.7 %all-reduce.14.cloned.1.call-start = ((), (), s32[]{:S(2)}) async-start(), calls=%async_computation.12 | async-start | bytes 2097152 | tf_op jit(solution)/shard_map/psum | solution.py:302
  2484.5 23.4 collective-permute-start.30
  2485.8 22.1 collective-permute-start.29
  2511.4 199.9 %reduce-scatter.18.cloned.1.call-start = ((), (), s32[]{:S(2)}) async-start(), calls=%async_computation.16 | async-start | bytes 2359296 | tf_op jit(solution)/shard_map/reduce_scatter | solution.py:327
  2513.5 268.5 %reduce-scatter.16.cloned.1.call-start = ((), (), s32[]{:S(2)}) async-start(), calls=%async_computation.15 | async-start | bytes 2359296 | tf_op jit(solution)/shard_map/reduce_scatter | solution.py:318
  2517.0 335.7 %reduce-scatter.14.cloned.1.call-start = ((), (), s32[]{:S(2)}) async-start(), calls=%async_computation.14 | async-start | bytes 2359296 | tf_op jit(solution)/shard_map/reduce_scatter | solution.py:315
  2519.2 404.1 %reduce-scatter.12.cloned.1.call-start = ((), (), s32[]{:S(2)}) async-start(), calls=%async_computation.13 | async-start | bytes 2359296 | tf_op jit(solution)/shard_map/reduce_scatter | solution.py:312
  (89 other events, 2272.7 us)
Sparse Core Ops, SparseCore 0:
  165.6 57.9 all-reduce.11
  2302.6 83.7 all-reduce.15
  2389.6 64.0 reduce-scatter.19
  2483.5 62.3 reduce-scatter.21
  2548.9 52.5 reduce-scatter.23
  2603.7 35.1 all-reduce.13
  2642.9 68.4 reduce-scatter.17
  2715.3 66.7 reduce-scatter.15
  2786.0 66.5 reduce-scatter.13
  2856.5 66.8 reduce-scatter.11
where the time goes:
time: 2940 us; the launch traced here: 2930 us
  waiting for transfers between devices  1500 us (51%)
  blocking collectives  784 us (27%)
  local copies, waits for them, and re-layouts  252 us (9%)
  matrix products  168 us (6%)
  starting transfers between devices  109 us (4%)
  other arithmetic  102 us (3%)
    all_to_all x1, waiting for transfers between devices, per_device(): lax.all_to_all(row_grad, 'dp', split_axis=0, concat_axis=0, tiled=True)  635 us
    all_to_all x1, blocking collectives, per_device(): lax.all_to_all(padded[slot_grid], 'dp', split_axis=0, concat_axis=0, tile...  371 us
    all_to_all x1, blocking collectives, per_device(): lax.all_to_all(part_grad, 'dp', split_axis=0, concat_axis=0, tiled=True)  368 us
    all_to_all x1, waiting for transfers between devices, per_device(): lax.all_to_all(partial_rows, 'dp', split_axis=0, concat_axis=0, tiled=True)  324 us
    ppermute x35, starting transfers between devices, from_behind(): return lax.ppermute(array, axis, pairs)  95.6 us
    ppermute x35, waiting for transfers between devices, from_behind(): return lax.ppermute(array, axis, pairs)  85.2 us
    psum x1, waiting for transfers between devices, per_device(): expert_full, gate_grad = lax.psum((expert_part, gate_dots), 'tensor')  81.6 us
    reduce_scatter x1, waiting for transfers between devices, per_device(): lax.psum_scatter(d_value.astype(jnp.bfloat16), 'dp', scatter_dimension=0,...  69 us
  transfers between devices with their start and end apart: 47, of which 22 were waited for; matrix products, arithmetic and copies ran while one was open for 9% of the time, Pallas kernels for 0%

commit v1 on v0

v1 whole, which is shorter than its diff:
```python
import functools
import math

import jax
import jax.numpy as jnp
from jax import lax
from jax.experimental import pallas as pl
from jax.experimental.pallas import tpu as pltpu
from jax.sharding import PartitionSpec as P

SPAN = 8


EPSILON = 1e-05
ROPE_BASE = 10000.0
NEGATIVE = -1e30
BF = jnp.bfloat16
F32 = jnp.float32
EVERY = ("dp", "tensor")
VMEM_LIMIT = 56 * 1024 * 1024
LANES = 128


def rope_tables(positions, head_size):
    frequency = ROPE_BASE ** (-jnp.arange(0, head_size, 2, dtype=jnp.float32) / head_size)
    angles = positions[:, None] * frequency[None, :]
    cos_table = jnp.concatenate([jnp.cos(angles), jnp.cos(angles)], -1)[:, None, :]
    sin_table = jnp.concatenate([jnp.sin(angles), jnp.sin(angles)], -1)[:, None, :]
    return (cos_table, sin_table)


def rotate(vector, cos_table, sin_table):
    half_size = vector.shape[-1] // 2
    turned = jnp.concatenate([-vector[..., half_size:], vector[..., :half_size]], -1)
    return vector * cos_table + turned * sin_table


def unrotate(gradient, cos_table, sin_table):
    half_size = gradient.shape[-1] // 2
    scaled = gradient * sin_table
    turned = jnp.concatenate([scaled[..., half_size:], -scaled[..., :half_size]], -1)
    return gradient * cos_table + turned


def dot(left_side, right_side, left_dim, right_dim):
    return lax.dot_general(
        left_side,
        right_side,
        (((left_dim,), (right_dim,)), ((), ())),
        preferred_element_type=jnp.float32,
    )


def span_groups(owners):
    return [list(range(g, g + SPAN)) for g in range(0, owners, SPAN)]


def swap(array, axis, bit):
    count = lax.axis_size(axis)
    return lax.ppermute(array, axis, [(i, i ^ bit) for i in range(count)])


def pick(array, index):
    return lax.dynamic_index_in_dim(array, index, 0, keepdims=False)


def sum_tensor(partial, place):
    rows = partial.shape[0] // 4
    blocks = partial.reshape(2, 2, rows, partial.shape[1])
    core, side = place % 2, place // 2
    given = lax.dynamic_index_in_dim(blocks, 1 - core, 1, keepdims=False).astype(BF)
    kept = lax.dynamic_index_in_dim(blocks, core, 1, keepdims=False)
    kept = kept + swap(given, "tensor", 1).astype(F32)
    return pick(kept, side) + swap(pick(kept, 1 - side).astype(BF), "tensor", 2).astype(F32)


def spread_tensor(block, place):
    core, side = place % 2, place // 2
    other = swap(block, "tensor", 2)
    both = jnp.where(side == 0, jnp.stack([block, other]), jnp.stack([other, block]))
    across = swap(both, "tensor", 1)
    full = jnp.where(core == 0, jnp.stack([both, across], 1), jnp.stack([across, both], 1))
    return full.reshape((4 * block.shape[0],) + block.shape[1:])


def resident(shape):
    return pl.BlockSpec(shape, lambda *_: (0,) * len(shape), pipeline_mode=pl.Buffered(1))


def cost(macs, size, transcendentals=0):
    return pl.CostEstimate(flops=2 * macs, bytes_accessed=size, transcendentals=transcendentals)


PARAMS = pltpu.CompilerParams(vmem_limit_bytes=VMEM_LIMIT)


def turn_kernel(gate_ref, up_ref, down_ref, both_ref, down_out_ref):
    count, _, hidden = gate_ref.shape
    for e in range(count):
        both_ref[pl.ds(e * hidden, hidden), :] = gate_ref[e].T
        both_ref[pl.ds((count + e) * hidden, hidden), :] = up_ref[e].T
        down_out_ref[:, pl.ds(e * hidden, hidden)] = down_ref[e].T


def turn_weights(w_gate, w_up, w_down, block=256):
    count, width, hidden = w_gate.shape
    mid = count * hidden
    rows = pl.BlockSpec((count, block, hidden), lambda d: (0, d, 0))
    return pl.pallas_call(
        turn_kernel,
        grid=(width // block,),
        in_specs=[rows, rows, pl.BlockSpec((count, hidden, block), lambda d: (0, 0, d))],
        out_specs=[
            pl.BlockSpec((2 * mid, block), lambda d: (0, d)),
            pl.BlockSpec((block, mid), lambda d: (d, 0)),
        ],
        out_shape=[
            jax.ShapeDtypeStruct((2 * mid, width), BF),
            jax.ShapeDtypeStruct((width, mid), BF),
        ],
        compiler_params=PARAMS,
        cost_estimate=cost(0, 12 * mid * width),
    )(w_gate, w_up, w_down)


def expert_kernel(
    experts, first_ref, rows_ref, grad_ref, gate_ref, up_ref, down_ref, *outs
):
    low_ref, dots_ref, hid_ref, hid_turned_ref, glow_ref, ulow_ref = outs
    count, width, hidden_size = gate_ref.shape
    mid = count * hidden_size
    rows = rows_ref[:, :width]
    side = rows_ref[:, width:].astype(F32)
    lane = lax.broadcasted_iota(jnp.int32, side.shape, 1)
    dots = jnp.zeros(side.shape, F32)
    back_all = dot(grad_ref[...], down_ref[...], 1, 0)
    for e in range(count):
        column = first_ref[0] + e
        gate = jnp.sum(
            jnp.where((lane == column) | (lane == experts + column), side, 0.0), -1, keepdims=True
        )
        gate_pre = dot(rows, gate_ref[e], 1, 0)
        up_pre = dot(rows, up_ref[e], 1, 0)
        out_back = back_all[:, e * hidden_size : (e + 1) * hidden_size]
        sigma = 1.0 / (1.0 + jnp.exp(-gate_pre))
        silu = gate_pre * sigma
        hidden = silu * up_pre
        inner = jnp.sum(hidden * out_back, -1, keepdims=True)
        high = inner.astype(BF).astype(F32)
        dots = jnp.where(lane == column, high, dots)
        dots = jnp.where(lane == experts + column, inner - high, dots)
        hidden_low = (gate * hidden).astype(BF)
        hidden_grad = gate * out_back
        glow = (hidden_grad * up_pre * sigma * (1.0 + gate_pre * (1.0 - sigma))).astype(BF)
        ulow = (hidden_grad * silu).astype(BF)
        span = pl.ds(e * hidden_size, hidden_size)
        hid_ref[:, span] = hidden_low
        hid_turned_ref[span, :] = hidden_low.T
        glow_ref[:, span] = glow
        ulow_ref[:, span] = ulow
        low_ref[:, pl.ds(e * hidden_size, hidden_size)] = glow
        low_ref[:, pl.ds(mid + e * hidden_size, hidden_size)] = ulow
    dots_ref[...] = dots.astype(BF)


def expert_rows(rows_all, grad_all, w_gate, w_up, down_turned, first, experts, block):
    count, width, hidden = w_gate.shape
    total, wide = rows_all.shape
    mid = count * hidden

    def rows(columns):
        return pl.BlockSpec((block, columns), lambda i, *_: (i, 0))

    def shape(columns):
        return jax.ShapeDtypeStruct((total, columns), BF)

    return pl.pallas_call(
        functools.partial(expert_kernel, experts),
        grid_spec=pltpu.PrefetchScalarGridSpec(
            num_scalar_prefetch=1,
            grid=(total // block,),
            in_specs=[
                rows(wide),
                rows(width),
                resident(w_gate.shape),
                resident(w_up.shape),
                resident(down_turned.shape),
            ],
            out_specs=[
                rows(2 * mid),
                rows(wide - width),
                rows(mid),
                pl.BlockSpec((mid, block), lambda i, *_: (0, i)),
                rows(mid),
                rows(mid),
            ],
        ),
        out_shape=[
            shape(2 * mid),
            shape(wide - width),
            shape(mid),
            jax.ShapeDtypeStruct((mid, total), BF),
            shape(mid),
            shape(mid),
        ],
        compiler_params=PARAMS,
        cost_estimate=cost(3 * total * width * mid, total * wide * 6, total * mid),
    )(first, rows_all, grad_all, w_gate, w_up, down_turned)


def back_kernel(with_dots, index_ref, low_ref, both_ref, dots_ref, kept_ref, sent_ref):
    own = kept_ref.shape[2]
    place = index_ref[1]
    starts = [pl.multiple_of((r ^ place) * own, own) for r in range(4)]
    low = jnp.concatenate([low_ref[pl.ds(start, own), :] for start in starts], 0)
    back = dot(low, both_ref[...], 1, 0).astype(BF)
    columns = back.shape[1]
    for r in range(4):
        ref = sent_ref if r % 2 else kept_ref
        ref[0, r // 2, :, :columns] = back[r * own : (r + 1) * own]
        if with_dots:
            ref[0, r // 2, :, columns:] = dots_ref[pl.ds(starts[r], own), :]


def row_back(low, dots, both_turned, index, begin, end, with_dots):
    total, mid2 = low.shape
    block = 4 * (total // (4 * lax.axis_size("dp")))
    side = dots.shape[1] if with_dots else 0
    columns = end - begin
    owners = total // block
    out = pl.BlockSpec(
        (1, 2, block // 4, columns + side), lambda i, index_ref: (i ^ index_ref[0], 0, 0, 0)
    )
    shape = jax.ShapeDtypeStruct((owners, 2, block // 4, columns + side), BF)
    return pl.pallas_call(
        functools.partial(back_kernel, with_dots),
        grid_spec=pltpu.PrefetchScalarGridSpec(
            num_scalar_prefetch=1,
            grid=(owners,),
            in_specs=[
                pl.BlockSpec((block, mid2), lambda i, *_: (i, 0)),
                pl.BlockSpec(
                    (mid2, pl.Element(columns)), lambda i, *_: (0, begin), pipeline_mode=pl.Buffered(1)
                )
                if begin % columns
                else pl.BlockSpec(
                    (mid2, columns),
                    lambda i, *_: (0, begin // columns),
                    pipeline_mode=pl.Buffered(1),
                ),
                pl.BlockSpec((block, dots.shape[1]), lambda i, *_: (i, 0)),
            ],
            out_specs=[out, out],
        ),
        out_shape=[shape, shape],
        compiler_params=PARAMS,
        cost_estimate=cost(total * mid2 * columns, total * (mid2 + columns) * 2),
    )(index, low, both_turned, dots)


def sum_every(kept, sent, order):
    bits = lax.axis_size("dp").bit_length() - 1
    own, columns = kept.shape[2:]
    total = (kept.astype(F32) + swap(sent, "tensor", 1).astype(F32)).astype(BF)
    total = total.reshape((2,) * (bits + 1) + (own, columns))
    names = [("dp", 1 << (bits - 1 - i)) for i in range(bits)] + [("tensor", 2)]
    for name in order:
        axis = names.index(name)
        names.pop(axis)
        given = lax.index_in_dim(total, 1, axis, keepdims=False)
        total = lax.index_in_dim(total, 0, axis, keepdims=False).astype(F32)
        total = total + swap(given, *name).astype(F32)
        if names:
            total = total.astype(BF)
    return total


def out_kernel(hid_ref, down_ref, out_ref):
    count, hidden, _ = down_ref.shape
    out = dot(hid_ref[...], down_ref[...].reshape(count * hidden, -1), 1, 0)
    out_ref[...] = out.astype(BF)


def expert_out(hid, w_down, block=256):
    count, hidden, width = w_down.shape
    total = hid.shape[0]
    return pl.pallas_call(
        out_kernel,
        grid=(total // block,),
        in_specs=[
            pl.BlockSpec((block, count * hidden), lambda i: (i, 0)),
            resident(w_down.shape),
        ],
        out_specs=pl.BlockSpec((block, width), lambda i: (i, 0)),
        out_shape=jax.ShapeDtypeStruct((total, width), BF),
        compiler_params=PARAMS,
        cost_estimate=cost(total * width * count * hidden, total * width * 3),
    )(hid, w_down)


def over_kernel(left_ref, right_ref, out_ref):
    count, _, hidden = out_ref.shape
    product = dot(left_ref[...], right_ref[...], 0, 0)

    @pl.when(pl.program_id(1) == 0)
    def _():
        for e in range(count):
            out_ref[e] = product[:, e * hidden : (e + 1) * hidden]

    @pl.when(pl.program_id(1) > 0)
    def _():
        for e in range(count):
            out_ref[e] += product[:, e * hidden : (e + 1) * hidden]


def over_rows(rows, low, shape, block=256, chunk=2048):
    count, width, hidden = shape
    total = rows.shape[0]
    chunk = min(chunk, total)
    return pl.pallas_call(
        over_kernel,
        grid=(width // block, total // chunk),
        in_specs=[
            pl.BlockSpec((chunk, block), lambda d, k: (k, d)),
            pl.BlockSpec((chunk, count * hidden), lambda d, k: (k, 0)),
        ],
        out_specs=pl.BlockSpec((count, block, hidden), lambda d, k: (0, d, 0)),
        out_shape=jax.ShapeDtypeStruct(shape, F32),
        compiler_params=PARAMS,
        cost_estimate=cost(total * width * count * hidden, total * width * 4),
    )(rows, low)


def turned_kernel(left_ref, right_ref, out_ref):
    product = dot(left_ref[...], right_ref[...], 1, 0)

    @pl.when(pl.program_id(1) == 0)
    def _():
        out_ref[...] = product

    @pl.when(pl.program_id(1) > 0)
    def _():
        out_ref[...] += product


def turned_rows(left, right, block=256, chunk=2048):
    mid, total = left.shape
    width = right.shape[1]
    chunk = min(chunk, total)
    return pl.pallas_call(
        turned_kernel,
        grid=(width // block, total // chunk),
        in_specs=[
            pl.BlockSpec((mid, chunk), lambda d, k: (0, k)),
            pl.BlockSpec((chunk, block), lambda d, k: (k, d)),
        ],
        out_specs=pl.BlockSpec((mid, block), lambda d, k: (0, d)),
        out_shape=jax.ShapeDtypeStruct((mid, width), F32),
        compiler_params=PARAMS,
        cost_estimate=cost(total * width * mid, total * width * 4),
    )(left, right)


def per_device(
    tokens,
    segment_ids,
    routes,
    norm1_gain,
    w_query,
    w_key,
    w_value,
    query_gain,
    key_gain,
    w_out,
    norm2_gain,
    w_router,
    w_gate,
    w_up,
    w_down,
    cotangent,
):
    tok_count, model_width = tokens.shape
    heads_here, head_size = query_gain.shape
    local_width = heads_here * head_size
    tensor_count = lax.axis_size("tensor")
    full_width = local_width * tensor_count
    experts = w_router.shape[1]
    owners = lax.axis_size("dp")
    local_experts, _, local_hidden = w_gate.shape
    dp_place = lax.axis_index("dp")
    place = lax.axis_index("tensor")
    score_root = math.sqrt(head_size)
    own = tok_count // tensor_count
    parts = SPAN // heads_here
    part = tok_count // parts
    groups = span_groups(owners)

    def mine(array):
        return lax.dynamic_slice_in_dim(array, place * own, own, 0)

    def trade(array):
        return lax.all_to_all(
            array, "dp", split_axis=0, concat_axis=0, tiled=True, axis_index_groups=groups
        )

    out_grad_all = lax.all_gather(mine(cotangent), EVERY, axis=0, tiled=True)
    both_turned, down_turned = turn_weights(w_gate, w_up, w_down)

    state_in = tokens.astype(F32)
    scale_in = lax.rsqrt(jnp.mean(state_in * state_in, -1, keepdims=True) + EPSILON)
    unit_in = state_in * scale_in
    normed_in = (unit_in * norm1_gain).astype(BF)
    normed_in_all = lax.all_gather(mine(normed_in), EVERY, axis=0, tiled=True)
    query_raw = jnp.dot(normed_in, w_query, preferred_element_type=F32)
    key_raw = jnp.dot(normed_in, w_key, preferred_element_type=F32)
    value_att = jnp.dot(normed_in, w_value, preferred_element_type=F32).astype(BF)
    squares = lax.psum(
        jnp.stack([jnp.sum(query_raw * query_raw, -1), jnp.sum(key_raw * key_raw, -1)]), "tensor"
    )
    query_scale = lax.rsqrt(squares[0] / full_width + EPSILON)[:, None]
    key_scale = lax.rsqrt(squares[1] / full_width + EPSILON)[:, None]
    query_unit = query_raw * query_scale
    key_unit = key_raw * key_scale
    local_pos = jnp.arange(tok_count, dtype=jnp.int32)
    positions = (dp_place % SPAN * tok_count + local_pos).astype(F32)
    cos_table, sin_table = rope_tables(positions, head_size)
    query_att = rotate(
        (query_unit * query_gain.reshape(-1)).reshape(tok_count, heads_here, head_size),
        cos_table,
        sin_table,
    ).astype(BF)
    key_att = rotate(
        (key_unit * key_gain.reshape(-1)).reshape(tok_count, heads_here, head_size),
        cos_table,
        sin_table,
    ).astype(BF)

    def head_parts(array):
        split = array.reshape(parts, part, heads_here, head_size)
        return split.transpose(2, 0, 1, 3)

    def head_blocks(array):
        split = array.reshape(tok_count, heads_here, head_size).transpose(1, 0, 2)
        return jnp.broadcast_to(
            split[:, None], (heads_here, parts, tok_count, head_size)
        )

    segment_rows = jnp.zeros((16, head_size), BF).at[: tok_count // head_size].set(
        segment_ids.astype(BF).reshape(-1, head_size)
    )
    segment_rows = jnp.broadcast_to(segment_rows, (heads_here, parts) + segment_rows.shape)
    sent = jnp.concatenate(
        [head_parts(query_att), head_blocks(key_att), head_blocks(value_att), segment_rows], 2
    ).reshape(SPAN, part + 2 * tok_count + 16, head_size)
    got = trade(sent)
    seq = SPAN * tok_count
    query_h = got[:, :part].reshape(SPAN * part, head_size)
    key_h = got[:, part : part + tok_count].reshape(seq, head_size)
    value_h = got[:, part + tok_count : part + 2 * tok_count].reshape(seq, head_size)
    segment_h = got[:, part + 2 * tok_count :].reshape(SPAN, -1)[:, :tok_count]
    half = dp_place % SPAN % parts
    key_pos = jnp.arange(seq, dtype=jnp.int32)
    query_pos = (
        jnp.arange(SPAN, dtype=jnp.int32)[:, None] * tok_count
        + half * part
        + jnp.arange(part, dtype=jnp.int32)[None]
    ).reshape(-1)
    segment_q = lax.dynamic_slice_in_dim(segment_h, half * part, part, 1).reshape(-1)
    visible = (segment_h.reshape(-1)[None, :] == segment_q[:, None]) & (
        key_pos[None, :] <= query_pos[:, None]
    )
    raw_scores = dot(query_h, key_h, 1, 1) / score_root
    masked = jnp.where(visible, raw_scores, NEGATIVE)
    row_top = jnp.max(masked, -1, keepdims=True)
    log_total = row_top + jnp.log(jnp.sum(jnp.exp(masked - row_top), -1, keepdims=True))
    attn_probs = jnp.where(visible, jnp.exp(masked - log_total), 0.0)
    probs_low = attn_probs.astype(BF)
    mix_h = dot(probs_low, value_h, 1, 0).astype(BF)

    def to_tokens(array):
        back = trade(array).reshape(heads_here, parts, part, head_size)
        return back.transpose(1, 2, 0, 3).reshape(tok_count, local_width)

    attn_mix = to_tokens(mix_h.reshape(SPAN, part, head_size))
    attn_full = sum_tensor(jnp.dot(attn_mix, w_out, preferred_element_type=F32), place)
    resid_state = mine(state_in) + attn_full
    scale_mid = lax.rsqrt(jnp.mean(resid_state * resid_state, -1, keepdims=True) + EPSILON)
    unit_mid = resid_state * scale_mid
    normed_mid = (unit_mid * norm2_gain).astype(BF)
    logits = jnp.dot(normed_mid, w_router, preferred_element_type=F32)
    router_probs = jax.nn.softmax(logits, -1)
    chosen = jnp.sum(
        (mine(routes)[:, :, None] == jnp.arange(experts, dtype=jnp.int32)).astype(F32), 1
    )
    gates = router_probs * chosen
    gates_high = gates.astype(BF)
    gates_low = (gates - gates_high.astype(F32)).astype(BF)
    side_width = -(-2 * experts // 128) * 128
    side = jnp.concatenate(
        [gates_high, gates_low, jnp.zeros((own, side_width - 2 * experts), BF)], 1
    )
    rows_all = lax.all_gather(
        jnp.concatenate([normed_mid, side], 1), EVERY, axis=0, tiled=True
    )
    index = jnp.stack([dp_place, place]).astype(jnp.int32)
    first = (dp_place * local_experts).astype(jnp.int32).reshape(1)
    low, dots, hid, hid_turned, glow, ulow = expert_rows(
        rows_all, out_grad_all, w_gate, w_up, down_turned, first, experts, tok_count
    )
    bits = owners.bit_length() - 1
    first_three = [("tensor", 2), ("dp", 1), ("dp", 2)]
    rest = [("dp", 1 << b) for b in range(2, bits)]
    lanes = -(-(model_width + side_width) // (3 * LANES)) * LANES
    homes = []
    for g in range(3):
        begin, end = g * lanes, min((g + 1) * lanes, model_width)
        kept, sent = row_back(low, dots, both_turned, index, begin, end, g == 2)
        homes.append(sum_every(kept, sent, first_three[g:] + first_three[:g] + rest))
    home = jnp.concatenate(homes, 1)
    out_part = expert_out(hid, w_down)
    expert_full = lax.psum_scatter(out_part, EVERY, scatter_dimension=0, tiled=True).astype(F32)
    block_output = spread_tensor((resid_state + expert_full).astype(BF), place)
    d_w_down = turned_rows(hid_turned, out_grad_all).reshape(w_down.shape)
    d_w_gate = over_rows(rows_all, glow, w_gate.shape)
    d_w_up = over_rows(rows_all, ulow, w_up.shape)

    row_home = home[:, :model_width]
    side_home = home[:, model_width:]
    probs_grad = chosen * (side_home[:, :experts] + side_home[:, experts : 2 * experts])
    logit_low = (
        router_probs * (probs_grad - jnp.sum(router_probs * probs_grad, -1, keepdims=True))
    ).astype(BF)
    d_router = dot(logit_low, normed_mid, 0, 0)
    mid_grad = row_home + dot(logit_low, w_router, 1, 1)
    d_gain_mid = jnp.sum(mid_grad * unit_mid, 0)
    mid_scaled = mid_grad * norm2_gain
    resid_grad = mine(cotangent).astype(F32) + scale_mid * (
        mid_scaled - unit_mid * jnp.mean(mid_scaled * unit_mid, -1, keepdims=True)
    )
    resid_low = spread_tensor(resid_grad.astype(BF), place)
    d_out = dot(attn_mix, resid_low, 0, 0)
    d_out = lax.psum_scatter(d_out.astype(BF), "dp", scatter_dimension=1, tiled=True).astype(F32)
    mix_grad = head_parts(dot(resid_low, w_out, 1, 1).astype(BF)).reshape(SPAN, part, head_size)
    mix_grad_h = trade(mix_grad).reshape(SPAN * part, head_size)

    p_grad = dot(mix_grad_h, value_h, 1, 1)
    score_low = (attn_probs * (p_grad - jnp.sum(attn_probs * p_grad, -1, keepdims=True))).astype(BF)
    query_back = (dot(score_low, key_h, 1, 0) / score_root).astype(BF)
    key_back = (dot(score_low, query_h, 0, 0) / score_root).astype(BF)
    value_back = dot(probs_low, mix_grad_h, 0, 0).astype(BF)
    back = trade(
        jnp.concatenate(
            [
                query_back.reshape(SPAN, part, head_size),
                key_back.reshape(SPAN, tok_count, head_size),
                value_back.reshape(SPAN, tok_count, head_size),
            ],
            1,
        )
    ).reshape(heads_here, parts, part + 2 * tok_count, head_size)
    query_att_grad = (
        back[:, :, :part].transpose(1, 2, 0, 3).reshape(tok_count, heads_here, head_size)
    )
    key_att_grad = jnp.sum(back[:, :, part : part + tok_count].astype(F32), 1).astype(BF)
    key_att_grad = key_att_grad.transpose(1, 0, 2)
    value_low = jnp.sum(back[:, :, part + tok_count :].astype(F32), 1).astype(BF)
    value_low = value_low.transpose(1, 0, 2).reshape(tok_count, local_width)

    query_gain_in = unrotate(query_att_grad.astype(F32), cos_table, sin_table).reshape(
        tok_count, local_width
    )
    key_gain_in = unrotate(key_att_grad.astype(F32), cos_table, sin_table).reshape(
        tok_count, local_width
    )
    d_query_gain = jnp.sum(query_gain_in * query_unit, 0).reshape(heads_here, head_size)
    d_key_gain = jnp.sum(key_gain_in * key_unit, 0).reshape(heads_here, head_size)
    query_scaled = query_gain_in * query_gain.reshape(-1)
    key_scaled = key_gain_in * key_gain.reshape(-1)
    inner = lax.psum(
        jnp.stack([jnp.sum(query_scaled * query_unit, -1), jnp.sum(key_scaled * key_unit, -1)]),
        "tensor",
    )
    query_low = (
        query_scale * (query_scaled - query_unit * (inner[0] / full_width)[:, None])
    ).astype(BF)
    key_low = (key_scale * (key_scaled - key_unit * (inner[1] / full_width)[:, None])).astype(BF)

    slice_width = local_width // owners
    columns = jnp.stack([query_low.T, key_low.T, value_low.T])
    columns = columns.reshape(3, owners, slice_width, tok_count).transpose(1, 0, 2, 3)
    columns = columns.reshape(owners, 3 * slice_width, tok_count)
    columns = lax.all_to_all(columns, "dp", split_axis=0, concat_axis=0, tiled=True)
    columns = columns.transpose(1, 0, 2).reshape(3 * slice_width, owners * tok_count)
    d_columns = dot(columns, normed_in_all, 1, 0)

    in_part = (
        dot(query_low, w_query, 1, 1) + dot(key_low, w_key, 1, 1) + dot(value_low, w_value, 1, 1)
    )
    in_grad_norm = sum_tensor(in_part, place)
    unit_own = mine(unit_in)
    d_gain_in = jnp.sum(in_grad_norm * unit_own, 0)
    in_scaled = in_grad_norm * norm1_gain
    input_grad = resid_grad + mine(scale_in) * (
        in_scaled - unit_own * jnp.mean(in_scaled * unit_own, -1, keepdims=True)
    )
    input_grad = spread_tensor(input_grad.astype(BF), place).astype(F32)

    model_slice = model_width // owners
    head_slice = head_size // owners
    gains = jnp.stack([d_query_gain, d_key_gain]).reshape(2 * heads_here, owners, head_slice)
    gains = gains.transpose(1, 0, 2).reshape(owners, 1, 2 * heads_here * head_slice)
    gains = jnp.pad(gains, ((0, 0), (0, 0), (0, max(0, model_slice - gains.shape[2]))))
    gain_rows = gains.reshape(owners, -1, model_slice)
    by_owner = jnp.concatenate([d_router, d_gain_mid[None], d_gain_in[None]], 0)
    by_owner = by_owner.reshape(-1, owners, model_slice).transpose(1, 0, 2)
    small = jnp.concatenate([by_owner, gain_rows], 1).astype(BF)
    pad_rows = -small.shape[1] % 16
    small = jnp.pad(small, ((0, 0), (0, pad_rows), (0, 0)))
    big = d_columns.reshape(3 * slice_width, owners, model_slice).transpose(1, 0, 2).astype(BF)
    final = lax.all_to_all(
        jnp.concatenate([big, small], 1), "dp", split_axis=0, concat_axis=0, tiled=True
    ).astype(F32)
    weights = final[:, : 3 * slice_width].reshape(owners, 3, slice_width, model_slice)
    weights = weights.transpose(1, 3, 0, 2).reshape(3, model_slice, local_width)
    small = jnp.sum(final[:, 3 * slice_width :], 0)
    shared = lax.psum(small[: experts + 2], "tensor")
    gains = small[experts + 2 : experts + 2 + gain_rows.shape[1]].reshape(-1)
    gains = gains[: 2 * heads_here * head_slice].reshape(2, heads_here, head_slice)

    return (
        block_output,
        input_grad,
        shared[experts + 1],
        weights[0],
        weights[1],
        weights[2],
        gains[0],
        gains[1],
        d_out,
        shared[experts],
        shared[:experts].T,
        d_w_gate,
        d_w_up,
        d_w_down,
    )


def solution(mesh):
    in_specs = (
        P("dp", None),
        P("dp"),
        P("dp", None),
        P(),
        P(None, "tensor"),
        P(None, "tensor"),
        P(None, "tensor"),
        P("tensor", None),
        P("tensor", None),
        P("tensor", None),
        P(),
        P(),
        P("dp", None, "tensor"),
        P("dp", None, "tensor"),
        P("dp", "tensor", None),
        P("dp", None),
    )
    out_specs = (
        P("dp", None),
        P("dp", None),
        P("dp"),
        P("dp", "tensor"),
        P("dp", "tensor"),
        P("dp", "tensor"),
        P("tensor", "dp"),
        P("tensor", "dp"),
        P("tensor", "dp"),
        P("dp"),
        P("dp", None),
        P("dp", None, "tensor"),
        P("dp", None, "tensor"),
        P("dp", "tensor", None),
    )
    return jax.shard_map(
        per_device, mesh=mesh, in_specs=in_specs, out_specs=out_specs, check_vma=False
    )
```

time: 2940 us -> 663 us (0.23)
  waiting for transfers between devices: 1500 us -> 233 us
  blocking collectives: 784 us -> 88.8 us
  local copies, waits for them, and re-layouts: 252 us -> 70.3 us
  matrix products: 168 us -> 38.2 us
  Pallas kernels: 0 us -> 101 us
  starting transfers between devices: 109 us -> 49.2 us
  other arithmetic: 102 us -> 58 us
    all_to_all x2 -> x4, waiting for transfers between devices: 960 us -> 65.6 us  [the longest x2 58.6 us: trade(): lax.all_to_all(array, 'dp', split_axis=0, concat_axis=0, tiled=True, axis...]
    all_to_all x2, blocking collectives: 739 us -> 62.7 us  [trade(): lax.all_to_all(array, 'dp', split_axis=0, concat_axis=0, tiled=True, axis...]
    reduce_scatter x5 -> x2, waiting for transfers between devices: 250 us -> 11 us  [the longest x1 11 us: per_device(): lax.psum_scatter(out_part, EVERY, scatter_dimension=0, tiled=True)]
    psum x3 -> x0, waiting for transfers between devices: 166 us -> none  [the longest x1 81.6 us: per_device(): expert_full, gate_grad = lax.psum((expert_part, gate_dots), 'tensor')]
    dot_general x30 -> x19, matrix products: 168 us -> 38.2 us  [the longest x14 29.2 us: dot(): lax.dot_general(left_side, right_side, (((left_dim,), (right_dim,)), ((),...]
    gather x4 -> x0, local copies, waits for them, and re-layouts: 106 us -> none  [the longest x1 33.3 us: per_device(): grad_padded[slot_grid]]
    pallas_call x0 -> x9, Pallas kernels: none -> 101 us  [the longest x3 28.2 us: row_back(): pl.pallas_call(functools.partial(back_kernel, with_dots), grid_spec=pltpu...]
    ppermute x35 -> x25, starting transfers between devices: 95.6 us -> 26.8 us  [swap(): return lax.ppermute(array, axis, [(i, i ^ bit) for i in range(count)])]
  transfers between devices with their start and end apart: 47 -> 34, of which waited for: 22 -> 19; matrix products, arithmetic and copies ran while one was open for 9% -> 22% of each run, Pallas kernels for 0% -> 15%
where the time goes in v1:
time: 663 us; the launch traced here: 654 us
  waiting for transfers between devices  233 us (35%)
  Pallas kernels  101 us (15%)
  blocking collectives  88.8 us (13%)
  local copies, waits for them, and re-layouts  70.3 us (11%)
  other arithmetic  58 us (9%)
  starting transfers between devices  49.2 us (7%)
  matrix products  38.2 us (6%)
  between operations  15.8 us (2%)
    ppermute x25, waiting for transfers between devices, swap(): return lax.ppermute(array, axis, [(i, i ^ bit) for i in range(count)])  89.8 us
    all_gather x1, waiting for transfers between devices, per_device(): lax.all_gather(jnp.concatenate([normed_mid, side], 1), EVERY, axis=0, til...  66.2 us
    all_to_all x2, blocking collectives, trade(): lax.all_to_all(array, 'dp', split_axis=0, concat_axis=0, tiled=True, axis...  62.7 us
    all_to_all x2, waiting for transfers between devices, trade(): lax.all_to_all(array, 'dp', split_axis=0, concat_axis=0, tiled=True, axis...  58.6 us
    dot_general x14, matrix products, dot(): lax.dot_general(left_side, right_side, (((left_dim,), (right_dim,)), ((),...  29.2 us
    pallas_call x3, Pallas kernels, row_back(): pl.pallas_call(functools.partial(back_kernel, with_dots), grid_spec=pltpu...  28.2 us
    ppermute x25, starting transfers between devices, swap(): return lax.ppermute(array, axis, [(i, i ^ bit) for i in range(count)])  26.8 us
    pallas_call x2, Pallas kernels, over_rows(): pl.pallas_call(over_kernel, grid=(width // block, total // chunk), in_spe...  22 us
  transfers between devices with their start and end apart: 34, of which 19 were waited for; matrix products, arithmetic and copies ran while one was open for 22% of the time, Pallas kernels for 15%

profile of v1, /device:TPU:0, one launch (start us, length us, event | category | flops | bytes accessed | tf_op | source)
XLA Modules:
  0.0 653.7 jit_solution(3349309079325202705)
XLA Ops:
  10.7 2.3 broadcast_multiply_fusion
  16.7 8.4 %psum.21 = f32[2,256]{1,0:T(2,128)S(1)} all-reduce(f32[2,256]{1,0:T(2,128)S(1)} %pad_maximum_fusion.9), channel_id=1, replica_groups=mesh['dp'=8,'tensor'=4] {'tensor'}, use_global_device_ids=true, to_apply=%region_3.0 | all-reduce | flops 512 | bytes 4096 | tf_op jit(solution)/shard_map/psum | solution.py:417
  31.1 3.4 convolution_convert_fusion.5
  46.1 6.1 all-to-all-start
  52.3 50.4 %all-to-all-done = bf16[8,656,128]{2,1,0:T(8,128)(2,1)} async-done(((bf16[8,656,128]{2,1,0:T(8,128)(2,1)}), bf16[8,656,128]{2,1,0:T(8,128)(2,1)}, u32[]{:S(2)}, u32[]{:S(2)}) %all-to-all-start) | async-done | bytes 1343520 | tf_op jit(solution)/shard_map/all_to_all | solution.py:402
  105.9 2.4 fusion.68
  111.6 3.0 exponential_select_fusion
  114.6 2.5 fusion.12
  118.1 5.8 all-to-all-start.1
  124.0 8.2 %all-to-all-done.1 = bf16[8,128,128]{2,1,0:T(8,128)(2,1)S(1)} async-done(((bf16[8,128,128]{2,1,0:T(8,128)(2,1)}), bf16[8,128,128]{2,1,0:T(8,128)(2,1)S(1)}, u32[]{:S(2)}, u32[]{:S(2)}) %all-to-all-start.1) | async-done | bytes 262176 | tf_op jit(solution)/shard_map/all_to_all | solution.py:402
  134.8 2.4 fusion.2
  139.4 2.2 collective-permute-done
  146.0 6.7 %collective-permute-done.1 = bf16[64,2048]{1,0:T(8,128)(2,1)} collective-permute-done((bf16[64,2048]{1,0:T(8,128)(2,1)S(1)}, bf16[64,2048]{1,0:T(8,128)(2,1)}, u32[]{:S(2)}, u32[]{:S(2)}) %collective-permute-start.1) | collective-permute-done | bytes 262176 | tf_op jit(solution)/shard_map/ppermute | solution.py:60
  158.0 8.4 %shard_map.263 = (bf16[1024,2048]{1,0:T(8,128)(2,1)}, bf16[2048,512]{1,0:T(8,128)(2,1)}) custom-call(bf16[2,2048,256]{2,1,0:T(8,128)(2,1)} %gate_ref.3, bf16[2,2048,256]{2,1,0:T(8,128)(2,1)} %up_ref.3, bf16[2,256,2048]{2,1,0:T(8,128)(2,1)} %down_ref.3), custom_call_target="tpu_custom_call" | custom-call | bytes 12582912 | tf_op jit(solution)/shard_map/pallas_call | solution.py:109
  167.0 66.2 %all-gather.4.cloned.1.call-done.rows_ref.left_ref = bf16[2048,2176]{1,0:T(8,128)(2,1)} async-done(((bf16[64,2176]{1,0:T(8,128)(2,1)}), bf16[2048,2176]{1,0:T(8,128)(2,1)}) %all-gather.4.cloned.1.call-update) | async-done | bytes 8912912 | tf_op jit(solution)/shard_map/all_gather | solution.py:502
  233.1 21.3 %shard_map.264 = (bf16[2048,1024]{1,0:T(8,128)(2,1)}, bf16[2048,128]{1,0:T(8,128)(2,1)}, bf16[2048,512]{1,0:T(8,128)(2,1)}, bf16[512,2048]{1,0:T(8,128)(2,1)}, b...) custom-call(s32[1]{0:T(128)} %bitcast.27.first_ref, ...), custom_call_target="tpu_custom_call" | custom-call | flops 12884901888 | bytes 26738688 | tf_op jit(solution)/shard_map/pallas_call | solution.py:177
  254.5 8.8 %shard_map.268 = (bf16[8,2,64,640]{3,2,1,0:T(8,128)(2,1)}, bf16[8,2,64,640]{3,2,1,0:T(8,128)(2,1)}) custom-call(s32[2]{0:T(128)} %pad_add_fusion.index_ref, bf16[2048,1024]{1,0:T(8,128)(2,1)} %get-tuple-element.42.low_ref, bf16[1024,2048]{1,0:T(8,128)(2,1)} %get-tuple-element.43.both_ref, bf16[2048,128]{1,0:T(8,128)(2,1)} %get-tuple-element.44.dots_ref), custom_call_target="tpu_custom_call" | custom-call | flops 2147483648 | bytes 6291456 | tf_op jit(solution)/shard_map/pallas_call | solution.py:235
  263.5 9.6 %shard_map.267 = (bf16[8,2,64,768]{3,2,1,0:T(8,128)(2,1)}, bf16[8,2,64,768]{3,2,1,0:T(8,128)(2,1)}) custom-call(s32[2]{0:T(128)} %pad_add_fusion.index_ref, bf16[2048,1024]{1,0:T(8,128)(2,1)} %get-tuple-element.42.low_ref, bf16[1024,2048]{1,0:T(8,128)(2,1)} %get-tuple-element.43.both_ref, bf16[2048,128]{1,0:T(8,128)(2,1)} %get-tuple-element.44.dots_ref), custom_call_target="tpu_custom_call" | custom-call | flops 3221225472 | bytes 7340032 | tf_op jit(solution)/shard_map/pallas_call | solution.py:235
  273.4 9.8 %shard_map.266 = (bf16[8,2,64,768]{3,2,1,0:T(8,128)(2,1)}, bf16[8,2,64,768]{3,2,1,0:T(8,128)(2,1)}) custom-call(s32[2]{0:T(128)} %pad_add_fusion.index_ref, bf16[2048,1024]{1,0:T(8,128)(2,1)} %get-tuple-element.42.low_ref, bf16[1024,2048]{1,0:T(8,128)(2,1)} %get-tuple-element.43.both_ref, bf16[2048,128]{1,0:T(8,128)(2,1)} %get-tuple-element.44.dots_ref), custom_call_target="tpu_custom_call" | custom-call | flops 3221225472 | bytes 7340032 | tf_op jit(solution)/shard_map/pallas_call | solution.py:235
  287.9 29.6 %collective-permute-done.15 = bf16[2,2,2,64,640]{4,3,0,1,2:T(8,128)(2,1)S(1)} collective-permute-done((bf16[2,2,2,64,640]{4,3,0,1,2:T(8,128)(2,1)S(1)}, bf16[2,2,2,64,640]{4,3,0,1,2:T(8,128)(2,1)S(1)}, u32[]{:S(2)}, u32[]{:S(2)}) %collective-permute-start.15) | collective-permute-done | bytes 655392 | tf_op jit(solution)/shard_map/ppermute | solution.py:60
  320.6 7.8 %collective-permute-done.16 = bf16[2,2,64,640]{3,2,0,1:T(8,128)(2,1)S(1)} collective-permute-done((bf16[2,2,64,640]{3,2,0,1:T(8,128)(2,1)S(1)}, bf16[2,2,64,640]{3,2,0,1:T(8,128)(2,1)S(1)}, u32[]{:S(2)}, u32[]{:S(2)}) %collective-permute-start.16) | collective-permute-done | bytes 327712 | tf_op jit(solution)/shard_map/ppermute | solution.py:60
  328.6 4.3 collective-permute-start.17
  333.2 10.7 %collective-permute-done.5 = bf16[2,2,2,64,768]{4,3,0,1,2:T(8,128)(2,1)S(1)} collective-permute-done((bf16[2,2,2,64,768]{4,3,0,1,2:T(8,128)(2,1)S(1)}, bf16[2,2,2,64,768]{4,3,0,1,2:T(8,128)(2,1)S(1)}, u32[]{:S(2)}, u32[]{:S(2)}) %collective-permute-start.5) | collective-permute-done | bytes 786464 | tf_op jit(solution)/shard_map/ppermute | solution.py:60
  344.4 4.9 collective-permute-start.6
  352.1 5.4 collective-permute-done.6
  360.5 3.5 collective-permute-done.7
  364.1 3.3 collective-permute-start.8
  368.5 2.5 collective-permute-done.8
  374.4 5.9 collective-permute-done.19
  388.1 10.1 %shard_map.265 = bf16[2048,2048]{1,0:T(8,128)(2,1)} custom-call(bf16[2048,512]{1,0:T(8,128)(2,1)} %get-tuple-element.41.hid_ref, bf16[2,256,2048]{2,1,0:T(8,128)(2,1)} %down_ref.3), custom_call_target="tpu_custom_call" | custom-call | flops 4294967296 | bytes 12582912 | tf_op jit(solution)/shard_map/pallas_call | solution.py:287
  398.2 3.4 convolution_convert_fusion.4
  402.7 19.2 %all_to_all.30 = bf16[8,128,128]{2,1,0:T(8,128)(2,1)S(1)} all-to-all(bf16[8,128,128]{2,1,0:T(8,128)(2,1)S(1)} %bitcast.374), channel_id=1, replica_groups={{0,4,8,12,16,20,24,28},{1,5,9,13,17,21,25,29},{2,6,10,14,18,22,26,30},{..., dimensions={0} | all-to-all | bytes 524288 | tf_op jit(solution)/shard_map/all_to_all | solution.py:402
  421.9 5.0 multiply_reduce_fusion
  427.0 6.0 multiply_convert_fusion
  437.1 43.5 %all_to_all.31 = bf16[8,640,128]{2,1,0:T(8,128)(2,1)S(1)} all-to-all(bf16[8,640,128]{2,1,0:T(8,128)(2,1)S(1)} %pad_maximum_fusion.1), channel_id=1, replica_groups={{0,4,8,12,16,20,24,28},{1,5,9,13,17,21,25,29},{2,6,10,14,18,22,26,30},{..., dimensions={0} | all-to-all | bytes 2621440 | tf_op jit(solution)/shard_map/all_to_all | solution.py:402
  489.7 6.7 %psum.22 = f32[2,256]{1,0:T(2,128)} all-reduce(f32[2,256]{1,0:T(2,128)} %pad_maximum_fusion.10), channel_id=1, replica_groups=mesh['dp'=8,'tensor'=4] {'tensor'}, use_global_device_ids=true, to_apply=%region_17.18 | all-reduce | flops 512 | bytes 4096 | tf_op jit(solution)/shard_map/psum | solution.py:579
  505.2 12.4 %copy.234 = bf16[2048,2048]{1,0:T(8,128)(2,1)} copy(bf16[2048,2048]{0,1:T(8,128)(2,1)} %bitcast.331) | data formatting | bytes 16777216 | tf_op jit(solution)/shard_map/dot_general | solution.py:46
  520.6 5.1 all-to-all-start.4
  530.3 11.8 %collective-permute-done.22 = bf16[64,2048]{1,0:T(8,128)(2,1)S(1)} collective-permute-done((bf16[64,2048]{1,0:T(8,128)(2,1)S(1)}, bf16[64,2048]{1,0:T(8,128)(2,1)S(1)}, u32[]{:S(2)}, u32[]{:S(2)}) %collective-permute-start.22) | collective-permute-done | bytes 262176 | tf_op jit(solution)/shard_map/ppermute | solution.py:60
  543.7 7.0 %all-to-all-done.4 = bf16[8,192,256]{2,1,0:T(8,128)(2,1)} async-done(((bf16[8,192,256]{2,1,0:T(8,128)(2,1)}), bf16[8,192,256]{2,1,0:T(8,128)(2,1)}, u32[]{:S(2)}, u32[]{:S(2)}) %all-to-all-start.4) | async-done | bytes 786464 | tf_op jit(solution)/shard_map/all_to_all | solution.py:592
  553.5 6.6 %fusion.11 = bf16[8,192,256]{2,1,0:T(8,128)(2,1)S(1)} fusion(bf16[192,2048,1]{1,0,2:T(8,128)(2,1)} %reshape.659, bf16[8,256,2048]{2,1,0:T(8,128)(2,1)} %bitcast.332), kind=kOutput, calls=%fused_computation.36 | convolution fusion | flops 1611005952 | bytes 9961472 | tf_op jit(solution)/shard_map/dot_general | solution.py:46
  561.2 4.9 all-to-all-start.5
  566.2 11.0 %shard_map.269 = f32[2,2048,256]{2,1,0:T(8,128)} custom-call(bf16[2048,2176]{1,0:T(8,128)(2,1)} %all-gather.4.cloned.1.call-done.rows_ref.left_ref, bf16[2048,512]{1,0:T(8,128)(2,1)} %get-tuple-element.51.right_ref), custom_call_target="tpu_custom_call" | custom-call | flops 4294967296 | bytes 16777216 | tf_op jit(solution)/shard_map/pallas_call | solution.py:320
  577.2 11.0 %shard_map.270 = f32[2,2048,256]{2,1,0:T(8,128)} custom-call(bf16[2048,2176]{1,0:T(8,128)(2,1)} %all-gather.4.cloned.1.call-done.rows_ref.left_ref, bf16[2048,512]{1,0:T(8,128)(2,1)} %get-tuple-element.52.right_ref), custom_call_target="tpu_custom_call" | custom-call | flops 4294967296 | bytes 16777216 | tf_op jit(solution)/shard_map/pallas_call | solution.py:320
  588.1 10.9 %shard_map.271 = f32[512,2048]{1,0:T(8,128)} custom-call(bf16[512,2048]{1,0:T(8,128)(2,1)} %get-tuple-element.53.left_ref, bf16[2048,2048]{1,0:T(8,128)(2,1)} %all-gather.6.cloned.1.call-done.grad_ref.right_ref), custom_call_target="tpu_custom_call" | custom-call | flops 4294967296 | bytes 16777216 | tf_op jit(solution)/shard_map/pallas_call | solution.py:350
  603.7 11.1 %psum.23 = f32[18,256]{1,0:T(8,128)S(1)} all-reduce(f32[18,256]{1,0:T(8,128)S(1)} %copy-done.59), channel_id=1, replica_groups=mesh['dp'=8,'tensor'=4] {'tensor'}, use_global_device_ids=true, to_apply=%region_25.26 | all-reduce | flops 4608 | bytes 36864 | tf_op jit(solution)/shard_map/psum | solution.py:626
  615.4 2.5 fusion.58
  617.9 11.0 %reduce-scatter.3.cloned.1.call-done = bf16[64,2048]{1,0:T(8,128)(2,1)} async-done(((bf16[2048,2048]{1,0:T(8,128)(2,1)}), bf16[64,2048]{1,0:T(8,128)(2,1)}) %reduce-scatter.3.cloned.1.call-update) | async-done | bytes 262160 | tf_op jit(solution)/shard_map/reduce_scatter | solution.py:521
  (420 shorter events, 133.0 us)
Async XLA Ops:
  7.2 159.8 %all-gather.6.cloned.1.call-start = ((), (), s32[]{:S(2)}) async-start(), calls=%async_computation.9 | async-start | bytes 8650752 | tf_op jit(solution)/shard_map/all_gather | solution.py:406
  46.1 56.6 %all-to-all-start = ((bf16[8,656,128]{2,1,0:T(8,128)(2,1)}), bf16[8,656,128]{2,1,0:T(8,128)(2,1)}, u32[]{:S(2)}, u32[]{:S(2)}) async-start(bf16[8,656,128]{2,1,0:T(8,128)(2,1)} %bitcast.339), calls=%async_computation | async-start | bytes 2686976 | tf_op jit(solution)/shard_map/all_to_all | solution.py:402
  52.3 57.4 %copy-start.64 = (s32[1024]{0:T(1024)}, s32[1024]{0:T(1024)S(1)}, u32[]{:S(2)}) copy-start(s32[1024]{0:T(1024)S(1)} %add_bitcast_fusion) | copy-start | bytes 12292
  118.1 14.1 %all-to-all-start.1 = ((bf16[8,128,128]{2,1,0:T(8,128)(2,1)}), bf16[8,128,128]{2,1,0:T(8,128)(2,1)S(1)}, u32[]{:S(2)}, u32[]{:S(2)}) async-start(bf16[8,128,128]{2,1,0:T(8,128)(2,1)} %bitcast.18), calls=%async_computation.1 | async-start | bytes 524288 | tf_op jit(solution)/shard_map/all_to_all | solution.py:402
  123.9 109.2 %all-gather.4.cloned.1.call-start = ((), (), s32[]{:S(2)}) async-start(), calls=%async_computation.8 | async-start | bytes 9191424 | tf_op jit(solution)/shard_map/all_gather | solution.py:502
  139.4 2.3 collective-permute-start
  144.2 8.5 %collective-permute-start.1 = (bf16[64,2048]{1,0:T(8,128)(2,1)S(1)}, bf16[64,2048]{1,0:T(8,128)(2,1)}, u32[]{:S(2)}, u32[]{:S(2)}) collective-permute-start(bf16[64,2048]{1,0:T(8,128)(2,1)S(1)} %fusion.38), channel_id=1, source_target_pairs={{0,2},{1,3},{2,0},{3,1},{4,6},{5,7},{6,4},{7,5},{8,10},{9,11},{10,... | collective-permute-start | bytes 786440 | tf_op jit(solution)/shard_map/ppermute | solution.py:60
  154.7 195.8 %copy-start.81 = (f32[64]{0:T(128)}, f32[64]{0:T(128)S(1)}, u32[]{:S(2)}) copy-start(f32[64]{0:T(128)S(1)} %get-tuple-element.187) | copy-start | bytes 772
  155.0 195.6 %copy-start.82 = (f32[64]{0:T(128)}, f32[64]{0:T(128)S(1)}, u32[]{:S(2)}) copy-start(f32[64]{0:T(128)S(1)} %fusion.49) | copy-start | bytes 772
  156.0 349.3 %all-gather.8.cloned.1.call-start = ((), (), s32[]{:S(2)}) async-start(), calls=%async_computation.11 | async-start | bytes 8650752 | tf_op jit(solution)/shard_map/all_gather | solution.py:413
  157.7 441.3 %reduce-scatter.5.cloned.1.call-start = ((), (), s32[]{:S(2)}) async-start(), calls=%async_computation.12 | async-start | bytes 2359296 | tf_op jit(solution)/shard_map/reduce_scatter | solution.py:542
  263.3 20.2 %collective-permute-start.14 = (bf16[8,2,64,640]{3,2,1,0:T(8,128)(2,1)}, bf16[8,2,64,640]{3,2,1,0:T(8,128)(2,1)S(1)}, u32[]{:S(2)}, u32[]{:S(2)}) collective-permute-start(bf16[8,2,64,640]{3,2,1,0:T(8,128)(2,1)} %get-tuple-element.50), channel_id=1, source_target_pairs={{0,1},{1,0},{2,3},{3,2},{4,5},{5,4},{6,7},{7,6},{8,9},{9,8},{10,11... | collective-permute-start | bytes 3932168 | tf_op jit(solution)/shard_map/ppermute | solution.py:60
  273.2 12.6 %collective-permute-start.9 = (bf16[8,2,64,768]{3,2,1,0:T(8,128)(2,1)}, bf16[8,2,64,768]{3,2,1,0:T(8,128)(2,1)S(1)}, u32[]{:S(2)}, u32[]{:S(2)}) collective-permute-start(bf16[8,2,64,768]{3,2,1,0:T(8,128)(2,1)} %get-tuple-element.48), channel_id=1, source_target_pairs={{0,1},{1,0},{2,3},{3,2},{4,5},{5,4},{6,7},{7,6},{8,9},{9,8},{10,11... | collective-permute-start | bytes 4718600 | tf_op jit(solution)/shard_map/ppermute | solution.py:60
  283.2 35.1 %collective-permute-start.4 = (bf16[8,2,64,768]{3,2,1,0:T(8,128)(2,1)}, bf16[8,2,64,768]{3,2,1,0:T(8,128)(2,1)S(1)}, u32[]{:S(2)}, u32[]{:S(2)}) collective-permute-start(bf16[8,2,64,768]{3,2,1,0:T(8,128)(2,1)} %get-tuple-element.46), channel_id=1, source_target_pairs={{0,1},{1,0},{2,3},{3,2},{4,5},{5,4},{6,7},{7,6},{8,9},{9,8},{10,11... | collective-permute-start | bytes 4718600 | tf_op jit(solution)/shard_map/ppermute | solution.py:60
  284.1 33.5 %collective-permute-start.15 = (bf16[2,2,2,64,640]{4,3,0,1,2:T(8,128)(2,1)S(1)}, bf16[2,2,2,64,640]{4,3,0,1,2:T(8,128)(2,1)S(1)}, u32[]{:S(2)}, u32[]{:S(2)}) collective-permute-start(bf16[2,2,2,64,640]{4,3,0,1,2:T(8,128)(2,1)S(1)} %bitcast.386), channel_id=1, source_target_pairs={{0,8},{4,12},{8,0},{12,4},{16,24},{20,28},{24,16},{28,20},{1,9},{5... | collective-permute-start | bytes 1966088 | tf_op jit(solution)/shard_map/ppermute | solution.py:60
  286.3 32.1 %copy-start.38 = (bf16[8,2,64,768]{3,2,1,0:T(8,128)(2,1)S(1)}, bf16[8,2,64,768]{3,2,1,0:T(8,128)(2,1)}, u32[]{:S(2)}) copy-start(bf16[8,2,64,768]{3,2,1,0:T(8,128)(2,1)} %get-tuple-element.45) | copy-start | bytes 4718596
  286.4 46.5 %collective-permute-start.10 = (bf16[2,2,2,64,768]{4,3,0,2,1:T(8,128)(2,1)S(1)}, bf16[2,2,2,64,768]{4,3,0,2,1:T(8,128)(2,1)S(1)}, u32[]{:S(2)}, u32[]{:S(2)}) collective-permute-start(bf16[2,2,2,64,768]{4,3,0,2,1:T(8,128)(2,1)S(1)} %bitcast.384), channel_id=1, source_target_pairs={{0,4},{4,0},{8,12},{12,8},{16,20},{20,16},{24,28},{28,24},{1,5},{5... | collective-permute-start | bytes 2359304 | tf_op jit(solution)/shard_map/ppermute | solution.py:60
  317.8 10.7 %collective-permute-start.16 = (bf16[2,2,64,640]{3,2,0,1:T(8,128)(2,1)S(1)}, bf16[2,2,64,640]{3,2,0,1:T(8,128)(2,1)S(1)}, u32[]{:S(2)}, u32[]{:S(2)}) collective-permute-start(bf16[2,2,64,640]{3,2,0,1:T(8,128)(2,1)S(1)} %slice_bitcast_fusion.4), channel_id=1, source_target_pairs={{0,2},{1,3},{2,0},{3,1},{4,6},{5,7},{6,4},{7,5},{8,10},{9,11},{10,... | collective-permute-start | bytes 983048 | tf_op jit(solution)/shard_map/ppermute | solution.py:60
  319.1 24.9 %collective-permute-start.5 = (bf16[2,2,2,64,768]{4,3,0,1,2:T(8,128)(2,1)S(1)}, bf16[2,2,2,64,768]{4,3,0,1,2:T(8,128)(2,1)S(1)}, u32[]{:S(2)}, u32[]{:S(2)}) collective-permute-start(bf16[2,2,2,64,768]{4,3,0,1,2:T(8,128)(2,1)S(1)} %bitcast.385), channel_id=1, source_target_pairs={{0,2},{1,3},{2,0},{3,1},{4,6},{5,7},{6,4},{7,5},{8,10},{9,11},{10,... | collective-permute-start | bytes 2359304 | tf_op jit(solution)/shard_map/ppermute | solution.py:60
  328.6 15.6 %collective-permute-start.17 = (bf16[2,64,640]{2,1,0:T(8,128)(2,1)S(1)}, bf16[2,64,640]{2,1,0:T(8,128)(2,1)S(1)}, u32[]{:S(2)}, u32[]{:S(2)}) collective-permute-start(bf16[2,64,640]{2,1,0:T(8,128)(2,1)S(1)} %slice_bitcast_fusion.10), channel_id=1, source_target_pairs={{0,4},{4,0},{8,12},{12,8},{16,20},{20,16},{24,28},{28,24},{1,5},{5... | collective-permute-start | bytes 491528 | tf_op jit(solution)/shard_map/ppermute | solution.py:60
  333.1 17.4 %copy-start.46 = (f32[64,16]{1,0:T(8,128)S(1)}, f32[64,16]{1,0:T(8,128)}, u32[]{:S(2)}) copy-start(f32[64,16]{1,0:T(8,128)} %copy-done.45) | copy-start | bytes 12292
  333.1 18.4 %collective-permute-start.11 = (bf16[2,2,64,768]{3,2,0,1:T(8,128)(2,1)S(1)}, bf16[2,2,64,768]{3,2,0,1:T(8,128)(2,1)S(1)}, u32[]{:S(2)}, u32[]{:S(2)}) collective-permute-start(bf16[2,2,64,768]{3,2,0,1:T(8,128)(2,1)S(1)} %slice_bitcast_fusion), channel_id=1, source_target_pairs={{0,8},{4,12},{8,0},{12,4},{16,24},{20,28},{24,16},{28,20},{1,9},{5... | collective-permute-start | bytes 1179656 | tf_op jit(solution)/shard_map/ppermute | solution.py:60
  344.2 6.3 collective-permute-start.18
  344.4 13.2 %collective-permute-start.6 = (bf16[2,2,64,768]{3,2,0,1:T(8,128)(2,1)S(1)}, bf16[2,2,64,768]{3,2,0,1:T(8,128)(2,1)S(1)}, u32[]{:S(2)}, u32[]{:S(2)}) collective-permute-start(bf16[2,2,64,768]{3,2,0,1:T(8,128)(2,1)S(1)} %slice_bitcast_fusion.2), channel_id=1, source_target_pairs={{0,4},{4,0},{8,12},{12,8},{16,20},{20,16},{24,28},{28,24},{1,5},{5... | collective-permute-start | bytes 1179656 | tf_op jit(solution)/shard_map/ppermute | solution.py:60
  351.6 19.4 %copy-start.54 = (bf16[2048,16]{0,1:T(8,128)(2,1)S(1)}, bf16[2048,16]{0,1:T(8,128)(2,1)}, u32[]{:S(2)}) copy-start(bf16[2048,16]{0,1:T(8,128)(2,1)} %param.29) | copy-start | bytes 196612
  351.7 19.4 %copy-start.56 = (f32[2048]{0:T(1024)S(1)}, f32[2048]{0:T(1024)}, u32[]{:S(2)}) copy-start(f32[2048]{0:T(1024)} %param.28) | copy-start | bytes 24580
  351.7 19.4 %copy-start.84 = (f32[64]{0:T(128)S(1)}, f32[64]{0:T(128)}, u32[]{:S(2)}) copy-start(f32[64]{0:T(128)} %copy-done.83) | copy-start | bytes 772
  351.7 8.0 %collective-permute-start.12 = (bf16[2,64,768]{2,1,0:T(8,128)(2,1)S(1)}, bf16[2,64,768]{2,1,0:T(8,128)(2,1)S(1)}, u32[]{:S(2)}, u32[]{:S(2)}) collective-permute-start(bf16[2,64,768]{2,1,0:T(8,128)(2,1)S(1)} %slice_bitcast_fusion.6), channel_id=1, source_target_pairs={{0,2},{1,3},{2,0},{3,1},{4,6},{5,7},{6,4},{7,5},{8,10},{9,11},{10,... | collective-permute-start | bytes 589832 | tf_op jit(solution)/shard_map/ppermute | solution.py:60
  357.7 6.3 collective-permute-start.7
  359.8 8.7 %collective-permute-start.13 = (bf16[64,768]{1,0:T(8,128)(2,1)S(1)}, bf16[64,768]{1,0:T(8,128)(2,1)S(1)}, u32[]{:S(2)}, u32[]{:S(2)}) collective-permute-start(bf16[64,768]{1,0:T(8,128)(2,1)S(1)} %slice_bitcast_fusion.12), channel_id=1, source_target_pairs={{0,16},{4,20},{8,24},{12,28},{16,0},{20,4},{24,8},{28,12},{1,17},{... | collective-permute-start | bytes 294920 | tf_op jit(solution)/shard_map/ppermute | solution.py:60
  364.1 7.0 %collective-permute-start.8 = (bf16[64,768]{1,0:T(8,128)(2,1)S(1)}, bf16[64,768]{1,0:T(8,128)(2,1)S(1)}, u32[]{:S(2)}, u32[]{:S(2)}) collective-permute-start(bf16[64,768]{1,0:T(8,128)(2,1)S(1)} %slice_bitcast_fusion.14), channel_id=1, source_target_pairs={{0,16},{4,20},{8,24},{12,28},{16,0},{20,4},{24,8},{28,12},{1,17},{... | collective-permute-start | bytes 294920 | tf_op jit(solution)/shard_map/ppermute | solution.py:60
  373.9 6.4 collective-permute-start.19
  381.2 2.3 collective-permute-start.20
  388.1 240.8 %reduce-scatter.3.cloned.1.call-start = ((), (), s32[]{:S(2)}) async-start(), calls=%async_computation.10 | async-start | bytes 8650752 | tf_op jit(solution)/shard_map/reduce_scatter | solution.py:521
  398.2 23.7 %copy-start.12 = (bf16[8,256,128]{2,1,0:T(8,128)(2,1)S(1)}, bf16[8,256,128]{2,1,0:T(8,128)(2,1)}, u32[]{:S(2)}) copy-start(bf16[8,256,128]{2,1,0:T(8,128)(2,1)} %copy-done.11) | copy-start | bytes 1572868
  505.2 20.5 %collective-permute-start.21 = (bf16[2,64,2048]{2,1,0:T(8,128)(2,1)}, bf16[2,64,2048]{2,1,0:T(8,128)(2,1)}, u32[]{:S(2)}, u32[]{:S(2)}) collective-permute-start(bf16[2,64,2048]{2,1,0:T(8,128)(2,1)} %fusion.26), channel_id=1, source_target_pairs={{0,1},{1,0},{2,3},{3,2},{4,5},{5,4},{6,7},{7,6},{8,9},{9,8},{10,11... | collective-permute-start | bytes 1572872 | tf_op jit(solution)/shard_map/ppermute | solution.py:60
  520.6 30.1 %all-to-all-start.4 = ((bf16[8,192,256]{2,1,0:T(8,128)(2,1)}), bf16[8,192,256]{2,1,0:T(8,128)(2,1)}, u32[]{:S(2)}, u32[]{:S(2)}) async-start(bf16[8,192,256]{2,1,0:T(8,128)(2,1)} %bitcast.348), calls=%async_computation.5 | async-start | bytes 1572864 | tf_op jit(solution)/shard_map/all_to_all | solution.py:592
  528.2 13.9 %collective-permute-start.22 = (bf16[64,2048]{1,0:T(8,128)(2,1)S(1)}, bf16[64,2048]{1,0:T(8,128)(2,1)S(1)}, u32[]{:S(2)}, u32[]{:S(2)}) collective-permute-start(bf16[64,2048]{1,0:T(8,128)(2,1)S(1)} %fusion.39), channel_id=1, source_target_pairs={{0,2},{1,3},{2,0},{3,1},{4,6},{5,7},{6,4},{7,5},{8,10},{9,11},{10,... | collective-permute-start | bytes 786440 | tf_op jit(solution)/shard_map/ppermute | solution.py:60
  561.2 39.6 %all-to-all-start.5 = ((bf16[8,224,256]{2,1,0:T(8,128)(2,1)}), bf16[8,224,256]{2,1,0:T(8,128)(2,1)S(1)}, u32[]{:S(2)}, u32[]{:S(2)}) async-start(bf16[8,224,256]{2,1,0:T(8,128)(2,1)} %fusion.17), calls=%async_computation.6 | async-start | bytes 1835008 | tf_op jit(solution)/shard_map/all_to_all | solution.py:620
  603.7 25.2 %copy-start.14 = (f32[64,2048]{1,0:T(8,128)S(1)}, f32[64,2048]{1,0:T(8,128)}, u32[]{:S(2)}) copy-start(f32[64,2048]{1,0:T(8,128)} %copy-done.13) | copy-start | bytes 1572868
  603.7 25.2 %copy-start.57 = (f32[2048]{0:T(1024)S(1)}, f32[2048]{0:T(1024)}, u32[]{:S(2)}) copy-start(f32[2048]{0:T(1024)} %param.28) | copy-start | bytes 24580
  603.7 25.2 %copy-start.61 = (f32[2048]{0:T(1024)S(1)}, f32[2048]{0:T(1024)}, u32[]{:S(2)}) copy-start(f32[2048]{0:T(1024)} %param.21) | copy-start | bytes 24580
  603.7 25.2 %copy-start.85 = (f32[64]{0:T(128)S(1)}, f32[64]{0:T(128)}, u32[]{:S(2)}) copy-start(f32[64]{0:T(128)} %copy-done.83) | copy-start | bytes 772
  603.7 25.2 %copy-start.92 = (f32[64]{0:T(128)S(1)}, f32[64]{0:T(128)}, u32[]{:S(2)}) copy-start(f32[64]{0:T(128)} %copy-done.91) | copy-start | bytes 772
  631.1 9.8 %collective-permute-start.2 = (bf16[64,2048]{1,0:T(8,128)(2,1)}, bf16[64,2048]{1,0:T(8,128)(2,1)S(1)}, u32[]{:S(2)}, u32[]{:S(2)}) collective-permute-start(bf16[64,2048]{1,0:T(8,128)(2,1)} %get-tuple-element.156), channel_id=1, source_target_pairs={{0,2},{1,3},{2,0},{3,1},{4,6},{5,7},{6,4},{7,5},{8,10},{9,11},{10,... | collective-permute-start | bytes 786440 | tf_op jit(solution)/shard_map/ppermute | solution.py:60
  631.7 10.4 %collective-permute-start.23 = (bf16[64,2048]{1,0:T(8,128)(2,1)S(1)}, bf16[64,2048]{1,0:T(8,128)(2,1)S(1)}, u32[]{:S(2)}, u32[]{:S(2)}) collective-permute-start(bf16[64,2048]{1,0:T(8,128)(2,1)S(1)} %get-tuple-element.155), channel_id=1, source_target_pairs={{0,2},{1,3},{2,0},{3,1},{4,6},{5,7},{6,4},{7,5},{8,10},{9,11},{10,... | collective-permute-start | bytes 786440 | tf_op jit(solution)/shard_map/ppermute | solution.py:60
  642.0 2.0 collective-permute-start.3
  642.2 3.0 collective-permute-start.24
  (82 other events, 354.6 us)
Sparse Core Ops, SparseCore 0:
  10.9 99.8 all-gather.5
  156.1 77.0 all-gather.3
  236.0 87.1 all-gather.7
  388.2 83.3 reduce-scatter.4
  473.8 155.0 reduce-scatter.2

commit v2 on v1

v2 whole, which is shorter than its diff:
```python
import functools
import math

import jax
import jax.numpy as jnp
from jax import lax
from jax.experimental import pallas as pl
from jax.experimental.pallas import tpu as pltpu
from jax.sharding import PartitionSpec as P

SPAN = 8


EPSILON = 1e-05
ROPE_BASE = 10000.0
NEGATIVE = -1e30
BF = jnp.bfloat16
F32 = jnp.float32
EVERY = ("dp", "tensor")
VMEM_LIMIT = 56 * 1024 * 1024
LANES = 128


def rope_tables(positions, head_size):
    frequency = ROPE_BASE ** (-jnp.arange(0, head_size, 2, dtype=jnp.float32) / head_size)
    angles = positions[:, None] * frequency[None, :]
    cosine, sine = jnp.cos(angles), jnp.sin(angles)
    return jnp.concatenate([cosine, cosine], -1), jnp.concatenate([-sine, sine], -1)


def dot(left_side, right_side, left_dim, right_dim):
    return lax.dot_general(
        left_side,
        right_side,
        (((left_dim,), (right_dim,)), ((), ())),
        preferred_element_type=jnp.float32,
    )


def swap(array, axis, bit):
    count = lax.axis_size(axis)
    return lax.ppermute(array, axis, [(i, i ^ bit) for i in range(count)])


def resident(shape):
    return pl.BlockSpec(shape, lambda *_: (0,) * len(shape), pipeline_mode=pl.Buffered(1))


def cost(macs, size, transcendentals=0):
    return pl.CostEstimate(flops=2 * macs, bytes_accessed=size, transcendentals=transcendentals)


PARAMS = pltpu.CompilerParams(vmem_limit_bytes=VMEM_LIMIT)


def turn_kernel(gate_ref, up_ref, down_ref, both_ref, down_out_ref):
    count, _, hidden = gate_ref.shape
    for e in range(count):
        both_ref[pl.ds(e * hidden, hidden), :] = gate_ref[e].T
        both_ref[pl.ds((count + e) * hidden, hidden), :] = up_ref[e].T
        down_out_ref[:, pl.ds(e * hidden, hidden)] = down_ref[e].T


def turn_weights(w_gate, w_up, w_down, block=256):
    count, width, hidden = w_gate.shape
    mid = count * hidden
    rows = pl.BlockSpec((count, block, hidden), lambda d: (0, d, 0))
    return pl.pallas_call(
        turn_kernel,
        grid=(width // block,),
        in_specs=[rows, rows, pl.BlockSpec((count, hidden, block), lambda d: (0, 0, d))],
        out_specs=[
            pl.BlockSpec((2 * mid, block), lambda d: (0, d)),
            pl.BlockSpec((block, mid), lambda d: (d, 0)),
        ],
        out_shape=[
            jax.ShapeDtypeStruct((2 * mid, width), BF),
            jax.ShapeDtypeStruct((width, mid), BF),
        ],
        compiler_params=PARAMS,
        cost_estimate=cost(0, 12 * mid * width),
    )(w_gate, w_up, w_down)


def hidden_back_kernel(grad_ref, down_ref, out_ref):
    out_ref[...] = dot(grad_ref[...], down_ref[...], 1, 0)


def hidden_back(grad_all, down_turned, block=256):
    width, mid = down_turned.shape
    total = grad_all.shape[0]
    return pl.pallas_call(
        hidden_back_kernel,
        grid=(total // block,),
        in_specs=[pl.BlockSpec((block, width), lambda i: (i, 0)), resident(down_turned.shape)],
        out_specs=pl.BlockSpec((block, mid), lambda i: (i, 0)),
        out_shape=jax.ShapeDtypeStruct((total, mid), F32),
        compiler_params=PARAMS,
        cost_estimate=cost(total * width * mid, total * width * 3),
    )(grad_all, down_turned)


def expert_kernel(experts, axes, index_ref, *refs):
    pieces, refs = (refs[:3], refs[3:6]), refs[6:]
    back_ref, gate_ref, up_ref, both_ref, rows_ref = refs[:5]
    hid_ref, hid_turned_ref, glow_ref, ulow_ref = refs[5:9]
    kept_refs, sent_refs, low_ref, side_ref = refs[9:12], refs[12:15], refs[15], refs[16]
    count, width, hidden_size = gate_ref.shape
    mid = count * hidden_size
    own = kept_refs[0].shape[2]
    starts = [pl.multiple_of((r ^ index_ref[1]) * own, own) for r in range(4)]
    for r in range(4):
        begin = 0
        for piece, axis in zip(pieces[r % 2], axes):
            place = [0] * (len(piece.shape) - 2)
            place[axis] = r // 2
            columns = piece.shape[-1]
            end = min(begin + columns, width)
            value = piece[tuple(place)]
            rows_ref[pl.ds(starts[r], own), begin:end] = value[:, : end - begin]
            if end - begin < columns:
                side_ref[pl.ds(starts[r], own), :] = value[:, end - begin :]
            begin = end
    rows = rows_ref[...]
    side = side_ref[...].astype(F32)
    lane = lax.broadcasted_iota(jnp.int32, side.shape, 1)
    dots = jnp.zeros(side.shape, F32)
    for e in range(count):
        column = index_ref[0] * count + e
        gate = jnp.sum(
            jnp.where((lane == column) | (lane == experts + column), side, 0.0), -1, keepdims=True
        )
        span = pl.ds(e * hidden_size, hidden_size)
        gate_pre = dot(rows, gate_ref[e], 1, 0)
        up_pre = dot(rows, up_ref[e], 1, 0)
        out_back = back_ref[:, span]
        sigma = 1.0 / (1.0 + jnp.exp(-gate_pre))
        silu = gate_pre * sigma
        hidden = silu * up_pre
        inner = jnp.sum(hidden * out_back, -1, keepdims=True)
        high = inner.astype(BF).astype(F32)
        dots = jnp.where(lane == column, high, dots)
        dots = jnp.where(lane == experts + column, inner - high, dots)
        hidden_low = (gate * hidden).astype(BF)
        hidden_grad = gate * out_back
        glow = (hidden_grad * up_pre * sigma * (1.0 + gate_pre * (1.0 - sigma))).astype(BF)
        ulow = (hidden_grad * silu).astype(BF)
        hid_ref[:, span] = hidden_low
        hid_turned_ref[span, :] = hidden_low.T
        glow_ref[:, span] = glow
        ulow_ref[:, span] = ulow
        low_ref[:, span] = glow
        low_ref[:, pl.ds(mid + e * hidden_size, hidden_size)] = ulow
    low_ref[:, 2 * mid :] = dots.astype(BF)
    low = jnp.concatenate([low_ref[pl.ds(start, own), :] for start in starts], 0)
    begin = 0
    for kept_ref, sent_ref in zip(kept_refs, sent_refs):
        columns = kept_ref.shape[3]
        end = min(begin + columns, width)
        back = dot(low[:, : 2 * mid], both_ref[:, begin:end], 1, 0).astype(BF)
        if end - begin < columns:
            back = jnp.concatenate([back, low[:, 2 * mid :]], 1)
        begin = end
        for r in range(4):
            ref = sent_ref if r % 2 else kept_ref
            ref[0, r // 2] = back[r * own : (r + 1) * own]


def expert_rows(pieces, names, back_all, w_gate, w_up, both_turned, index, experts, block):
    count, width, hidden = w_gate.shape
    total, mid = back_all.shape
    owners = total // block
    groups = [piece.shape[-1] for piece in pieces[0]]
    side = sum(groups) - width

    def rows(columns):
        return pl.BlockSpec((block, columns), lambda i, index_ref: (i ^ index_ref[0], 0))

    def shape(columns):
        return jax.ShapeDtypeStruct((total, columns), BF)

    def given(columns, order):
        sizes = tuple(1 if axis == "dp" else 2 for axis, _ in order)

        def place(i, *_):
            return tuple(i // bit % 2 if axis == "dp" else 0 for axis, bit in order) + (0, 0)

        return pl.BlockSpec(sizes + (block // 4, columns), place)

    def part(columns):
        return pl.BlockSpec((1, 2, block // 4, columns), lambda i, *_: (i, 0, 0, 0))

    def part_shape(columns):
        return jax.ShapeDtypeStruct((owners, 2, block // 4, columns), BF)

    given_specs = [given(columns, order) for columns, order in zip(groups, names)]
    axes = [[axis for axis, _ in order].index("tensor") for order in names]
    outs = pl.pallas_call(
        functools.partial(expert_kernel, experts, axes),
        grid_spec=pltpu.PrefetchScalarGridSpec(
            num_scalar_prefetch=1,
            grid=(owners,),
            in_specs=given_specs * 2
            + [
                rows(mid),
                resident(w_gate.shape),
                resident(w_up.shape),
                resident(both_turned.shape),
            ],
            out_specs=[
                rows(width),
                rows(mid),
                pl.BlockSpec((mid, block), lambda i, index_ref: (0, i ^ index_ref[0])),
                rows(mid),
                rows(mid),
            ]
            + [part(columns) for columns in groups] * 2,
            scratch_shapes=[pltpu.VMEM((block, 2 * mid + side), BF), pltpu.VMEM((block, side), BF)],
        ),
        out_shape=[
            shape(width),
            shape(mid),
            jax.ShapeDtypeStruct((mid, total), BF),
            shape(mid),
            shape(mid),
        ]
        + [part_shape(columns) for columns in groups] * 2,
        compiler_params=PARAMS,
        cost_estimate=cost(4 * total * width * mid, total * width * 8, total * mid),
    )(index, *pieces[0], *pieces[1], back_all, w_gate, w_up, both_turned)
    return outs[:5], outs[5:8], outs[8:]


def gather_every(groups, orders, beside, later):
    totals, names = list(groups), [[] for _ in groups]
    for step in range(len(orders[0])):
        if step == len(orders[0]) - 1:
            totals, later = lax.optimization_barrier((totals, later))
        others = [swap(total, *order[step]) for total, order in zip(totals, orders)]
        if step == len(orders[0]) - 1:
            others, beside = lax.optimization_barrier((others, beside))
        totals = [jnp.stack([total, other]) for total, other in zip(totals, others)]
        for name, order in zip(names, orders):
            name.insert(0, order[step])
    return (totals, [swap(total, "tensor", 1) for total in totals]), names, beside, later


def sum_every(kept, sent, orders, beside, finish):
    bits = lax.axis_size("dp").bit_length() - 1
    totals, names = [], []
    for kept_group, sent_group in zip(kept, sent):
        own, columns = kept_group.shape[2:]
        total = kept_group.astype(F32) + swap(sent_group, "tensor", 1).astype(F32)
        totals.append(total.astype(BF).reshape((2,) * (bits + 1) + (own, columns)))
        names.append([("dp", 1 << (bits - 1 - i)) for i in range(bits)] + [("tensor", 2)])
    for step in range(bits + 1):
        if step == bits:
            totals, beside = lax.optimization_barrier((totals, beside[:1] + finish(*beside[1:])))
        halves, others = [], []
        for total, left, order in zip(totals, names, orders):
            axis = left.index(order[step])
            left.pop(axis)
            given = lax.index_in_dim(total, 1, axis, keepdims=False)
            halves.append(lax.index_in_dim(total, 0, axis, keepdims=False))
            others.append(swap(given, *order[step]))
        if step == 0:
            others, beside = lax.optimization_barrier((others, beside))
        totals = [(a.astype(F32) + b.astype(F32)).astype(BF) for a, b in zip(halves, others)]
    return list(zip(halves, others)), *beside


def out_kernel(core_ref, hid_ref, down_ref, kept_ref, sent_ref):
    count, hidden, _ = down_ref.shape
    own = kept_ref.shape[1]
    rows = []
    for r in range(4):
        start = pl.multiple_of((r // 2 * 2 + ((r % 2) ^ core_ref[0])) * own, own)
        rows.append(hid_ref[pl.ds(start, own), :])
    weight = down_ref[...].reshape(count * hidden, -1)
    out = dot(jnp.concatenate(rows, 0), weight, 1, 0).astype(BF)
    for r in range(4):
        ref = sent_ref if r % 2 else kept_ref
        ref[r // 2] = out[r * own : (r + 1) * own]


def expert_out(hid, w_down, core, block):
    count, hidden, width = w_down.shape
    total = hid.shape[0]
    out = pl.BlockSpec((2, block // 4, width), lambda i, *_: (i, 0, 0))
    shape = jax.ShapeDtypeStruct((total // block * 2, block // 4, width), BF)
    return pl.pallas_call(
        out_kernel,
        grid_spec=pltpu.PrefetchScalarGridSpec(
            num_scalar_prefetch=1,
            grid=(total // block,),
            in_specs=[
                pl.BlockSpec((block, count * hidden), lambda i, *_: (i, 0)),
                resident(w_down.shape),
            ],
            out_specs=[out, out],
        ),
        out_shape=[shape, shape],
        compiler_params=PARAMS,
        cost_estimate=cost(total * width * count * hidden, total * width * 3),
    )(core, hid, w_down)


def over_kernel(left_ref, right_ref, out_ref):
    count, _, hidden = out_ref.shape
    product = dot(left_ref[...], right_ref[...], 0, 0)

    @pl.when(pl.program_id(1) == 0)
    def _():
        for e in range(count):
            out_ref[e] = product[:, e * hidden : (e + 1) * hidden]

    @pl.when(pl.program_id(1) > 0)
    def _():
        for e in range(count):
            out_ref[e] += product[:, e * hidden : (e + 1) * hidden]


def over_rows(rows, low, shape, block=256, chunk=2048):
    count, width, hidden = shape
    total = rows.shape[0]
    chunk = min(chunk, total)
    return pl.pallas_call(
        over_kernel,
        grid=(width // block, total // chunk),
        in_specs=[
            pl.BlockSpec((chunk, block), lambda d, k: (k, d)),
            pl.BlockSpec((chunk, count * hidden), lambda d, k: (k, 0)),
        ],
        out_specs=pl.BlockSpec((count, block, hidden), lambda d, k: (0, d, 0)),
        out_shape=jax.ShapeDtypeStruct(shape, F32),
        compiler_params=PARAMS,
        cost_estimate=cost(total * width * count * hidden, total * width * 4),
    )(rows, low)


def turned_kernel(left_ref, right_ref, out_ref):
    product = dot(left_ref[...], right_ref[...], 1, 0)

    @pl.when(pl.program_id(1) == 0)
    def _():
        out_ref[...] = product

    @pl.when(pl.program_id(1) > 0)
    def _():
        out_ref[...] += product


def turned_rows(left, right, block=256, chunk=2048):
    mid, total = left.shape
    width = right.shape[1]
    chunk = min(chunk, total)
    return pl.pallas_call(
        turned_kernel,
        grid=(width // block, total // chunk),
        in_specs=[
            pl.BlockSpec((mid, chunk), lambda d, k: (0, k)),
            pl.BlockSpec((chunk, block), lambda d, k: (k, d)),
        ],
        out_specs=pl.BlockSpec((mid, block), lambda d, k: (0, d)),
        out_shape=jax.ShapeDtypeStruct((mid, width), F32),
        compiler_params=PARAMS,
        cost_estimate=cost(total * width * mid, total * width * 4),
    )(left, right)


def front_kernel(tokens_ref, gain_ref, query_ref, key_ref, value_ref, *outs):
    normed_ref, query_out_ref, key_out_ref, value_out_ref, squares_ref = outs

    @pl.when(pl.program_id(0) == 0)
    def _():
        state = tokens_ref[...].astype(F32)
        scale = lax.rsqrt(jnp.mean(state * state, -1, keepdims=True) + EPSILON)
        normed_ref[...] = (state * scale * gain_ref[...]).astype(BF)
        squares_ref[...] = jnp.zeros_like(squares_ref)

    normed = normed_ref[...]
    query = dot(normed, query_ref[...], 1, 0)
    key = dot(normed, key_ref[...], 1, 0)
    query_out_ref[...] = query
    key_out_ref[...] = key
    value_out_ref[...] = dot(normed, value_ref[...], 1, 0).astype(BF)
    squares_ref[...] += two_rows(query * query, key * key)


def row_sums(array):
    ones = jnp.ones((8, array.shape[1]), F32)
    return lax.dot_general(
        ones,
        array,
        (((1,), (1,)), ((), ())),
        precision=lax.Precision.HIGHEST,
        preferred_element_type=F32,
    )


def two_rows(first, second):
    row = lax.broadcasted_iota(jnp.int32, (8, first.shape[0]), 0)
    return jnp.where(row == 0, row_sums(first), jnp.where(row == 1, row_sums(second), 0.0))


def norm_kernel(tokens_ref, gain_ref, out_ref):
    state = tokens_ref[...].astype(F32)
    scale = lax.rsqrt(jnp.mean(state * state, -1, keepdims=True) + EPSILON)
    out_ref[...] = (state * scale * gain_ref[...]).astype(BF)


def norm_all(tokens, gain, block):
    total, width = tokens.shape
    return pl.pallas_call(
        norm_kernel,
        grid=(total // block,),
        in_specs=[pl.BlockSpec((block, width), lambda i: (i, 0)), resident((1, width))],
        out_specs=pl.BlockSpec((block, width), lambda i: (i, 0)),
        out_shape=jax.ShapeDtypeStruct((total, width), BF),
        compiler_params=PARAMS,
        cost_estimate=cost(0, total * width * 4),
    )(tokens, gain[None])


def project(tokens, gain, w_query, w_key, w_value, block=256):
    count, width = tokens.shape
    local = w_query.shape[1]
    weight = pl.BlockSpec((width, block), lambda i: (0, i))
    out = pl.BlockSpec((count, block), lambda i: (0, i))
    return pl.pallas_call(
        front_kernel,
        grid=(local // block,),
        in_specs=[resident(tokens.shape), resident((1, width)), weight, weight, weight],
        out_specs=[resident((count, width)), out, out, out, resident((8, count))],
        out_shape=[
            jax.ShapeDtypeStruct((count, width), BF),
            jax.ShapeDtypeStruct((count, local), F32),
            jax.ShapeDtypeStruct((count, local), F32),
            jax.ShapeDtypeStruct((count, local), BF),
            jax.ShapeDtypeStruct((8, count), F32),
        ],
        compiler_params=PARAMS,
        cost_estimate=cost(3 * count * width * local, 6 * width * local),
    )(tokens, gain[None], w_query, w_key, w_value)


def scales_of(sums, full_width):
    return lax.rsqrt(sums.T / full_width + EPSILON)


def pack_kernel(full_width, query_ref, key_ref, value_ref, sums_ref, *refs):
    query_gain_ref, key_gain_ref, cos_ref, sin_ref, segment_ref, out_ref = refs
    parts, heads = out_ref.shape[0] // query_gain_ref.shape[0], query_gain_ref.shape[0]
    size = cos_ref.shape[1]
    count = cos_ref.shape[0]
    part = count // parts
    scales = scales_of(sums_ref[...], full_width)
    for h in range(heads):
        span = slice(h * size, (h + 1) * size)

        def turned(ref, column, gain_ref):
            unit = ref[:, span] * scales[:, column : column + 1]
            vector = unit * gain_ref[pl.ds(h, 1), :]
            rolled = pltpu.roll(vector, size // 2, 1)
            return (vector * cos_ref[...] + rolled * sin_ref[...]).astype(BF)

        query = turned(query_ref, 0, query_gain_ref)
        key = turned(key_ref, 1, key_gain_ref)
        value = value_ref[:, span]
        for p in range(parts):
            place = h * parts + p
            out_ref[place, :part] = query[p * part : (p + 1) * part]
            out_ref[place, part : part + count] = key
            out_ref[place, part + count : part + 2 * count] = value
            out_ref[place, part + 2 * count :] = segment_ref[...]


def pack_heads(query, key, value, sums, query_gain, key_gain, cos, sin, segments, full_width):
    count = query.shape[0]
    size = cos.shape[1]
    parts = SPAN // query_gain.shape[0]
    return pl.pallas_call(
        functools.partial(pack_kernel, full_width),
        out_shape=jax.ShapeDtypeStruct(
            (SPAN, count // parts + 2 * count + segments.shape[0], size), BF
        ),
        compiler_params=PARAMS,
        cost_estimate=cost(0, 12 * query.size),
    )(query, key, value, sums, query_gain, key_gain, cos, sin, segments)


def head_views(got_ref, s, part, count):
    length = (s + 1) * count
    size = got_ref.shape[2]
    query = got_ref[s, :part]
    key = got_ref[: s + 1, part : part + count].reshape(length, size)
    value = got_ref[: s + 1, part + count : part + 2 * count].reshape(length, size)
    return query, key, value


def visible_pairs(got_ref, half, s, part, count):
    size = got_ref.shape[2]
    per_block = count // size
    first = part + 2 * count

    def rows(block):
        return got_ref[block, first : first + 16].astype(F32)

    row = lax.broadcasted_iota(jnp.int32, (16, size), 0)
    chosen = jnp.sum(jnp.where(row == half, rows(s), 0.0), 0, keepdims=True)
    own = jnp.broadcast_to(chosen, (size, size)).T
    pieces = []
    for block in range(s + 1):
        values = rows(block)
        for r in range(per_block):
            pieces.append(own == values[r : r + 1])
    pieces = [jnp.where(piece, 1.0, 0.0) for piece in pieces]
    same = jnp.concatenate(pieces, 1) > 0.5
    query_pos = s * count + half * part + lax.broadcasted_iota(jnp.int32, same.shape, 0)
    return same & (lax.broadcasted_iota(jnp.int32, same.shape, 1) <= query_pos)


def attend_kernel(part, count, half_ref, got_ref, mix_ref, log_ref):
    half = half_ref[0]
    size = got_ref.shape[2]
    for s in range(SPAN):
        query, key, value = head_views(got_ref, s, part, count)
        visible = visible_pairs(got_ref, half, s, part, count)
        scores = jnp.where(visible, dot(query, key, 1, 1) / math.sqrt(size), NEGATIVE)
        top = jnp.max(scores, -1, keepdims=True)
        weights = jnp.where(visible, jnp.exp(scores - top), 0.0)
        total = jnp.sum(weights, -1, keepdims=True)
        mix_ref[s] = dot((weights / total).astype(BF), value, 1, 0).astype(BF)
        log_ref[s] = jnp.broadcast_to(top + jnp.log(total), (part, size))


def attend(got, half, part, count):
    size = got.shape[2]
    return pl.pallas_call(
        functools.partial(attend_kernel, part, count),
        in_specs=[
            pl.BlockSpec(memory_space=pltpu.SMEM),
            pl.BlockSpec(memory_space=pltpu.VMEM),
        ],
        out_shape=[
            jax.ShapeDtypeStruct((SPAN, part, size), BF),
            jax.ShapeDtypeStruct((SPAN, part, size), F32),
        ],
        compiler_params=PARAMS,
        cost_estimate=cost(SPAN * SPAN * part * count * size, 4 * got.size, SPAN * SPAN * part * count),
    )(half, got)


def attend_back_kernel(part, count, half_ref, got_ref, log_ref, grad_ref, out_ref, key_sum, value_sum):
    half = half_ref[0]
    size = got_ref.shape[2]
    root = math.sqrt(size)
    for s in reversed(range(SPAN)):
        length = (s + 1) * count
        query, key, value = head_views(got_ref, s, part, count)
        visible = visible_pairs(got_ref, half, s, part, count)
        scores = dot(query, key, 1, 1) / root - log_ref[s, :, :1]
        probs = jnp.where(visible, jnp.exp(jnp.where(visible, scores, 0.0)), 0.0)
        grad = grad_ref[s]
        probs_grad = dot(grad, value, 1, 1)
        inner = jnp.sum(probs * probs_grad, -1, keepdims=True)
        low = (probs * (probs_grad - inner)).astype(BF)
        out_ref[s, :part] = (dot(low, key, 1, 0) / root).astype(BF)
        key_back = dot(low, query, 0, 0)
        value_back = dot(probs.astype(BF), grad, 0, 0)
        if s == SPAN - 1:
            key_sum[...] = key_back
            value_sum[...] = value_back
        else:
            key_sum[:length] += key_back
            value_sum[:length] += value_back
    for s in range(SPAN):
        span = slice(s * count, (s + 1) * count)
        out_ref[s, part : part + count] = (key_sum[span] / root).astype(BF)
        out_ref[s, part + count :] = value_sum[span].astype(BF)


def attend_back(got, half, log_total, mix_grad, part, count):
    size = got.shape[2]
    vmem = pl.BlockSpec(memory_space=pltpu.VMEM)
    return pl.pallas_call(
        functools.partial(attend_back_kernel, part, count),
        in_specs=[pl.BlockSpec(memory_space=pltpu.SMEM), vmem, vmem, vmem],
        out_shape=jax.ShapeDtypeStruct((SPAN, part + 2 * count, size), BF),
        scratch_shapes=[pltpu.VMEM((SPAN * count, size), F32)] * 2,
        compiler_params=PARAMS,
        cost_estimate=cost(
            3 * SPAN * SPAN * part * count * size, 6 * got.size, SPAN * SPAN * part * count
        ),
    )(half, got, log_total, mix_grad)


def block_rows(place, r, own, part):
    block = r ^ place
    per_part = part // own
    return block // per_part, pl.multiple_of(block % per_part * own, own)


def project_out_kernel(own, place_ref, mix_ref, weight_ref, kept_ref, sent_ref):
    parts = SPAN * LANES // weight_ref.shape[0]
    part = mix_ref.shape[1]
    rows = []
    for r in range(4):
        p, start = block_rows(place_ref[0], r, own, part)
        rows.append(
            jnp.concatenate(
                [mix_ref[h + p, pl.ds(start, own), :] for h in range(0, SPAN, parts)], 1
            )
        )
    product = dot(jnp.concatenate(rows, 0), weight_ref[...], 1, 0).astype(BF)
    for r in range(4):
        ref = sent_ref if r % 2 else kept_ref
        ref[r // 2] = product[r * own : (r + 1) * own]


def project_out(mix, w_out, place, own, block=512):
    local, width = w_out.shape
    out = pl.BlockSpec((2, own, block), lambda d, *_: (0, 0, d))
    shape = jax.ShapeDtypeStruct((2, own, width), BF)
    return pl.pallas_call(
        functools.partial(project_out_kernel, own),
        grid_spec=pltpu.PrefetchScalarGridSpec(
            num_scalar_prefetch=1,
            grid=(width // block,),
            in_specs=[resident(mix.shape), pl.BlockSpec((local, block), lambda d, *_: (0, d))],
            out_specs=[out, out],
        ),
        out_shape=[shape, shape],
        compiler_params=PARAMS,
        cost_estimate=cost(4 * own * local * width, local * width * 3),
    )(place, mix, w_out)


def middle_kernel(experts, place_ref, tokens_ref, kept_ref, core_ref, side_ref, *refs):
    gain_ref, router_ref, routes_ref, resid_ref, probs_ref, chosen_ref = refs[:6]
    row_refs = refs[6:]
    width = tokens_ref.shape[1]
    state = tokens_ref[...].astype(F32) + kept_ref[0].astype(F32)
    state = state + core_ref[0].astype(F32) + side_ref[...].astype(F32)
    resid_ref[...] = state
    scale = lax.rsqrt(jnp.mean(state * state, -1, keepdims=True) + EPSILON)
    normed = (state * scale * gain_ref[...]).astype(BF)
    logits = dot(normed, router_ref[...], 1, 0)
    lane = lax.broadcasted_iota(jnp.int32, logits.shape, 1)
    real = lane < experts
    top = jnp.max(jnp.where(real, logits, NEGATIVE), -1, keepdims=True)
    powers = jnp.exp(jnp.minimum(logits - top, 0.0))
    total = jnp.sum(jnp.where(real, powers, 0.0), -1, keepdims=True)
    probs = powers / total
    routes = routes_ref[...]
    chosen = jnp.zeros(logits.shape, F32)
    for k in range(routes.shape[1]):
        column = routes[:, k : k + 1]
        hit = (lane == column) | (lane == column + experts)
        chosen = jnp.where(hit, 1.0, chosen)
    probs_ref[...] = jnp.where(real, probs, 0.0)
    chosen_ref[...] = jnp.where(real, chosen, 0.0)
    gates = probs * chosen
    high = gates.astype(BF).astype(F32)
    side = jnp.where(real, high, jnp.where(lane < 2 * experts, gates - high, 0.0))
    rows = jnp.concatenate([normed, side.astype(BF)], 1)
    begin = 0
    for ref in row_refs:
        ref[...] = rows[:, begin : begin + ref.shape[1]]
        begin += ref.shape[1]


def middle(tokens, kept, core, side, gain, router_wide, routes, place, experts, groups):
    own, width = side.shape
    wide = router_wide.shape[1]
    shape = jax.ShapeDtypeStruct
    return pl.pallas_call(
        functools.partial(middle_kernel, experts),
        grid_spec=pltpu.PrefetchScalarGridSpec(
            num_scalar_prefetch=1,
            grid=(1,),
            in_specs=[
                pl.BlockSpec((own, width), lambda i, place_ref: (place_ref[0], 0)),
                resident(kept.shape),
                resident(core.shape),
                resident(side.shape),
                resident((1, width)),
                resident(router_wide.shape),
                pl.BlockSpec((own, routes.shape[1]), lambda i, place_ref: (place_ref[0], 0)),
            ],
            out_specs=[
                resident((own, width)),
                resident((own, wide)),
                resident((own, wide)),
            ]
            + [resident((own, columns)) for columns in groups],
        ),
        out_shape=[
            shape((own, width), F32),
            shape((own, wide), F32),
            shape((own, wide), F32),
        ]
        + [shape((own, columns), BF) for columns in groups],
        compiler_params=PARAMS,
        cost_estimate=cost(own * width * wide, own * width * 20),
    )(place, tokens, kept, core, side, gain[None], router_wide, routes)


def middle_back_kernel(experts, place_ref, *refs):
    homes = refs[:6]
    resid_ref, probs_ref, chosen_ref, gain_ref, router_ref, cotangent_ref = refs[6:12]
    grad_ref, low_ref, small_ref = refs[12:]
    width = resid_ref.shape[1]
    parts = [a[...].astype(F32) + b[...].astype(F32) for a, b in zip(homes[:3], homes[3:])]
    home = jnp.concatenate(parts, 1)
    side = home[:, width:]
    lanes = side.shape[1]
    gate_grad = (side + pltpu.roll(side, lanes - experts, 1)) * chosen_ref[...]
    probs = probs_ref[...]
    inner = jnp.sum(probs * gate_grad, -1, keepdims=True)
    logit_low = (probs * (gate_grad - inner)).astype(BF)
    state = resid_ref[...]
    scale = lax.rsqrt(jnp.mean(state * state, -1, keepdims=True) + EPSILON)
    unit = state * scale
    mid_grad = home[:, :width] + dot(logit_low, router_ref[...], 1, 1)
    scaled = mid_grad * gain_ref[...]
    grad = cotangent_ref[...].astype(F32) + scale * (
        scaled - unit * jnp.mean(scaled * unit, -1, keepdims=True)
    )
    grad_ref[...] = grad
    low_ref[...] = grad.astype(BF)
    normed = (unit * gain_ref[...]).astype(BF)
    small_ref[:experts] = dot(logit_low, normed, 0, 0)[:experts]
    d_gain = jnp.sum(mid_grad * unit, 0, keepdims=True)
    row = lax.broadcasted_iota(jnp.int32, (8, width), 0)
    small_ref[experts:] = jnp.where(row == 0, d_gain, 0.0)


def middle_back(homes, resid, probs, chosen, gain, router_wide, cotangent, place, experts):
    own, width = resid.shape
    shape = jax.ShapeDtypeStruct
    arrays = list(homes) + [resid, probs, chosen, gain[None], router_wide]
    return pl.pallas_call(
        functools.partial(middle_back_kernel, experts),
        grid_spec=pltpu.PrefetchScalarGridSpec(
            num_scalar_prefetch=1,
            grid=(1,),
            in_specs=[resident(a.shape) for a in arrays]
            + [pl.BlockSpec((own, width), lambda i, place_ref: (place_ref[0], 0))],
            out_specs=[
                resident((own, width)),
                resident((own, width)),
                resident((experts + 8, width)),
            ],
        ),
        out_shape=[
            shape((own, width), F32),
            shape((own, width), BF),
            shape((experts + 8, width), F32),
        ],
        compiler_params=PARAMS,
        cost_estimate=cost(2 * own * width * LANES, own * width * 30),
    )(place, *arrays, cotangent)


def spread(block):
    side = swap(block, "tensor", 2)
    core = swap(block, "tensor", 1)
    return block, core, side, swap(side, "tensor", 1)


def mix_back_kernel(place_ref, *refs):
    blocks, weight_ref, out_ref = refs[:4], refs[4], refs[5]
    own = blocks[0].shape[0]
    part, size = out_ref.shape[1:]
    parts = SPAN * size // weight_ref.shape[0]
    lows = jnp.concatenate([ref[...] for ref in blocks], 0)
    product = dot(lows, weight_ref[...], 1, 1).astype(BF)
    for r in range(4):
        p, start = block_rows(place_ref[0], r, own, part)
        for h in range(SPAN // parts):
            out_ref[h * parts + p, pl.ds(start, own), :] = product[
                r * own : (r + 1) * own, h * size : (h + 1) * size
            ]


def mix_back(blocks, w_out, place, part, size):
    vmem = pl.BlockSpec(memory_space=pltpu.VMEM)
    local, width = w_out.shape
    return pl.pallas_call(
        mix_back_kernel,
        in_specs=[pl.BlockSpec(memory_space=pltpu.SMEM)] + [vmem] * 5,
        out_shape=jax.ShapeDtypeStruct((SPAN, part, size), BF),
        compiler_params=PARAMS,
        cost_estimate=cost(4 * blocks[0].shape[0] * local * width, local * width * 4),
    )(place, *blocks, w_out)


def out_grad_kernel(place_ref, *refs):
    blocks, mix_ref, out_ref = refs[:4], refs[4], refs[5]
    own = blocks[0].shape[0]
    heads_parts, part, size = mix_ref.shape
    lows = jnp.concatenate([ref[...] for ref in blocks], 0)
    parts = 4 * own // part
    pieces = []
    for h in range(heads_parts // parts):
        rows = []
        for r in range(4):
            p, start = block_rows(place_ref[0], r, own, part)
            rows.append(mix_ref[h * parts + p, pl.ds(start, own), :])
        pieces.append(dot(jnp.concatenate(rows, 0), lows, 0, 0).astype(BF))
    if len(out_ref.shape) == 2:
        out_ref[...] = jnp.concatenate(pieces, 0)
        return
    rows, wide = out_ref.shape[1:]
    block = lows.shape[1]
    product = jnp.concatenate(pieces, 0)
    for q in range(wide // block):
        out_ref[0, :, q * block : (q + 1) * block] = product[q * rows : (q + 1) * rows]


def out_weight_grad(blocks, mix, place, local, owners):
    own, width = blocks[0].shape
    block = width // owners
    if block % LANES == 0:
        rows = local // owners
        out = pl.BlockSpec((1, rows, width), lambda d, *_: (d, 0, 0))
        shape = jax.ShapeDtypeStruct((owners, rows, width), BF)
    else:
        block = 4 * LANES
        out = pl.BlockSpec((local, block), lambda d, *_: (0, d))
        shape = jax.ShapeDtypeStruct((local, width), BF)
    column = pl.BlockSpec((own, block), lambda d, *_: (0, d))
    return pl.pallas_call(
        out_grad_kernel,
        grid_spec=pltpu.PrefetchScalarGridSpec(
            num_scalar_prefetch=1,
            grid=(width // block,),
            in_specs=[column] * 4 + [resident(mix.shape)],
            out_specs=out,
        ),
        out_shape=shape,
        compiler_params=PARAMS,
        cost_estimate=cost(4 * own * local * width, local * width * 3),
    )(place, *blocks, mix)


def unturn_kernel(full_width, back_ref, query_ref, key_ref, sums_ref, *refs):
    query_gain_ref, key_gain_ref, cos_ref, sin_ref = refs[:4]
    query_out_ref, key_out_ref, value_out_ref, inner_ref, gains_ref = refs[4:]
    heads, size = query_gain_ref.shape
    parts = SPAN // heads
    count = cos_ref.shape[0]
    part = count // parts
    scales = scales_of(sums_ref[...], full_width)
    inner = [0.0, 0.0]
    for h in range(heads):
        span = slice(h * size, (h + 1) * size)
        first = h * parts
        query = jnp.concatenate([back_ref[first + p, :part] for p in range(parts)], 0)
        key = sum(back_ref[first + p, part : part + count].astype(F32) for p in range(parts))
        value = sum(back_ref[first + p, part + count :].astype(F32) for p in range(parts))
        value_out_ref[:, span] = value.astype(BF)
        key = key.astype(BF)
        items = ((query, query_ref, query_gain_ref, query_out_ref), (key, key_ref, key_gain_ref, key_out_ref))
        for n, (grad, raw_ref, gain_ref, out_ref) in enumerate(items):
            grad = grad.astype(F32)
            gain_in = grad * cos_ref[...] - pltpu.roll(grad, size // 2, 1) * sin_ref[...]
            unit = raw_ref[:, span] * scales[:, n : n + 1]
            gains_ref[n * heads + h] = jnp.broadcast_to(
                jnp.sum(gain_in * unit, 0, keepdims=True), (8, size)
            )
            scaled = gain_in * gain_ref[pl.ds(h, 1), :]
            out_ref[:, span] = scaled
            inner[n] = inner[n] + scaled * unit
    inner_ref[...] = two_rows(inner[0], inner[1])


def unturn(back, query, key, sums, query_gain, key_gain, cos, sin, full_width):
    count, local = query.shape
    heads, size = query_gain.shape
    shape = jax.ShapeDtypeStruct
    return pl.pallas_call(
        functools.partial(unturn_kernel, full_width),
        out_shape=[
            shape((count, local), F32),
            shape((count, local), F32),
            shape((count, local), BF),
            shape((8, count), F32),
            shape((2 * heads, 8, size), F32),
        ],
        compiler_params=PARAMS,
        cost_estimate=cost(0, 24 * query.size),
    )(back, query, key, sums, query_gain, key_gain, cos, sin)


def columns_kernel(full_width, *refs):
    query_scaled_ref, key_scaled_ref, value_ref, query_ref, key_ref, sums_ref, inner_ref = refs[:7]
    query_low_ref, key_low_ref, out_ref = refs[7:]
    owners, rows, _ = out_ref.shape
    rows = rows // 3
    scales = scales_of(sums_ref[...], full_width)
    means = inner_ref[...].T / full_width
    items = ((query_scaled_ref, query_ref, query_low_ref), (key_scaled_ref, key_ref, key_low_ref))
    lows = []
    for n, (scaled_ref, raw_ref, low_ref) in enumerate(items):
        scale = scales[:, n : n + 1]
        unit = raw_ref[...] * scale
        low = (scale * (scaled_ref[...] - unit * means[:, n : n + 1])).astype(BF)
        low_ref[...] = low
        lows.append(low)
    for n, low in enumerate(lows + [value_ref[...]]):
        turned = low.T
        for d in range(owners):
            out_ref[d, n * rows : (n + 1) * rows] = turned[d * rows : (d + 1) * rows]


def columns_of(query_scaled, key_scaled, value, query, key, sums, inner, full_width, owners):
    count, local = query.shape
    low = jax.ShapeDtypeStruct((count, local), BF)
    return pl.pallas_call(
        functools.partial(columns_kernel, full_width),
        out_shape=[low, low, jax.ShapeDtypeStruct((owners, 3 * local // owners, count), BF)],
        compiler_params=PARAMS,
        cost_estimate=cost(0, 24 * query.size),
    )(query_scaled, key_scaled, value, query, key, sums, inner)


def input_kernel(own, place_ref, *refs):
    lows, weights, kept_ref, sent_ref = refs[:3], refs[3:6], refs[6], refs[7]
    place = place_ref[0]
    total = None
    for low_ref, weight_ref in zip(lows, weights):
        rows = [
            low_ref[pl.ds(pl.multiple_of((r ^ place) * own, own), own), :] for r in range(4)
        ]
        product = dot(jnp.concatenate(rows, 0), weight_ref[...], 1, 1)
        total = product if total is None else total + product
    total = total.astype(BF)
    for r in range(4):
        ref = sent_ref if r % 2 else kept_ref
        ref[r // 2] = total[r * own : (r + 1) * own]


def input_back(lows, weights, place, own, block=512):
    width, local = weights[0].shape
    out = pl.BlockSpec((2, own, block), lambda d, *_: (0, 0, d))
    shape = jax.ShapeDtypeStruct((2, own, width), BF)
    return pl.pallas_call(
        functools.partial(input_kernel, own),
        grid_spec=pltpu.PrefetchScalarGridSpec(
            num_scalar_prefetch=1,
            grid=(width // block,),
            in_specs=[resident(lows[0].shape)] * 3
            + [pl.BlockSpec((block, local), lambda d, *_: (d, 0))] * 3,
            out_specs=[out, out],
        ),
        out_shape=[shape, shape],
        compiler_params=PARAMS,
        cost_estimate=cost(12 * own * local * width, local * width * 7),
    )(place, *lows, *weights)


def last_kernel(place_ref, tokens_ref, *refs):
    kept_ref, core_ref, side_ref, grad_ref, gain_ref, small_ref, out_ref = refs
    own = grad_ref.shape[0]
    extra = out_ref.shape[0] - own
    used = small_ref.shape[0]
    state = tokens_ref[...].astype(F32)
    scale = lax.rsqrt(jnp.mean(state * state, -1, keepdims=True) + EPSILON)
    unit = state * scale
    grad = kept_ref[0].astype(F32) + core_ref[0].astype(F32) + side_ref[...].astype(F32)
    scaled = grad * gain_ref[...]
    out = grad_ref[...] + scale * (scaled - unit * jnp.mean(scaled * unit, -1, keepdims=True))
    out_ref[:own] = out.astype(BF)
    d_gain = jnp.sum(grad * unit, 0, keepdims=True)
    row = lax.broadcasted_iota(jnp.int32, (8, state.shape[1]), 0)
    gains = small_ref[used - 8 :] + jnp.where(row == 1, d_gain, 0.0)
    rows = [small_ref[: used - 8], gains]
    if extra > used:
        rows.append(jnp.zeros((extra - used, state.shape[1]), F32))
    out_ref[own:] = jnp.concatenate(rows, 0).astype(BF)


def last(tokens, kept, core, side, grad, gain, small, place):
    own, width = side.shape
    arrays = [kept, core, side, grad, gain[None], small]
    rows = own + -(-small.shape[0] // 16) * 16
    return pl.pallas_call(
        last_kernel,
        grid_spec=pltpu.PrefetchScalarGridSpec(
            num_scalar_prefetch=1,
            grid=(1,),
            in_specs=[pl.BlockSpec((own, width), lambda i, place_ref: (place_ref[0], 0))]
            + [resident(a.shape) for a in arrays],
            out_specs=resident((rows, width)),
        ),
        out_shape=jax.ShapeDtypeStruct((rows, width), BF),
        compiler_params=PARAMS,
        cost_estimate=cost(0, own),
    )(place, tokens, *arrays)


def join_kernel(own, place_ref, *refs):
    out_ref = refs[4]
    for r in range(4):
        start = pl.multiple_of((r ^ place_ref[0]) * own, own)
        out_ref[pl.ds(start, own), :] = refs[r][:own].astype(out_ref.dtype)


def join_blocks(blocks, place, own, kind):
    width = blocks[0].shape[1]
    vmem = pl.BlockSpec(memory_space=pltpu.VMEM)
    return pl.pallas_call(
        functools.partial(join_kernel, own),
        in_specs=[pl.BlockSpec(memory_space=pltpu.SMEM)] + [vmem] * 4,
        out_shape=jax.ShapeDtypeStruct((4 * own, width), kind),
        compiler_params=PARAMS,
        cost_estimate=cost(0, own),
    )(place, *blocks)


def weights_kernel(columns_ref, rows_ref, small_ref, out_ref):
    owners, columns, count = columns_ref.shape
    total = None
    for s in range(owners):
        product = dot(columns_ref[s], rows_ref[pl.ds(s * count, count), :], 1, 0)
        total = product if total is None else total + product
    out_ref[0, :columns] = total.astype(BF)
    out_ref[0, columns:] = small_ref[0]


def weight_columns(columns, rows, small):
    owners, count3, count = columns.shape
    width = rows.shape[1]
    slab = width // owners
    extra = small.shape[1]
    return pl.pallas_call(
        weights_kernel,
        grid=(owners,),
        in_specs=[
            resident(columns.shape),
            pl.BlockSpec((rows.shape[0], slab), lambda d: (0, d)),
            pl.BlockSpec((1, extra, slab), lambda d: (d, 0, 0)),
        ],
        out_specs=pl.BlockSpec((1, count3 + extra, slab), lambda d: (d, 0, 0)),
        out_shape=jax.ShapeDtypeStruct((owners, count3 + extra, slab), BF),
        compiler_params=PARAMS,
        cost_estimate=cost(rows.shape[0] * width * count3, rows.size * 2),
    )(columns, rows, small)


def per_device(
    tokens,
    segment_ids,
    routes,
    norm1_gain,
    w_query,
    w_key,
    w_value,
    query_gain,
    key_gain,
    w_out,
    norm2_gain,
    w_router,
    w_gate,
    w_up,
    w_down,
    cotangent,
):
    tok_count, model_width = tokens.shape
    heads_here, head_size = query_gain.shape
    local_width = heads_here * head_size
    tensor_count = lax.axis_size("tensor")
    full_width = local_width * tensor_count
    experts = w_router.shape[1]
    owners = lax.axis_size("dp")
    dp_place = lax.axis_index("dp")
    tensor_place = lax.axis_index("tensor")
    own = tok_count // tensor_count
    parts = SPAN // heads_here
    part = tok_count // parts
    groups = [list(range(g, g + SPAN)) for g in range(0, owners, SPAN)]
    place = tensor_place.astype(jnp.int32).reshape(1)
    index = jnp.stack([dp_place, tensor_place]).astype(jnp.int32)
    half = (dp_place % SPAN % parts).astype(jnp.int32).reshape(1)

    def mine(array):
        return lax.dynamic_slice_in_dim(array, tensor_place * own, own, 0)

    def trade(array):
        return lax.all_to_all(
            array, "dp", split_axis=0, concat_axis=0, tiled=True, axis_index_groups=groups
        )

    def sum_tensor(kept, sent):
        core = swap(sent, "tensor", 1)
        given = (kept[1].astype(F32) + core[1].astype(F32)).astype(BF)
        return kept, core, swap(given, "tensor", 2)

    out_grad_all = lax.all_gather(mine(cotangent), EVERY, axis=0, tiled=True)
    both_turned, down_turned = turn_weights(w_gate, w_up, w_down)
    side_width = -(-2 * experts // LANES) * LANES
    router_wide = jnp.pad(
        jnp.concatenate([w_router, w_router], 1), ((0, 0), (0, side_width - 2 * experts))
    )
    local_pos = jnp.arange(tok_count, dtype=jnp.int32)
    positions = (dp_place % SPAN * tok_count + local_pos).astype(F32)
    cos_table, sin_table = rope_tables(positions, head_size)
    segment_rows = jnp.pad(
        segment_ids.astype(BF).reshape(-1, head_size), ((0, 16 - tok_count // head_size), (0, 0))
    )

    normed_in, query_raw, key_raw, value_att, squares = project(
        tokens, norm1_gain, w_query, w_key, w_value
    )
    squares = lax.psum(squares, "tensor")
    packed = pack_heads(
        query_raw,
        key_raw,
        value_att,
        squares,
        query_gain,
        key_gain,
        cos_table,
        sin_table,
        segment_rows,
        full_width,
    )
    got, both_turned, down_turned = lax.optimization_barrier(
        (trade(packed), both_turned, down_turned)
    )
    mix_heads, log_total = attend(got, half, part, tok_count)
    mix = trade(mix_heads)
    kept, core, side = sum_tensor(*project_out(mix, w_out, place, own))
    lanes = -(-(model_width + side_width) // (3 * LANES)) * LANES
    resid_state, router_probs, chosen, *rows_own = middle(
        tokens,
        kept,
        core,
        side,
        norm2_gain,
        router_wide,
        routes,
        place,
        experts,
        [lanes, lanes, model_width + side_width - 2 * lanes],
    )
    bits = owners.bit_length() - 1
    first_three = [("tensor", 2), ("dp", 1), ("dp", 2)]
    rest = [("dp", 1 << b) for b in range(2, bits)]
    orders = [first_three[g:] + first_three[:g] + rest for g in range(3)]
    pieces, names, back_all, tokens_own = gather_every(
        rows_own,
        [order[::-1] for order in orders],
        hidden_back(out_grad_all, down_turned),
        mine(tokens),
    )
    tokens_all = lax.all_gather(tokens_own, EVERY, axis=0, tiled=True)
    (rows_all, hid, hid_turned, glow, ulow), kept_groups, sent_groups = expert_rows(
        pieces, names, back_all, w_gate, w_up, both_turned, index, experts, tok_count
    )
    d_w_gate = over_rows(rows_all, glow, w_gate.shape)
    out_kept, out_sent = expert_out(hid, w_down, place % 2, tok_count)

    def add_core(kept_rows, sent_rows):
        core_rows = swap(sent_rows, "tensor", 1)
        return ((kept_rows.astype(F32) + core_rows.astype(F32)).astype(BF),)

    homes, d_w_gate, out_part = sum_every(
        kept_groups, sent_groups, orders, (d_w_gate, out_kept, out_sent), add_core
    )
    core_groups = [
        [d * tensor_count + x * 2 + c for d in range(owners) for x in range(2)] for c in range(2)
    ]
    expert_full = lax.psum_scatter(
        out_part.reshape(-1, model_width),
        EVERY,
        scatter_dimension=0,
        tiled=True,
        axis_index_groups=core_groups,
    )
    d_w_down = turned_rows(hid_turned, out_grad_all).reshape(w_down.shape)
    d_w_up = over_rows(rows_all, ulow, w_up.shape)
    normed_in_all = norm_all(tokens_all, norm1_gain, tok_count)

    resid_grad, resid_low, small = middle_back(
        [home[0] for home in homes] + [home[1] for home in homes],
        resid_state,
        router_probs,
        chosen,
        norm2_gain,
        router_wide,
        cotangent,
        place,
        experts,
    )
    resid_blocks = spread(resid_low)
    mix_grad = trade(mix_back(resid_blocks, w_out, place, part, head_size))
    d_out = out_weight_grad(resid_blocks, mix, place, local_width, owners)
    mix_grad, d_out = lax.optimization_barrier((mix_grad, d_out))
    back, d_w_down, d_w_up, normed_in_all = lax.optimization_barrier(
        (
            trade(attend_back(got, half, log_total, mix_grad, part, tok_count)),
            d_w_down,
            d_w_up,
            normed_in_all,
        )
    )
    d_out, expert_full = lax.optimization_barrier((d_out, expert_full))
    model_slice = model_width // owners
    if model_slice % LANES == 0:
        d_out = lax.psum_scatter(d_out, "dp", scatter_dimension=0, tiled=True)[0]
        d_out = d_out.reshape(own, owners, model_slice).transpose(1, 0, 2)
        d_out = d_out.reshape(local_width, model_slice).astype(F32)
    else:
        d_out = lax.psum_scatter(d_out, "dp", scatter_dimension=1, tiled=True).astype(F32)
    block_own = (resid_state + expert_full.astype(F32)).astype(BF)
    block_output = join_blocks(spread(block_own), place, own, BF)

    query_scaled, key_scaled, value_low, inner, gains = unturn(
        back, query_raw, key_raw, squares, query_gain, key_gain, cos_table, sin_table, full_width
    )
    inner = lax.psum(inner, "tensor")
    query_low, key_low, columns = columns_of(
        query_scaled, key_scaled, value_low, query_raw, key_raw, squares, inner, full_width, owners
    )
    columns = lax.all_to_all(columns, "dp", split_axis=0, concat_axis=0, tiled=True)
    kept, core, side = sum_tensor(
        *input_back(
            (query_low, key_low, value_low), (w_query, w_key, w_value), place, own
        )
    )
    input_blocks = spread(
        last(tokens, kept, core, side, resid_grad, norm1_gain, small, place)
    )
    input_grad = join_blocks(input_blocks, place, own, F32)

    head_slice = head_size // owners
    slice_width = local_width // owners
    gain_count = 2 * heads_here * head_slice
    gain_rows = -(-gain_count // model_slice)
    gains = gains[:, 0].reshape(2 * heads_here, owners, head_slice).transpose(1, 0, 2)
    gains = jnp.pad(
        gains.reshape(owners, gain_count), ((0, 0), (0, gain_rows * model_slice - gain_count))
    ).reshape(owners, gain_rows, model_slice)
    shared = sum(block[own : own + experts + 2].astype(F32) for block in input_blocks)
    shared = shared.reshape(experts + 2, owners, model_slice).transpose(1, 0, 2)
    extra = jnp.concatenate([shared, gains], 1).astype(BF)
    extra = jnp.pad(extra, ((0, 0), (0, -extra.shape[1] % 16), (0, 0)))
    if model_slice % LANES == 0:
        final = weight_columns(columns, normed_in_all, extra)
    else:
        columns = columns.transpose(1, 0, 2).reshape(3 * slice_width, owners * tok_count)
        final = dot(columns, normed_in_all, 1, 0).reshape(3 * slice_width, owners, model_slice)
        final = jnp.concatenate([final.transpose(1, 0, 2).astype(BF), extra], 1)
    final = lax.all_to_all(final, "dp", split_axis=0, concat_axis=0, tiled=True)
    weights = final[:, : 3 * slice_width].reshape(owners, 3, slice_width, model_slice)
    weights = weights.transpose(1, 3, 0, 2).reshape(3, model_slice, local_width).astype(F32)
    extra = jnp.sum(final[:, 3 * slice_width :].astype(F32), 0)
    gains = extra[experts + 2 : experts + 2 + gain_rows].reshape(-1)[:gain_count]
    gains = gains.reshape(2, heads_here, head_slice)

    return (
        block_output,
        input_grad,
        extra[experts + 1],
        weights[0],
        weights[1],
        weights[2],
        gains[0],
        gains[1],
        d_out,
        extra[experts],
        extra[:experts].T,
        d_w_gate,
        d_w_up,
        d_w_down,
    )


def solution(mesh):
    in_specs = (
        P("dp", None),
        P("dp"),
        P("dp", None),
        P(),
        P(None, "tensor"),
        P(None, "tensor"),
        P(None, "tensor"),
        P("tensor", None),
        P("tensor", None),
        P("tensor", None),
        P(),
        P(),
        P("dp", None, "tensor"),
        P("dp", None, "tensor"),
        P("dp", "tensor", None),
        P("dp", None),
    )
    out_specs = (
        P("dp", None),
        P("dp", None),
        P("dp"),
        P("dp", "tensor"),
        P("dp", "tensor"),
        P("dp", "tensor"),
        P("tensor", "dp"),
        P("tensor", "dp"),
        P("tensor", "dp"),
        P("dp"),
        P("dp", None),
        P("dp", None, "tensor"),
        P("dp", None, "tensor"),
        P("dp", "tensor", None),
    )
    return jax.shard_map(
        per_device, mesh=mesh, in_specs=in_specs, out_specs=out_specs, check_vma=False
    )
```

time: 663 us -> 538 us (0.81)
  Pallas kernels: 101 us -> 176 us
  blocking collectives: 88.8 us -> 33.8 us
  waiting for transfers between devices: 233 us -> 185 us
  local copies, waits for them, and re-layouts: 70.3 us -> 29.8 us
  matrix products: 38.2 us -> 0 us
  other arithmetic: 58 us -> 22.1 us
  starting transfers between devices: 49.2 us -> 66.1 us
    pallas_call x5 -> x20, Pallas kernels: 59.6 us -> 135 us  [the longest x1 29.1 us: expert_rows(): pl.pallas_call(functools.partial(expert_kernel, experts, axes), grid_spec...]
    all_gather x2 -> x1, waiting for transfers between devices: 66.2 us -> 0.01 us  [per_device(): tokens_all = lax.all_gather(tokens_own, EVERY, axis=0, tiled=True)]
    all_to_all x2 -> x1, blocking collectives: 62.7 us -> 18 us  [trade(): lax.all_to_all(array, 'dp', split_axis=0, concat_axis=0, tiled=True, axis...]
    dot_general x19 -> x0, matrix products: 38.2 us -> none  [the longest x14 29.2 us: dot(): lax.dot_general(left_side, right_side, (((left_dim,), (right_dim,)), ((),...]
    all_to_all x1, waiting for transfers between devices: 0.01 us -> 27.9 us  [per_device(): final = lax.all_to_all(final, 'dp', split_axis=0, concat_axis=0, tiled=True)]
    all_to_all x2 -> x3, waiting for transfers between devices: 58.6 us -> 44.6 us  [trade(): lax.all_to_all(array, 'dp', split_axis=0, concat_axis=0, tiled=True, axis...]
    dot_general x3 -> x0, local copies, waits for them, and re-layouts: 13.3 us -> none  [the longest x1 12.4 us: dot(): lax.dot_general(left_side, right_side, (((left_dim,), (right_dim,)), ((),...]
    reshape x11 -> x5, local copies, waits for them, and re-layouts: 11.9 us -> 0.13 us  [the longest x1 0.09 us: per_device(): gains.reshape(owners, gain_count)]
  transfers between devices with their start and end apart: 34 -> 53, of which waited for: 19 -> 31; matrix products, arithmetic and copies ran while one was open for 22% -> 7% of each run, Pallas kernels for 15% -> 33%
where the time goes in v2:
time: 538 us; the launch traced here: 527 us
  waiting for transfers between devices  185 us (34%)
  Pallas kernels  176 us (33%)
  starting transfers between devices  66.1 us (12%)
  blocking collectives  33.8 us (6%)
  local copies, waits for them, and re-layouts  29.8 us (6%)
  other arithmetic  22.1 us (4%)
  between operations  14.9 us (3%)
    ppermute x44, waiting for transfers between devices, swap(): return lax.ppermute(array, axis, [(i, i ^ bit) for i in range(count)])  99.5 us
    all_to_all x3, waiting for transfers between devices, trade(): lax.all_to_all(array, 'dp', split_axis=0, concat_axis=0, tiled=True, axis...  44.6 us
    ppermute x44, starting transfers between devices, swap(): return lax.ppermute(array, axis, [(i, i ^ bit) for i in range(count)])  36 us
    pallas_call x1, Pallas kernels, expert_rows(): pl.pallas_call(functools.partial(expert_kernel, experts, axes), grid_spec...  29.1 us
    all_to_all x1, waiting for transfers between devices, per_device(): final = lax.all_to_all(final, 'dp', split_axis=0, concat_axis=0, tiled=True)  27.9 us
    pallas_call x2, Pallas kernels, over_rows(): pl.pallas_call(over_kernel, grid=(width // block, total // chunk), in_spe...  21.9 us
    all_to_all x3, starting transfers between devices, trade(): lax.all_to_all(array, 'dp', split_axis=0, concat_axis=0, tiled=True, axis...  18.6 us
    all_to_all x1, blocking collectives, trade(): lax.all_to_all(array, 'dp', split_axis=0, concat_axis=0, tiled=True, axis...  18 us
  transfers between devices with their start and end apart: 53, of which 31 were waited for; matrix products, arithmetic and copies ran while one was open for 7% of the time, Pallas kernels for 33%

profile of v2, /device:TPU:0, one launch (start us, length us, event | category | flops | bytes accessed | tf_op | source)
XLA Modules:
  0.0 527.3 jit_solution(9235248889793761042)
XLA Ops:
  10.2 6.6 %shard_map.263 = (bf16[256,2048]{1,0:T(8,128)(2,1)}, f32[256,512]{1,0:T(8,128)}, f32[256,512]{1,0:T(8,128)}, bf16[256,512]{1,0:T(8,128)(2,1)}, f32[8,256]{1,0:T(8,128)}) custom-call(bf16[256,2048]{1,0:T(8,128)(2,1)} %tokens_ref.5, f32[1,2048]{1,0:T(1,128)} %bitcast.183, bf16[2048,512]{1,0:T(8,128)(2,1)} %refs_3_.1, bf16[2048,512]{1,0:T(8,128)(2,1)} %refs_4_.3, ...), custom_call_target="tpu_custom_call" | custom-call | flops 1610612736 | bytes 6291456 | tf_op jit(solution)/shard_map/pallas_call | solution.py:430
  16.8 9.2 %psum.14.sums_ref.refs_5_ = f32[8,256]{1,0:T(8,128)} all-reduce(f32[8,256]{1,0:T(8,128)} %get-tuple-element.89), channel_id=1, replica_groups=mesh['dp'=8,'tensor'=4] {'tensor'}, use_global_device_ids=true, to_apply=%region_0.1 | all-reduce | flops 2048 | bytes 16384 | tf_op jit(solution)/shard_map/psum | solution.py:1117
  27.4 3.1 shard_map.264
  30.5 5.8 %all-to-all-start = ((bf16[8,656,128]{2,1,0:T(8,128)(2,1)}), bf16[8,656,128]{2,1,0:T(8,128)(2,1)S(1)}, u32[]{:S(2)}, u32[]{:S(2)}) async-start(bf16[8,656,128]{2,1,0:T(8,128)(2,1)} %shard_map.264), calls=%async_computation | async-start | bytes 2686976 | tf_op jit(solution)/shard_map/all_to_all | solution.py:1092
  36.4 8.4 %shard_map.265 = (bf16[1024,2048]{1,0:T(8,128)(2,1)}, bf16[2048,512]{1,0:T(8,128)(2,1)}) custom-call(bf16[2,2048,256]{2,1,0:T(8,128)(2,1)} %refs_7_.1, bf16[2,2048,256]{2,1,0:T(8,128)(2,1)} %refs_8_.1, bf16[2,256,2048]{2,1,0:T(8,128)(2,1)} %down_ref.3), custom_call_target="tpu_custom_call" | custom-call | bytes 12582912 | tf_op jit(solution)/shard_map/pallas_call | solution.py:68
  44.7 33.8 %all-to-all-done.got_ref = bf16[8,656,128]{2,1,0:T(8,128)(2,1)S(1)} async-done(((bf16[8,656,128]{2,1,0:T(8,128)(2,1)}), bf16[8,656,128]{2,1,0:T(8,128)(2,1)S(1)}, u32[]{:S(2)}, u32[]{:S(2)}) %all-to-all-start) | async-done | bytes 1343520 | tf_op jit(solution)/shard_map/all_to_all | solution.py:1092
  79.6 7.1 %shard_map.266 = (bf16[8,128,128]{2,1,0:T(8,128)(2,1)}, f32[8,128,128]{2,1,0:T(8,128)}) custom-call(s32[1]{0:T(128)} %bitcast.1.half_ref, bf16[8,656,128]{2,1,0:T(8,128)(2,1)} %copy-done.8), custom_call_target="tpu_custom_call" | custom-call | flops 536870912 | bytes 2686976 | tf_op jit(solution)/shard_map/pallas_call | solution.py:539
  86.7 18.0 %all_to_all.30.mix_ref.refs_4_ = bf16[8,128,128]{2,1,0:T(8,128)(2,1)} all-to-all(bf16[8,128,128]{2,1,0:T(8,128)(2,1)} %get-tuple-element.93), channel_id=1, replica_groups={{0,4,8,12,16,20,24,28},{1,5,9,13,17,21,25,29},{2,6,10,14,18,22,26,30},{..., dimensions={0} | all-to-all | bytes 524288 | tf_op jit(solution)/shard_map/all_to_all | solution.py:1092
  104.7 4.3 shard_map.267
  116.1 4.9 collective-permute-done.1.side_ref
  121.8 2.8 shard_map.268
  127.9 8.2 %collective-permute-done.8 = bf16[64,640]{1,0:T(8,128)(2,1)S(1)} collective-permute-done((bf16[64,640]{1,0:T(8,128)(2,1)}, bf16[64,640]{1,0:T(8,128)(2,1)S(1)}, u32[]{:S(2)}, u32[]{:S(2)}) %collective-permute-start.8) | collective-permute-done | bytes 81952 | tf_op jit(solution)/shard_map/ppermute | solution.py:42
  144.0 4.0 collective-permute-done.6
  152.6 3.6 collective-permute-done.7
  161.4 10.8 %shard_map.269.refs_6_ = f32[2048,512]{1,0:T(8,128)} custom-call(bf16[2048,2048]{1,0:T(8,128)(2,1)} %all-gather.3.cloned.1.call-done.grad_ref.right_ref, bf16[2048,512]{1,0:T(8,128)(2,1)} %get-tuple-element.103.down_ref), custom_call_target="tpu_custom_call" | custom-call | flops 4294967296 | bytes 12582912 | tf_op jit(solution)/shard_map/pallas_call | solution.py:92
  172.2 3.1 collective-permute-done.13
  181.2 3.9 collective-permute-done.16.refs_5_
  188.0 29.1 %shard_map.270 = (bf16[2048,2048]{1,0:T(8,128)(2,1)}, bf16[2048,512]{1,0:T(8,128)(2,1)}, bf16[512,2048]{1,0:T(8,128)(2,1)}, bf16[2048,512]{1,0:T(8,128)(2,1)}, b...) custom-call(s32[2]{0:T(128)} %pad_add_fusion.index_ref, ...), custom_call_target="tpu_custom_call" | custom-call | flops 17179869184 | bytes 33554432 | tf_op jit(solution)/shard_map/pallas_call | solution.py:198
  227.8 10.9 %shard_map.271 = f32[2,2048,256]{2,1,0:T(8,128)} custom-call(bf16[2048,2048]{1,0:T(8,128)(2,1)} %get-tuple-element.115.left_ref, bf16[2048,512]{1,0:T(8,128)(2,1)} %get-tuple-element.116.right_ref), custom_call_target="tpu_custom_call" | custom-call | flops 4294967296 | bytes 16777216 | tf_op jit(solution)/shard_map/pallas_call | solution.py:327
  238.8 10.2 %shard_map.272 = (bf16[16,64,2048]{2,1,0:T(8,128)(2,1)}, bf16[16,64,2048]{2,1,0:T(8,128)(2,1)}) custom-call(s32[1]{0:T(128)S(6)} %select_n.26.core_ref, bf16[2048,512]{1,0:T(8,128)(2,1)} %get-tuple-element.117.hid_ref, bf16[2,256,2048]{2,1,0:T(8,128)(2,1)} %down_ref.3), custom_call_target="tpu_custom_call" | custom-call | flops 4294967296 | bytes 12582912 | tf_op jit(solution)/shard_map/pallas_call | solution.py:291
  252.7 6.8 %collective-permute-done.27 = bf16[2,2,64,640]{3,2,0,1:T(8,128)(2,1)S(1)} collective-permute-done((bf16[2,2,64,640]{3,2,0,1:T(8,128)(2,1)S(1)}, bf16[2,2,64,640]{3,2,0,1:T(8,128)(2,1)S(1)}, u32[]{:S(2)}, u32[]{:S(2)}) %collective-permute-start.27) | collective-permute-done | bytes 327712 | tf_op jit(solution)/shard_map/ppermute | solution.py:42
  269.3 4.1 add_convert_fusion
  274.0 5.5 %collective-permute-start.30 = (bf16[64,768]{1,0:T(8,128)(2,1)S(1)}, bf16[64,768]{1,0:T(8,128)(2,1)S(1)}, u32[]{:S(2)}, u32[]{:S(2)}) collective-permute-start(bf16[64,768]{1,0:T(8,128)(2,1)S(1)} %get-tuple-element.219), channel_id=1, source_target_pairs={{0,16},{4,20},{8,24},{12,28},{16,0},{20,4},{24,8},{28,12},{1,17},{... | collective-permute-start | bytes 294920 | tf_op jit(solution)/shard_map/ppermute | solution.py:42
  280.9 2.9 collective-permute-start.32
  283.8 12.2 %collective-permute-done.32.refs_5_ = bf16[64,640]{1,0:T(8,128)(2,1)S(1)} collective-permute-done((bf16[64,640]{1,0:T(8,128)(2,1)S(1)}, bf16[64,640]{1,0:T(8,128)(2,1)S(1)}, u32[]{:S(2)}, u32[]{:S(2)}) %collective-permute-start.32) | collective-permute-done | bytes 81952 | tf_op jit(solution)/shard_map/ppermute | solution.py:42
  296.7 3.2 shard_map.273
  299.9 16.5 %collective-permute-done.34.refs_2_ = bf16[64,2048]{1,0:T(8,128)(2,1)S(1)} collective-permute-done((bf16[64,2048]{1,0:T(8,128)(2,1)}, bf16[64,2048]{1,0:T(8,128)(2,1)S(1)}, u32[]{:S(2)}, u32[]{:S(2)}) %collective-permute-start.34) | collective-permute-done | bytes 262176 | tf_op jit(solution)/shard_map/ppermute | solution.py:42
  318.7 3.4 shard_map.274
  322.1 7.3 %all-to-all-start.2 = ((bf16[8,128,128]{2,1,0:T(8,128)(2,1)}), bf16[8,128,128]{2,1,0:T(8,128)(2,1)S(1)}, u32[]{:S(2)}, u32[]{:S(2)}) async-start(bf16[8,128,128]{2,1,0:T(8,128)(2,1)} %shard_map.274), calls=%async_computation.2 | async-start | bytes 524288 | tf_op jit(solution)/shard_map/all_to_all | solution.py:1092
  329.4 6.3 %shard_map.275 = bf16[8,64,2048]{2,1,0:T(8,128)(2,1)} custom-call(s32[1]{0:T(128)} %bitcast.place_ref, bf16[64,2048]{1,0:T(8,128)(2,1)} %get-tuple-element.131.refs_0_, bf16[64,2048]{1,0:T(8,128)(2,1)} %copy-done.13, bf16[64,2048]{1,0:T(8,128)(2,1)} %copy-done.12, bf16[64,2048]{1,0:T(8,128)(2,1)} %copy-done.14, bf16[8,128,128]{2,1,0:T(8,128)(2,1)} %all_to_all.30.mix_ref.refs_4_), custom_call_target="tpu_custom_call" | custom-call | flops 536870912 | bytes 3145728 | tf_op jit(solution)/shard_map/pallas_call | solution.py:834
  335.7 5.4 %all-to-all-done.2.grad_ref = bf16[8,128,128]{2,1,0:T(8,128)(2,1)S(1)} async-done(((bf16[8,128,128]{2,1,0:T(8,128)(2,1)}), bf16[8,128,128]{2,1,0:T(8,128)(2,1)S(1)}, u32[]{:S(2)}, u32[]{:S(2)}) %all-to-all-start.2) | async-done | bytes 262176 | tf_op jit(solution)/shard_map/all_to_all | solution.py:1092
  341.8 8.6 %shard_map.277 = bf16[8,640,128]{2,1,0:T(8,128)(2,1)} custom-call(s32[1]{0:T(128)} %bitcast.1.half_ref, bf16[8,656,128]{2,1,0:T(8,128)(2,1)} %copy-done.8, f32[8,128,128]{2,1,0:T(8,128)} %get-tuple-element.135.log_ref, bf16[8,128,128]{2,1,0:T(8,128)(2,1)} %copy-done.24), custom_call_target="tpu_custom_call" | custom-call | flops 1610612736 | bytes 4030464 | tf_op jit(solution)/shard_map/pallas_call | solution.py:586
  350.4 5.4 %all-to-all-start.3 = ((bf16[8,640,128]{2,1,0:T(8,128)(2,1)}), bf16[8,640,128]{2,1,0:T(8,128)(2,1)S(1)}, u32[]{:S(2)}, u32[]{:S(2)}) async-start(bf16[8,640,128]{2,1,0:T(8,128)(2,1)} %shard_map.277), calls=%async_computation.4 | async-start | bytes 2621440 | tf_op jit(solution)/shard_map/all_to_all | solution.py:1092
  355.8 11.0 %shard_map.279 = f32[2,2048,256]{2,1,0:T(8,128)} custom-call(bf16[2048,2048]{1,0:T(8,128)(2,1)} %get-tuple-element.115.left_ref, bf16[2048,512]{1,0:T(8,128)(2,1)} %get-tuple-element.138.right_ref), custom_call_target="tpu_custom_call" | custom-call | flops 4294967296 | bytes 16777216 | tf_op jit(solution)/shard_map/pallas_call | solution.py:327
  366.8 10.9 %shard_map.278 = f32[512,2048]{1,0:T(8,128)} custom-call(bf16[512,2048]{1,0:T(8,128)(2,1)} %get-tuple-element.137.left_ref, bf16[2048,2048]{1,0:T(8,128)(2,1)} %all-gather.3.cloned.1.call-done.grad_ref.right_ref), custom_call_target="tpu_custom_call" | custom-call | flops 4294967296 | bytes 16777216 | tf_op jit(solution)/shard_map/pallas_call | solution.py:357
  377.6 10.2 %shard_map.280.rows_ref = bf16[2048,2048]{1,0:T(8,128)(2,1)} custom-call(bf16[2048,2048]{1,0:T(8,128)(2,1)} %all-gather.5.cloned.1.call-done.tokens_ref, f32[1,2048]{1,0:T(1,128)} %bitcast.184), custom_call_target="tpu_custom_call" | custom-call | bytes 16777216 | tf_op jit(solution)/shard_map/pallas_call | solution.py:414
  387.9 5.4 %all-to-all-done.3.back_ref = bf16[8,640,128]{2,1,0:T(8,128)(2,1)S(1)} async-done(((bf16[8,640,128]{2,1,0:T(8,128)(2,1)}), bf16[8,640,128]{2,1,0:T(8,128)(2,1)S(1)}, u32[]{:S(2)}, u32[]{:S(2)}) %all-to-all-start.3) | async-done | bytes 1310752 | tf_op jit(solution)/shard_map/all_to_all | solution.py:1092
  394.4 3.3 shard_map.281
  397.7 6.5 %psum.15.refs_6_ = f32[8,256]{1,0:T(8,128)} all-reduce(f32[8,256]{1,0:T(8,128)} %get-tuple-element.144), channel_id=1, replica_groups=mesh['dp'=8,'tensor'=4] {'tensor'}, use_global_device_ids=true, to_apply=%region_2.3 | all-reduce | flops 2048 | bytes 16384 | tf_op jit(solution)/shard_map/psum | solution.py:1224
  404.2 3.2 shard_map.282
  407.4 5.9 %shard_map.283 = (bf16[2,64,2048]{2,1,0:T(8,128)(2,1)}, bf16[2,64,2048]{2,1,0:T(8,128)(2,1)}) custom-call(s32[1]{0:T(128)} %bitcast.place_ref, bf16[256,512]{1,0:T(8,128)(2,1)} %get-tuple-element.145.refs_0_, bf16[256,512]{1,0:T(8,128)(2,1)} %get-tuple-element.146.refs_1_, bf16[256,512]{1,0:T(8,128)(2,1)} %get-tuple-element.143.refs_2_, ...), custom_call_target="tpu_custom_call" | custom-call | flops 1610612736 | bytes 7340032 | tf_op jit(solution)/shard_map/pallas_call | solution.py:949
  417.1 6.4 %all-to-all-start.4 = ((bf16[8,192,256]{2,1,0:T(8,128)(2,1)}), bf16[8,192,256]{2,1,0:T(8,128)(2,1)S(1)}, u32[]{:S(2)}, u32[]{:S(2)}) async-start(bf16[8,192,256]{2,1,0:T(8,128)(2,1)} %get-tuple-element.151), calls=%async_computation.5 | async-start | bytes 1572864 | tf_op jit(solution)/shard_map/all_to_all | solution.py:1228
  428.9 10.1 %collective-permute-done.42.refs_2_ = bf16[96,2048]{1,0:T(8,128)(2,1)S(1)} collective-permute-done((bf16[96,2048]{1,0:T(8,128)(2,1)}, bf16[96,2048]{1,0:T(8,128)(2,1)S(1)}, u32[]{:S(2)}, u32[]{:S(2)}) %collective-permute-start.42) | collective-permute-done | bytes 393248 | tf_op jit(solution)/shard_map/ppermute | solution.py:42
  444.5 8.7 %shard_map.286 = bf16[8,224,256]{2,1,0:T(8,128)(2,1)} custom-call(bf16[8,192,256]{2,1,0:T(8,128)(2,1)} %copy-done.2, bf16[2048,2048]{1,0:T(8,128)(2,1)} %shard_map.280.rows_ref, bf16[8,32,256]{2,1,0:T(8,128)(2,1)} %fusion.13.small_ref), custom_call_target="tpu_custom_call" | custom-call | flops 1610612736 | bytes 8388608 | tf_op jit(solution)/shard_map/pallas_call | solution.py:1038
  453.2 4.8 all-to-all-start.5
  460.9 27.9 %all-to-all-done.5 = bf16[8,224,256]{2,1,0:T(8,128)(2,1)S(1)} async-done(((bf16[8,224,256]{2,1,0:T(8,128)(2,1)}), bf16[8,224,256]{2,1,0:T(8,128)(2,1)S(1)}, u32[]{:S(2)}, u32[]{:S(2)}) %all-to-all-start.5) | async-done | bytes 917536 | tf_op jit(solution)/shard_map/all_to_all | solution.py:1257
  491.8 6.1 %collective-permute-done.37.refs_2_ = bf16[64,2048]{1,0:T(8,128)(2,1)S(1)} collective-permute-done((bf16[64,2048]{1,0:T(8,128)(2,1)S(1)}, bf16[64,2048]{1,0:T(8,128)(2,1)S(1)}, u32[]{:S(2)}, u32[]{:S(2)}) %collective-permute-start.37) | collective-permute-done | bytes 262176 | tf_op jit(solution)/shard_map/ppermute | solution.py:42
  506.6 11.8 %reduce-scatter.5.cloned.1.call-done = bf16[1,64,2048]{2,1,0:T(8,128)(2,1)} async-done(((bf16[8,64,2048]{2,1,0:T(8,128)(2,1)}), bf16[1,64,2048]{2,1,0:T(8,128)(2,1)}) %reduce-scatter.5.cloned.1.call-update) | async-done | bytes 262160 | tf_op jit(solution)/shard_map/reduce_scatter | solution.py:1213
  (238 shorter events, 104.6 us)
Async XLA Ops:
  7.2 154.2 %all-gather.3.cloned.1.call-start = ((), (), s32[]{:S(2)}) async-start(), calls=%async_computation.8 | async-start | bytes 8650752 | tf_op jit(solution)/shard_map/all_gather | solution.py:1101
  30.5 48.1 %all-to-all-start = ((bf16[8,656,128]{2,1,0:T(8,128)(2,1)}), bf16[8,656,128]{2,1,0:T(8,128)(2,1)S(1)}, u32[]{:S(2)}, u32[]{:S(2)}) async-start(bf16[8,656,128]{2,1,0:T(8,128)(2,1)} %shard_map.264), calls=%async_computation | async-start | bytes 2686976 | tf_op jit(solution)/shard_map/all_to_all | solution.py:1092
  36.3 341.3 %all-gather.5.cloned.1.call-start = ((), (), s32[]{:S(2)}) async-start(), calls=%async_computation.10 | async-start | bytes 8650752 | tf_op jit(solution)/shard_map/all_gather | solution.py:1159
  112.6 8.4 %collective-permute-start.1 = (bf16[64,2048]{1,0:T(8,128)(2,1)S(1)}, bf16[64,2048]{1,0:T(8,128)(2,1)S(1)}, u32[]{:S(2)}, u32[]{:S(2)}) collective-permute-start(bf16[64,2048]{1,0:T(8,128)(2,1)S(1)} %fusion.9), channel_id=1, source_target_pairs={{0,2},{1,3},{2,0},{3,1},{4,6},{5,7},{6,4},{7,5},{8,10},{9,11},{10,... | collective-permute-start | bytes 786440 | tf_op jit(solution)/shard_map/ppermute | solution.py:42
  124.6 11.6 %collective-permute-start.8 = (bf16[64,640]{1,0:T(8,128)(2,1)}, bf16[64,640]{1,0:T(8,128)(2,1)S(1)}, u32[]{:S(2)}, u32[]{:S(2)}) collective-permute-start(bf16[64,640]{1,0:T(8,128)(2,1)} %get-tuple-element.99), channel_id=1, source_target_pairs={{0,16},{4,20},{8,24},{12,28},{16,0},{20,4},{24,8},{28,12},{1,17},{... | collective-permute-start | bytes 245768 | tf_op jit(solution)/shard_map/ppermute | solution.py:42
  125.0 14.2 %collective-permute-start.5 = (bf16[64,768]{1,0:T(8,128)(2,1)}, bf16[64,768]{1,0:T(8,128)(2,1)S(1)}, u32[]{:S(2)}, u32[]{:S(2)}) collective-permute-start(bf16[64,768]{1,0:T(8,128)(2,1)} %get-tuple-element.98), channel_id=1, source_target_pairs={{0,16},{4,20},{8,24},{12,28},{16,0},{20,4},{24,8},{28,12},{1,17},{... | collective-permute-start | bytes 294920 | tf_op jit(solution)/shard_map/ppermute | solution.py:42
  127.5 13.5 %collective-permute-start.2 = (bf16[64,768]{1,0:T(8,128)(2,1)}, bf16[64,768]{1,0:T(8,128)(2,1)S(1)}, u32[]{:S(2)}, u32[]{:S(2)}) collective-permute-start(bf16[64,768]{1,0:T(8,128)(2,1)} %get-tuple-element.97), channel_id=1, source_target_pairs={{0,16},{4,20},{8,24},{12,28},{16,0},{20,4},{24,8},{28,12},{1,17},{... | collective-permute-start | bytes 294920 | tf_op jit(solution)/shard_map/ppermute | solution.py:42
  137.1 5.4 %collective-permute-start.9 = (bf16[2,64,640]{2,1,0:T(8,128)(2,1)S(1)}, bf16[2,64,640]{2,1,0:T(8,128)(2,1)S(1)}, u32[]{:S(2)}, u32[]{:S(2)}) collective-permute-start(bf16[2,64,640]{2,1,0:T(8,128)(2,1)S(1)} %get-tuple-element.228), channel_id=1, source_target_pairs={{0,4},{4,0},{8,12},{12,8},{16,20},{20,16},{24,28},{28,24},{1,5},{5... | collective-permute-start | bytes 491528 | tf_op jit(solution)/shard_map/ppermute | solution.py:42
  140.1 7.9 %collective-permute-start.6 = (bf16[2,64,768]{2,1,0:T(8,128)(2,1)S(1)}, bf16[2,64,768]{2,1,0:T(8,128)(2,1)S(1)}, u32[]{:S(2)}, u32[]{:S(2)}) collective-permute-start(bf16[2,64,768]{2,1,0:T(8,128)(2,1)S(1)} %get-tuple-element.222), channel_id=1, source_target_pairs={{0,2},{1,3},{2,0},{3,1},{4,6},{5,7},{6,4},{7,5},{8,10},{9,11},{10,... | collective-permute-start | bytes 589832 | tf_op jit(solution)/shard_map/ppermute | solution.py:42
  142.0 7.5 %collective-permute-start.3 = (bf16[2,64,768]{2,1,0:T(8,128)(2,1)S(1)}, bf16[2,64,768]{2,1,0:T(8,128)(2,1)S(1)}, u32[]{:S(2)}, u32[]{:S(2)}) collective-permute-start(bf16[2,64,768]{2,1,0:T(8,128)(2,1)S(1)} %get-tuple-element.224), channel_id=1, source_target_pairs={{0,8},{4,12},{8,0},{12,4},{16,24},{20,28},{24,16},{28,20},{1,9},{5... | collective-permute-start | bytes 589832 | tf_op jit(solution)/shard_map/ppermute | solution.py:42
  142.5 10.0 %collective-permute-start.10 = (bf16[2,2,64,640]{3,2,1,0:T(8,128)(2,1)S(1)}, bf16[2,2,64,640]{3,2,1,0:T(8,128)(2,1)S(1)}, u32[]{:S(2)}, u32[]{:S(2)}) collective-permute-start(bf16[2,2,64,640]{3,2,1,0:T(8,128)(2,1)S(1)} %get-tuple-element.216), channel_id=1, source_target_pairs={{0,2},{1,3},{2,0},{3,1},{4,6},{5,7},{6,4},{7,5},{8,10},{9,11},{10,... | collective-permute-start | bytes 983048 | tf_op jit(solution)/shard_map/ppermute | solution.py:42
  148.0 8.1 %collective-permute-start.7 = (bf16[2,2,64,768]{3,2,1,0:T(8,128)(2,1)S(1)}, bf16[2,2,64,768]{3,2,1,0:T(8,128)(2,1)S(1)}, u32[]{:S(2)}, u32[]{:S(2)}) collective-permute-start(bf16[2,2,64,768]{3,2,1,0:T(8,128)(2,1)S(1)} %get-tuple-element.212), channel_id=1, source_target_pairs={{0,8},{4,12},{8,0},{12,4},{16,24},{20,28},{24,16},{28,20},{1,9},{5... | collective-permute-start | bytes 1179656 | tf_op jit(solution)/shard_map/ppermute | solution.py:42
  149.6 7.9 %collective-permute-start.4 = (bf16[2,2,64,768]{3,2,1,0:T(8,128)(2,1)S(1)}, bf16[2,2,64,768]{3,2,1,0:T(8,128)(2,1)}, u32[]{:S(2)}, u32[]{:S(2)}) collective-permute-start(bf16[2,2,64,768]{3,2,1,0:T(8,128)(2,1)S(1)} %get-tuple-element.214), channel_id=1, source_target_pairs={{0,4},{4,0},{8,12},{12,8},{16,20},{20,16},{24,28},{28,24},{1,5},{5... | collective-permute-start | bytes 1179656 | tf_op jit(solution)/shard_map/ppermute | solution.py:42
  158.6 280.4 %reduce-scatter.3.cloned.1.call-start = ((), (), s32[]{:S(2)}) async-start(), calls=%async_computation.9 | async-start | bytes 4456448 | tf_op jit(solution)/shard_map/reduce_scatter | solution.py:1176
  158.8 16.5 %collective-permute-start.11 = (bf16[2,2,2,64,768]{4,3,2,1,0:T(8,128)(2,1)S(1)}, bf16[2,2,2,64,768]{4,3,2,1,0:T(8,128)(2,1)S(1)}, u32[]{:S(2)}, u32[]{:S(2)}) collective-permute-start(bf16[2,2,2,64,768]{4,3,2,1,0:T(8,128)(2,1)S(1)} %pad_maximum_fusion.3), channel_id=1, source_target_pairs={{0,2},{1,3},{2,0},{3,1},{4,6},{5,7},{6,4},{7,5},{8,10},{9,11},{10,... | collective-permute-start | bytes 2359304 | tf_op jit(solution)/shard_map/ppermute | solution.py:42
  161.0 15.3 %collective-permute-start.12 = (bf16[2,2,2,64,768]{4,3,2,1,0:T(8,128)(2,1)S(1)}, bf16[2,2,2,64,768]{4,3,2,1,0:T(8,128)(2,1)}, u32[]{:S(2)}, u32[]{:S(2)}) collective-permute-start(bf16[2,2,2,64,768]{4,3,2,1,0:T(8,128)(2,1)S(1)} %pad_maximum_fusion.4), channel_id=1, source_target_pairs={{0,4},{4,0},{8,12},{12,8},{16,20},{20,16},{24,28},{28,24},{1,5},{5... | collective-permute-start | bytes 2359304 | tf_op jit(solution)/shard_map/ppermute | solution.py:42
  161.1 14.2 %collective-permute-start.13 = (bf16[2,2,2,64,640]{4,3,2,1,0:T(8,128)(2,1)S(1)}, bf16[2,2,2,64,640]{4,3,2,1,0:T(8,128)(2,1)}, u32[]{:S(2)}, u32[]{:S(2)}) collective-permute-start(bf16[2,2,2,64,640]{4,3,2,1,0:T(8,128)(2,1)S(1)} %pad_maximum_fusion.5), channel_id=1, source_target_pairs={{0,8},{4,12},{8,0},{12,4},{16,24},{20,28},{24,16},{28,20},{1,9},{5... | collective-permute-start | bytes 1966088 | tf_op jit(solution)/shard_map/ppermute | solution.py:42
  177.5 7.6 %collective-permute-start.15 = (bf16[2,2,2,2,64,768]{5,4,3,2,1,0:T(8,128)(2,1)S(1)}, bf16[2,2,2,2,64,768]{5,4,3,2,1,0:T(8,128)(2,1)S(1)}, u32[]{:S(2)}, u32[]{:S(2)}) collective-permute-start(bf16[2,2,2,2,64,768]{5,4,3,2,1,0:T(8,128)(2,1)S(1)} %pad_maximum_fusion.1.refs_1_), channel_id=1, source_target_pairs={{0,1},{1,0},{2,3},{3,2},{4,5},{5,4},{6,7},{7,6},{8,9},{9,8},{10,11... | collective-permute-start | bytes 4718600 | tf_op jit(solution)/shard_map/ppermute | solution.py:42
  178.7 6.4 %collective-permute-start.14 = (bf16[2,2,2,2,64,768]{5,4,3,2,1,0:T(8,128)(2,1)S(1)}, bf16[2,2,2,2,64,768]{5,4,3,2,1,0:T(8,128)(2,1)S(1)}, u32[]{:S(2)}, u32[]{:S(2)}) collective-permute-start(bf16[2,2,2,2,64,768]{5,4,3,2,1,0:T(8,128)(2,1)S(1)} %pad_maximum_fusion.refs_0_), channel_id=1, source_target_pairs={{0,1},{1,0},{2,3},{3,2},{4,5},{5,4},{6,7},{7,6},{8,9},{9,8},{10,11... | collective-permute-start | bytes 4718600 | tf_op jit(solution)/shard_map/ppermute | solution.py:42
  180.4 4.7 collective-permute-start.16
  217.3 5.8 %collective-permute-start.19 = (bf16[8,2,64,768]{3,2,1,0:T(8,128)(2,1)}, bf16[8,2,64,768]{3,2,1,0:T(8,128)(2,1)S(1)}, u32[]{:S(2)}, u32[]{:S(2)}) collective-permute-start(bf16[8,2,64,768]{3,2,1,0:T(8,128)(2,1)} %get-tuple-element.112), channel_id=1, source_target_pairs={{0,1},{1,0},{2,3},{3,2},{4,5},{5,4},{6,7},{7,6},{8,9},{9,8},{10,11... | collective-permute-start | bytes 4718600 | tf_op jit(solution)/shard_map/ppermute | solution.py:42
  217.7 7.8 %collective-permute-start.17 = (bf16[8,2,64,768]{3,2,1,0:T(8,128)(2,1)}, bf16[8,2,64,768]{3,2,1,0:T(8,128)(2,1)S(1)}, u32[]{:S(2)}, u32[]{:S(2)}) collective-permute-start(bf16[8,2,64,768]{3,2,1,0:T(8,128)(2,1)} %get-tuple-element.110), channel_id=1, source_target_pairs={{0,1},{1,0},{2,3},{3,2},{4,5},{5,4},{6,7},{7,6},{8,9},{9,8},{10,11... | collective-permute-start | bytes 4718600 | tf_op jit(solution)/shard_map/ppermute | solution.py:42
  222.3 26.7 %collective-permute-start.22 = (bf16[2,2,2,64,640]{4,3,0,1,2:T(8,128)(2,1)S(1)}, bf16[2,2,2,64,640]{4,3,0,1,2:T(8,128)(2,1)S(1)}, u32[]{:S(2)}, u32[]{:S(2)}) collective-permute-start(bf16[2,2,2,64,640]{4,3,0,1,2:T(8,128)(2,1)S(1)} %bitcast.166), channel_id=1, source_target_pairs={{0,8},{4,12},{8,0},{12,4},{16,24},{20,28},{24,16},{28,20},{1,9},{5... | collective-permute-start | bytes 1966088 | tf_op jit(solution)/shard_map/ppermute | solution.py:42
  224.2 24.8 %collective-permute-start.20 = (bf16[2,2,2,64,768]{4,3,0,2,1:T(8,128)(2,1)S(1)}, bf16[2,2,2,64,768]{4,3,0,2,1:T(8,128)(2,1)S(1)}, u32[]{:S(2)}, u32[]{:S(2)}) collective-permute-start(bf16[2,2,2,64,768]{4,3,0,2,1:T(8,128)(2,1)S(1)} %bitcast.163), channel_id=1, source_target_pairs={{0,4},{4,0},{8,12},{12,8},{16,20},{20,16},{24,28},{28,24},{1,5},{5... | collective-permute-start | bytes 2359304 | tf_op jit(solution)/shard_map/ppermute | solution.py:42
  226.3 22.7 %collective-permute-start.18 = (bf16[2,2,2,64,768]{4,3,0,1,2:T(8,128)(2,1)S(1)}, bf16[2,2,2,64,768]{4,3,0,1,2:T(8,128)(2,1)S(1)}, u32[]{:S(2)}, u32[]{:S(2)}) collective-permute-start(bf16[2,2,2,64,768]{4,3,0,1,2:T(8,128)(2,1)S(1)} %bitcast.164), channel_id=1, source_target_pairs={{0,2},{1,3},{2,0},{3,1},{4,6},{5,7},{6,4},{7,5},{8,10},{9,11},{10,... | collective-permute-start | bytes 2359304 | tf_op jit(solution)/shard_map/ppermute | solution.py:42
  249.0 20.2 %collective-permute-start.29 = (bf16[16,64,2048]{2,1,0:T(8,128)(2,1)}, bf16[16,64,2048]{2,1,0:T(8,128)(2,1)S(1)}, u32[]{:S(2)}, u32[]{:S(2)}) collective-permute-start(bf16[16,64,2048]{2,1,0:T(8,128)(2,1)} %get-tuple-element.125), channel_id=1, source_target_pairs={{0,1},{1,0},{2,3},{3,2},{4,5},{5,4},{6,7},{7,6},{8,9},{9,8},{10,11... | collective-permute-start | bytes 12582920 | tf_op jit(solution)/shard_map/ppermute | solution.py:42
  249.4 10.1 %collective-permute-start.27 = (bf16[2,2,64,640]{3,2,0,1:T(8,128)(2,1)S(1)}, bf16[2,2,64,640]{3,2,0,1:T(8,128)(2,1)S(1)}, u32[]{:S(2)}, u32[]{:S(2)}) collective-permute-start(bf16[2,2,64,640]{3,2,0,1:T(8,128)(2,1)S(1)} %slice_bitcast_fusion.4), channel_id=1, source_target_pairs={{0,2},{1,3},{2,0},{3,1},{4,6},{5,7},{6,4},{7,5},{8,10},{9,11},{10,... | collective-permute-start | bytes 983048 | tf_op jit(solution)/shard_map/ppermute | solution.py:42
  250.5 11.3 %collective-permute-start.25 = (bf16[2,2,64,768]{3,2,0,1:T(8,128)(2,1)S(1)}, bf16[2,2,64,768]{3,2,0,1:T(8,128)(2,1)S(1)}, u32[]{:S(2)}, u32[]{:S(2)}) collective-permute-start(bf16[2,2,64,768]{3,2,0,1:T(8,128)(2,1)S(1)} %slice_bitcast_fusion), channel_id=1, source_target_pairs={{0,8},{4,12},{8,0},{12,4},{16,24},{20,28},{24,16},{28,20},{1,9},{5... | collective-permute-start | bytes 1179656 | tf_op jit(solution)/shard_map/ppermute | solution.py:42
  251.4 11.8 %collective-permute-start.23 = (bf16[2,2,64,768]{3,2,0,1:T(8,128)(2,1)S(1)}, bf16[2,2,64,768]{3,2,0,1:T(8,128)(2,1)S(1)}, u32[]{:S(2)}, u32[]{:S(2)}) collective-permute-start(bf16[2,2,64,768]{3,2,0,1:T(8,128)(2,1)S(1)} %slice_bitcast_fusion.2), channel_id=1, source_target_pairs={{0,4},{4,0},{8,12},{12,8},{16,20},{20,16},{24,28},{28,24},{1,5},{5... | collective-permute-start | bytes 1179656 | tf_op jit(solution)/shard_map/ppermute | solution.py:42
  259.6 6.3 %collective-permute-start.28 = (bf16[2,64,640]{2,1,0:T(8,128)(2,1)S(1)}, bf16[2,64,640]{2,1,0:T(8,128)(2,1)S(1)}, u32[]{:S(2)}, u32[]{:S(2)}) collective-permute-start(bf16[2,64,640]{2,1,0:T(8,128)(2,1)S(1)} %slice_bitcast_fusion.10), channel_id=1, source_target_pairs={{0,4},{4,0},{8,12},{12,8},{16,20},{20,16},{24,28},{28,24},{1,5},{5... | collective-permute-start | bytes 491528 | tf_op jit(solution)/shard_map/ppermute | solution.py:42
  261.9 6.2 %collective-permute-start.26 = (bf16[2,64,768]{2,1,0:T(8,128)(2,1)S(1)}, bf16[2,64,768]{2,1,0:T(8,128)(2,1)S(1)}, u32[]{:S(2)}, u32[]{:S(2)}) collective-permute-start(bf16[2,64,768]{2,1,0:T(8,128)(2,1)S(1)} %slice_bitcast_fusion.6), channel_id=1, source_target_pairs={{0,2},{1,3},{2,0},{3,1},{4,6},{5,7},{6,4},{7,5},{8,10},{9,11},{10,... | collective-permute-start | bytes 589832 | tf_op jit(solution)/shard_map/ppermute | solution.py:42
  263.3 5.9 %collective-permute-start.24 = (bf16[2,64,768]{2,1,0:T(8,128)(2,1)S(1)}, bf16[2,64,768]{2,1,0:T(8,128)(2,1)S(1)}, u32[]{:S(2)}, u32[]{:S(2)}) collective-permute-start(bf16[2,64,768]{2,1,0:T(8,128)(2,1)S(1)} %slice_bitcast_fusion.8), channel_id=1, source_target_pairs={{0,8},{4,12},{8,0},{12,4},{16,24},{20,28},{24,16},{28,20},{1,9},{5... | collective-permute-start | bytes 589832 | tf_op jit(solution)/shard_map/ppermute | solution.py:42
  274.0 22.0 %collective-permute-start.30 = (bf16[64,768]{1,0:T(8,128)(2,1)S(1)}, bf16[64,768]{1,0:T(8,128)(2,1)S(1)}, u32[]{:S(2)}, u32[]{:S(2)}) collective-permute-start(bf16[64,768]{1,0:T(8,128)(2,1)S(1)} %get-tuple-element.219), channel_id=1, source_target_pairs={{0,16},{4,20},{8,24},{12,28},{16,0},{20,4},{24,8},{28,12},{1,17},{... | collective-permute-start | bytes 294920 | tf_op jit(solution)/shard_map/ppermute | solution.py:42
  280.2 15.8 %collective-permute-start.31 = (bf16[64,768]{1,0:T(8,128)(2,1)S(1)}, bf16[64,768]{1,0:T(8,128)(2,1)S(1)}, u32[]{:S(2)}, u32[]{:S(2)}) collective-permute-start(bf16[64,768]{1,0:T(8,128)(2,1)S(1)} %get-tuple-element.217), channel_id=1, source_target_pairs={{0,16},{4,20},{8,24},{12,28},{16,0},{20,4},{24,8},{28,12},{1,17},{... | collective-permute-start | bytes 294920 | tf_op jit(solution)/shard_map/ppermute | solution.py:42
  280.9 15.1 %collective-permute-start.32 = (bf16[64,640]{1,0:T(8,128)(2,1)S(1)}, bf16[64,640]{1,0:T(8,128)(2,1)S(1)}, u32[]{:S(2)}, u32[]{:S(2)}) collective-permute-start(bf16[64,640]{1,0:T(8,128)(2,1)S(1)} %get-tuple-element.225), channel_id=1, source_target_pairs={{0,16},{4,20},{8,24},{12,28},{16,0},{20,4},{24,8},{28,12},{1,17},{... | collective-permute-start | bytes 245768 | tf_op jit(solution)/shard_map/ppermute | solution.py:42
  299.9 16.6 %collective-permute-start.34 = (bf16[64,2048]{1,0:T(8,128)(2,1)}, bf16[64,2048]{1,0:T(8,128)(2,1)S(1)}, u32[]{:S(2)}, u32[]{:S(2)}) collective-permute-start(bf16[64,2048]{1,0:T(8,128)(2,1)} %get-tuple-element.131.refs_0_), channel_id=1, source_target_pairs={{0,2},{1,3},{2,0},{3,1},{4,6},{5,7},{6,4},{7,5},{8,10},{9,11},{10,... | collective-permute-start | bytes 786440 | tf_op jit(solution)/shard_map/ppermute | solution.py:42
  299.9 16.6 %collective-permute-start.33 = (bf16[64,2048]{1,0:T(8,128)(2,1)}, bf16[64,2048]{1,0:T(8,128)(2,1)S(1)}, u32[]{:S(2)}, u32[]{:S(2)}) collective-permute-start(bf16[64,2048]{1,0:T(8,128)(2,1)} %get-tuple-element.131.refs_0_), channel_id=1, source_target_pairs={{0,1},{1,0},{2,3},{3,2},{4,5},{5,4},{6,7},{7,6},{8,9},{9,8},{10,11... | collective-permute-start | bytes 786440 | tf_op jit(solution)/shard_map/ppermute | solution.py:42
  322.1 19.0 %all-to-all-start.2 = ((bf16[8,128,128]{2,1,0:T(8,128)(2,1)}), bf16[8,128,128]{2,1,0:T(8,128)(2,1)S(1)}, u32[]{:S(2)}, u32[]{:S(2)}) async-start(bf16[8,128,128]{2,1,0:T(8,128)(2,1)} %shard_map.274), calls=%async_computation.2 | async-start | bytes 524288 | tf_op jit(solution)/shard_map/all_to_all | solution.py:1092
  350.4 42.9 %all-to-all-start.3 = ((bf16[8,640,128]{2,1,0:T(8,128)(2,1)}), bf16[8,640,128]{2,1,0:T(8,128)(2,1)S(1)}, u32[]{:S(2)}, u32[]{:S(2)}) async-start(bf16[8,640,128]{2,1,0:T(8,128)(2,1)} %shard_map.277), calls=%async_computation.4 | async-start | bytes 2621440 | tf_op jit(solution)/shard_map/all_to_all | solution.py:1092
  416.6 8.4 %collective-permute-start.40 = (bf16[64,2048]{1,0:T(8,128)(2,1)S(1)}, bf16[64,2048]{1,0:T(8,128)(2,1)S(1)}, u32[]{:S(2)}, u32[]{:S(2)}) collective-permute-start(bf16[64,2048]{1,0:T(8,128)(2,1)S(1)} %fusion.10), channel_id=1, source_target_pairs={{0,2},{1,3},{2,0},{3,1},{4,6},{5,7},{6,4},{7,5},{8,10},{9,11},{10,... | collective-permute-start | bytes 786440 | tf_op jit(solution)/shard_map/ppermute | solution.py:42
  417.1 26.6 %all-to-all-start.4 = ((bf16[8,192,256]{2,1,0:T(8,128)(2,1)}), bf16[8,192,256]{2,1,0:T(8,128)(2,1)S(1)}, u32[]{:S(2)}, u32[]{:S(2)}) async-start(bf16[8,192,256]{2,1,0:T(8,128)(2,1)} %get-tuple-element.151), calls=%async_computation.5 | async-start | bytes 1572864 | tf_op jit(solution)/shard_map/all_to_all | solution.py:1228
  423.5 94.9 %reduce-scatter.5.cloned.1.call-start = ((), (), s32[]{:S(2)}) async-start(), calls=%async_computation.11 | async-start | bytes 2359296 | tf_op jit(solution)/shard_map/reduce_scatter | solution.py:1213
  428.5 10.5 %collective-permute-start.42 = (bf16[96,2048]{1,0:T(8,128)(2,1)}, bf16[96,2048]{1,0:T(8,128)(2,1)S(1)}, u32[]{:S(2)}, u32[]{:S(2)}) collective-permute-start(bf16[96,2048]{1,0:T(8,128)(2,1)} %shard_map.284.refs_0_), channel_id=1, source_target_pairs={{0,2},{1,3},{2,0},{3,1},{4,6},{5,7},{6,4},{7,5},{8,10},{9,11},{10,... | collective-permute-start | bytes 1179656 | tf_op jit(solution)/shard_map/ppermute | solution.py:42
  428.9 11.2 %collective-permute-start.41 = (bf16[96,2048]{1,0:T(8,128)(2,1)}, bf16[96,2048]{1,0:T(8,128)(2,1)S(1)}, u32[]{:S(2)}, u32[]{:S(2)}) collective-permute-start(bf16[96,2048]{1,0:T(8,128)(2,1)} %shard_map.284.refs_0_), channel_id=1, source_target_pairs={{0,1},{1,0},{2,3},{3,2},{4,5},{5,4},{6,7},{7,6},{8,9},{9,8},{10,11... | collective-permute-start | bytes 1179656 | tf_op jit(solution)/shard_map/ppermute | solution.py:42
  453.2 35.6 %all-to-all-start.5 = ((bf16[8,224,256]{2,1,0:T(8,128)(2,1)}), bf16[8,224,256]{2,1,0:T(8,128)(2,1)S(1)}, u32[]{:S(2)}, u32[]{:S(2)}) async-start(bf16[8,224,256]{2,1,0:T(8,128)(2,1)} %shard_map.286), calls=%async_computation.6 | async-start | bytes 1835008 | tf_op jit(solution)/shard_map/all_to_all | solution.py:1257
  490.0 7.9 %collective-permute-start.37 = (bf16[64,2048]{1,0:T(8,128)(2,1)S(1)}, bf16[64,2048]{1,0:T(8,128)(2,1)S(1)}, u32[]{:S(2)}, u32[]{:S(2)}) collective-permute-start(bf16[64,2048]{1,0:T(8,128)(2,1)S(1)} %add_convert_fusion.5.refs_0_), channel_id=1, source_target_pairs={{0,2},{1,3},{2,0},{3,1},{4,6},{5,7},{6,4},{7,5},{8,10},{9,11},{10,... | collective-permute-start | bytes 786440 | tf_op jit(solution)/shard_map/ppermute | solution.py:42
  491.7 11.2 %collective-permute-start.36 = (bf16[64,2048]{1,0:T(8,128)(2,1)S(1)}, bf16[64,2048]{1,0:T(8,128)(2,1)S(1)}, u32[]{:S(2)}, u32[]{:S(2)}) collective-permute-start(bf16[64,2048]{1,0:T(8,128)(2,1)S(1)} %add_convert_fusion.5.refs_0_), channel_id=1, source_target_pairs={{0,1},{1,0},{2,3},{3,2},{4,5},{5,4},{6,7},{7,6},{8,9},{9,8},{10,11... | collective-permute-start | bytes 786440 | tf_op jit(solution)/shard_map/ppermute | solution.py:42
  497.9 5.0 collective-permute-start.38
  (39 other events, 120.4 us)
Sparse Core Ops, SparseCore 0:
  11.4 99.9 all-gather.2
  158.7 81.5 all-gather.4
  273.5 105.9 reduce-scatter.2
  439.2 79.1 reduce-scatter.4
